TPU v7x, 128 devices: a whole 4x4x4 slice. The times are simulated.
128 devices in a mesh: seq: 16 (over x, y_hi, core), res: 8 (over z, y_lo).
Axes of the slice: x: 4, y: 4 (y_hi: 2, y_lo: 2; y = y_hi * 2 + y_lo), z: 4, core: 2. Of those that a mesh axis runs over, the one named last changes fastest.
Arguments:
- left_alignment: bfloat16 [256, 256, 32], P('seq', 'res'), may hold values from -6 to 6
- right_alignment: bfloat16 [256, 256, 32], P('seq', 'res'), may hold values from -6 to 6
- alignment_mask: int32 [256, 256], P('seq', 'res'), may hold values from 0 to 1, as said below
- output_weight: bfloat16 [32, 32, 128], replicated, may hold values from -3 to 3
- output_bias: float32 [128], replicated, may hold values from -4 to 4
- pair_update_cotangent: bfloat16 [256, 256, 128], P('seq', 'res'), may hold values from -6 to 6
Outputs:
- pair_update: bfloat16 [256, 256, 128], P('seq', 'res')
- left_operand_gradient: float32 [256, 256, 32], P('seq', 'res')
- right_operand_gradient: float32 [256, 256, 32], P('seq', 'res')
- weight_grad: float32 [32, 32, 128], replicated
- bias_grad: float32 [128], replicated
Inputs may be any that keep to these rules, and one draw needn't show every extreme that they name: alignment_mask is 0 or 1; sequence 0 is 1 at every residue.
All inputs are finite; a program needn't handle non-finite values.
Results may differ from a plain program's by a relative error of at most 0.0049.
Values may be sent and summed in bfloat16 or wider, within the bound.
No kernel may reach another device: no remote copies, remote signals or barrier semaphores. Data moves between devices by JAX's collectives and lax.ppermute only.
A program may use at most 256 MiB of HBM per device.

v0:
```python
import jax
import jax.numpy as jnp
from jax import lax
from jax.sharding import PartitionSpec as P


def per_device(
    left_alignment,
    right_alignment,
    alignment_mask,
    output_weight,
    output_bias,
    pair_update_cotangent,
):
    local_sequences, local_residues, channel_count = left_alignment.shape
    pair_ch = output_weight.shape[2]
    row_block = pair_update_cotangent.shape[0]
    mask_float = alignment_mask.astype(jnp.float32)
    mask_bfloat = alignment_mask.astype(jnp.bfloat16)
    left_under_mask = left_alignment * mask_bfloat[:, :, None]
    right_under_mask = right_alignment * mask_bfloat[:, :, None]
    projected = jnp.einsum(
        "sjd,cdh->scjh", right_under_mask, output_weight, preferred_element_type=jnp.float32
    ).astype(jnp.bfloat16)
    proj_flat = projected.reshape(local_sequences * channel_count, local_residues * pair_ch)
    full_mask = lax.all_gather(alignment_mask, "res", axis=1, tiled=True)
    left_all = lax.all_gather(left_under_mask, "res", axis=1, tiled=True)
    residues = left_all.shape[1]
    left_rows = left_all.transpose(1, 0, 2).reshape(residues, local_sequences * channel_count)
    count_terms = jnp.dot(
        full_mask.astype(jnp.float32).T, mask_float, precision=lax.Precision.HIGHEST
    )
    counts = (
        lax.psum_scatter(
            count_terms.astype(jnp.bfloat16), "seq", scatter_dimension=0, tiled=True
        ).astype(jnp.float32)
        + 0.001
    )
    picked = left_rows
    summed = lax.psum_scatter(
        jnp.dot(picked, proj_flat, preferred_element_type=jnp.float32).reshape(
            row_block * lax.axis_size("seq"), local_residues, pair_ch
        ),
        "seq",
        scatter_dimension=0,
        tiled=True,
    )
    pair_update = (summed / counts[:, :, None] + output_bias).astype(jnp.bfloat16)
    scaled = (pair_update_cotangent.astype(jnp.float32) / counts[:, :, None]).astype(jnp.bfloat16)
    portion = lax.all_gather(scaled, "seq", axis=0, tiled=True)
    height = portion.shape[0]
    flat = portion.reshape(height, local_residues * pair_ch)
    picked = left_rows
    grad_acc = lax.dot_general(
        picked, flat, (((0,), (0,)), ((), ())), preferred_element_type=jnp.float32
    )
    left_piece = lax.dot_general(
        flat, proj_flat, (((1,), (1,)), ((), ())), preferred_element_type=jnp.float32
    )
    left_sum = lax.psum_scatter(left_piece, "res", scatter_dimension=0, tiled=True)
    left_operand_gradient = (
        left_sum.reshape(local_residues, local_sequences, channel_count).transpose(1, 0, 2)
        * mask_float[:, :, None]
    )
    grad_four = grad_acc.reshape(local_sequences, channel_count, local_residues, pair_ch)
    weight32 = output_weight.astype(jnp.float32)
    right_operand_gradient = (
        jnp.einsum("scjh,cdh->sjd", grad_four, weight32, precision=lax.Precision.HIGHEST)
        * mask_float[:, :, None]
    )
    weight_terms = jnp.einsum(
        "sjd,scjh->cdh",
        right_under_mask.astype(jnp.float32),
        grad_four,
        precision=lax.Precision.HIGHEST,
    )
    bias_terms = jnp.sum(pair_update_cotangent.astype(jnp.float32), axis=(0, 1))
    weight_grad, bias_grad = lax.psum((weight_terms, bias_terms), ("seq", "res"))
    return (pair_update, left_operand_gradient, right_operand_gradient, weight_grad, bias_grad)


def solution(mesh):
    return jax.shard_map(
        per_device,
        mesh=mesh,
        in_specs=(
            P("seq", "res", None),
            P("seq", "res", None),
            P("seq", "res"),
            P(),
            P(),
            P("seq", "res", None),
        ),
        out_specs=(P("seq", "res", None), P("seq", "res", None), P("seq", "res", None), P(), P()),
        check_vma=False,
    )
```

profile of v0, /device:TPU:1, one launch (start us, length us, event | category | flops | bytes accessed | tf_op | source)
XLA Modules:
  0.0 477.2 jit_solution(3804345761741627732)
XLA Ops:
  7.2 24.7 %all-gather = s32[8,32,16]{1,2,0:T(8,128)S(1)} all-gather(s32[1,32,16]{1,2,0:T(8,128)} %bitcast.72), channel_id=1, replica_groups=mesh['seq'=16,'res'=8] {'res'}, dimensions={0}, use_global_device_ids=true | all-gather | bytes 18432 | tf_op jit(solution)/shard_map/all_gather | solution.py:26
  31.9 0.1 reshape.37
  32.0 1.7 convolution_convert_fusion.1
  33.8 0.0 reduce-scatter.4.cloned.1.call-start
  33.8 0.8 fusion.25
  34.6 0.1 copy.34
  34.7 1.1 fusion.23
  35.8 26.7 %all_gather.9 = bf16[16,256,32]{2,0,1:T(8,128)(2,1)S(1)} all-gather(bf16[16,32,32]{2,0,1:T(8,128)(2,1)S(1)} %get-tuple-element.26), channel_id=1, replica_groups=mesh['seq'=16,'res'=8] {'res'}, dimensions={1}, use_global_device_ids=true | all-gather | bytes 294912 | tf_op jit(solution)/shard_map/all_gather | solution.py:27
  62.5 0.8 copy.36
  63.3 1.2 convolution_convert_fusion
  64.6 6.2 %copy.87 = bf16[64,8,32,128]{3,1,2,0:T(8,128)(2,1)} copy(bf16[64,8,32,128]{3,2,1,0:T(8,128)(2,1)S(1)} %bitcast.67) | data formatting | bytes 8388608
  70.8 6.5 %copy.39 = bf16[4096,512]{1,0:T(8,128)(2,1)} copy(bf16[4096,512]{0,1:T(8,128)(2,1)} %bitcast.69) | data formatting | bytes 8388608 | tf_op jit(solution)/shard_map/dot_general | solution.py:41
  77.3 5.5 %fusion.26 = f32[256,32,128]{2,0,1:T(8,128)} fusion(bf16[256,512,1]{0,1,2:T(8,128)(2,1)S(1)} %bitcast.71, bf16[32,128,512]{2,1,0:T(8,128)(2,1)} %bitcast.66), kind=kOutput, calls=%fused_computation.30 | convolution fusion | flops 1073741824 | bytes 8650752 | tf_op jit(solution)/shard_map/dot_general | solution.py:41
  82.8 17.7 %reduce-scatter.6.cloned.1.call-done = bf16[16,32]{1,0:T(8,128)(2,1)} async-done(((bf16[256,32]{1,0:T(8,128)(2,1)}), bf16[16,32]{1,0:T(8,128)(2,1)}) %reduce-scatter.6.cloned.1.call-update) | async-done | bytes 1040 | tf_op jit(solution)/shard_map/reduce_scatter | solution.py:34
  100.6 0.7 convert_add_fusion
  101.2 0.1 copy.42
  101.3 83.3 %reduce-scatter.4.cloned.1.call-done = f32[16,32,128]{2,0,1:T(8,128)} async-done(((f32[256,32,128]{2,0,1:T(8,128)}), f32[16,32,128]{2,0,1:T(8,128)}) %reduce-scatter.4.cloned.1.call-update) | async-done | bytes 262160 | tf_op jit(solution)/shard_map/reduce_scatter | solution.py:40
  184.7 1.7 convert_reduce_fusion
  186.4 0.2 reduce-scatter.8.cloned.1.call-start
  186.7 51.4 %all-gather.3.cloned.1.call-done = bf16[256,32,128]{2,0,1:T(8,128)(2,1)} async-done(((bf16[16,32,128]{2,0,1:T(8,128)(2,1)}), bf16[256,32,128]{2,0,1:T(8,128)(2,1)}) %all-gather.3.cloned.1.call-update) | async-done | bytes 2097168 | tf_op jit(solution)/shard_map/all_gather | solution.py:50
  238.0 3.3 copy.44
  241.3 5.7 %fusion.4 = f32[256,512]{1,0:T(8,128)} fusion(bf16[256,4096]{0,1:T(8,128)(2,1)S(1)} %bitcast.70, bf16[64,8,32,128]{3,2,1,0:T(8,128)(2,1)} %bitcast.68), kind=kOutput, calls=%fused_computation.4 | convolution fusion | flops 1073741824 | bytes 6815744 | tf_op jit(solution)/shard_map/dot_general | solution.py:57
  247.1 0.7 copy.49
  247.8 64.9 %psum.15 = f32[128]{0:T(128)} all-reduce(f32[128]{0:T(128)S(1)} %get-tuple-element.20), channel_id=1, replica_groups=mesh['seq'=16,'res'=8] {'seq','res'}, use_global_device_ids=true, to_apply=%region_5.0 | all-reduce | flops 128 | bytes 1024 | tf_op jit(solution)/shard_map/psum | solution.py:78
  312.7 1.3 fusion.7
  314.0 3.2 copy-done.1
  317.3 8.7 %fusion.9 = f32[32,32,128]{2,1,0:T(8,128)} fusion(bf16[16,32,32,1]{2,0,1,3:T(8,128)(2,1)S(1)} %get-tuple-element.25, f32[16,32,32,128]{3,1,2,0:T(8,128)S(1)} %fusion.7), kind=kOutput, calls=%fused_computation.11 | convolution fusion | flops 805306368 | bytes 8945664 | tf_op jit(solution)/shard_map/sjd,scjh->cdh/dot_general | solution.py:71
  326.0 10.4 %fusion.15 = f32[16,32,32]{2,1,0:T(8,128)} fusion(f32[16,32,32,128]{3,1,2,0:T(8,128)} %copy-done.1, bf16[32,32,128]{2,1,0:T(8,128)(2,1)S(1)} %copy-done, f32[16,32]{1,0:T(8,128)S(1)} %get-tuple-element.23), kind=kOutput, calls=%fused_computation.13 | convolution fusion | flops 805322752 | bytes 8718336 | tf_op jit(solution)/shard_map/scjh,cdh->sjd/dot_general | solution.py:68
  336.4 1.0 reshape.34
  337.4 0.8 bitcast_multiply_fusion
  338.2 130.6 %all-reduce.2.cloned.1.call-done = f32[32,32,128]{2,1,0:T(8,128)} async-done(((f32[32,32,128]{2,1,0:T(8,128)}), f32[32,32,128]{2,1,0:T(8,128)}) %all-reduce.2.cloned.1.call-update) | async-done | bytes 524304 | tf_op jit(solution)/shard_map/psum | solution.py:78
  468.8 1.9 copy.89
  (20 shorter events, 0.3 us)
Async XLA Ops:
  7.2 56.2 %copy-start = (bf16[32,32,128]{2,1,0:T(8,128)(2,1)S(1)}, bf16[32,32,128]{2,1,0:T(8,128)(2,1)}, u32[]{:S(2)}) copy-start(bf16[32,32,128]{2,1,0:T(8,128)(2,1)} %param.9) | copy-start | bytes 786436
  7.2 93.4 %reduce-scatter.6.cloned.1.call-start = ((), (), s32[]{:S(2)}) async-start(), calls=%async_computation.4 | async-start | bytes 69632 | tf_op jit(solution)/shard_map/reduce_scatter | solution.py:34
  33.8 150.9 %reduce-scatter.4.cloned.1.call-start = ((), (), s32[]{:S(2)}) async-start(), calls=%async_computation.3 | async-start | bytes 4456448 | tf_op jit(solution)/shard_map/reduce_scatter | solution.py:40
  64.6 6.3 %copy-start.2 = (bf16[16,32,32,128]{3,1,2,0:T(8,128)(2,1)}, bf16[16,32,32,128]{3,1,2,0:T(8,128)(2,1)S(1)}, u32[]{:S(2)}) copy-start(bf16[16,32,32,128]{3,1,2,0:T(8,128)(2,1)S(1)} %convolution_convert_fusion) | copy-start | bytes 12582916
  82.8 101.9 %copy-start.3 = (bf16[16,32,128]{2,1,0:T(8,128)(2,1)S(1)}, bf16[16,32,128]{2,1,0:T(8,128)(2,1)}, u32[]{:S(2)}) copy-start(bf16[16,32,128]{2,1,0:T(8,128)(2,1)} %param.11) | copy-start | bytes 393220
  82.8 101.9 %copy-start.4 = (f32[128]{0:T(128)S(1)}, f32[128]{0:T(128)}, u32[]{:S(2)}) copy-start(f32[128]{0:T(128)} %param.10) | copy-start | bytes 1540
  82.8 155.2 %all-gather.3.cloned.1.call-start = ((), (), s32[]{:S(2)}) async-start(), calls=%async_computation.5 | async-start | bytes 2228224 | tf_op jit(solution)/shard_map/all_gather | solution.py:50
  186.4 150.0 %reduce-scatter.8.cloned.1.call-start = ((), (), s32[]{:S(2)}) async-start(), calls=%async_computation.6 | async-start | bytes 589824 | tf_op jit(solution)/shard_map/reduce_scatter | solution.py:60
  247.1 221.8 %all-reduce.2.cloned.1.call-start = ((), (), s32[]{:S(2)}) async-start(), calls=%async_computation.7 | async-start | bytes 1048576 | tf_op jit(solution)/shard_map/psum | solution.py:78
  314.0 3.2 copy-start.1
Sparse Core Ops, SparseCore 0:
  33.9 66.6 reduce-scatter.5
  104.6 79.9 reduce-scatter.3
  187.7 50.2 all-gather.2
  247.2 31.7 reduce-scatter.7
  326.1 142.6 all-reduce.1
where the time goes:
time: 478 us; the launch traced here: 477 us
  waiting for transfers between devices  283 us (59%)
  blocking collectives  116 us (24%)
  matrix products  34.6 us (7%)
  local copies, waits for them, and re-layouts  23.8 us (5%)
  between operations  13.9 us (3%)
  other arithmetic  5.16 us (1%)
    psum x1, waiting for transfers between devices, per_device(): lax.psum((weight_terms, bias_terms), ('seq', 'res'))  131 us
    reduce_scatter x1, waiting for transfers between devices, per_device(): lax.psum_scatter(jnp.dot(picked, proj_flat, preferred_element_type=jnp.fl...  83.3 us
    psum x1, blocking collectives, per_device(): lax.psum((weight_terms, bias_terms), ('seq', 'res'))  64.9 us
    all_gather x1, waiting for transfers between devices, per_device(): portion = lax.all_gather(scaled, 'seq', axis=0, tiled=True)  51.4 us
    all_gather x1, blocking collectives, per_device(): left_all = lax.all_gather(left_under_mask, 'res', axis=1, tiled=True)  26.7 us
    all_gather x1, blocking collectives, per_device(): full_mask = lax.all_gather(alignment_mask, 'res', axis=1, tiled=True)  24.7 us
    reduce_scatter x1, waiting for transfers between devices, per_device(): lax.psum_scatter(count_terms.astype(jnp.bfloat16), 'seq', scatter_dimensi...  17.7 us
    unnamed x13, local copies, waits for them, and re-layouts  12 us
  transfers between devices with their start and end apart: 5, of which 4 were waited for; matrix products, arithmetic and copies ran while one was open for 10% of the time, Pallas kernels for 0%

commit v1 on v0

v1 whole, which is shorter than its diff:
```python
import jax
import jax.numpy as jnp
from jax import lax
from jax.experimental import pallas as pl
from jax.experimental.pallas import tpu as pltpu
from jax.sharding import PartitionSpec as P

F32 = jnp.float32
BF16 = jnp.bfloat16
ROWS_ROWS = (((0,), (0,)), ((), ()))
LANES_LANES = (((1,), (1,)), ((), ()))


def iota(shape, dim):
    return lax.broadcasted_iota(jnp.int32, shape, dim)


def swap_groups(blocks):
    lane = iota(blocks[0].shape, 1)
    upper = lane >= 64
    odd = (lane // 32) % 2 == 1
    b0, b1, b2, b3 = blocks
    r0, r1, r2, r3 = (pltpu.roll(b, 64, 1) for b in blocks)
    b0, b2 = jnp.where(upper, r2, b0), jnp.where(upper, b2, r0)
    b1, b3 = jnp.where(upper, r3, b1), jnp.where(upper, b3, r1)
    up1, up3 = pltpu.roll(b1, 32, 1), pltpu.roll(b3, 32, 1)
    down0, down2 = pltpu.roll(b0, 96, 1), pltpu.roll(b2, 96, 1)
    return (
        jnp.where(odd, up1, b0),
        jnp.where(odd, b1, down0),
        jnp.where(odd, up3, b2),
        jnp.where(odd, b3, down2),
    )


def pair_kernel(
    g_ref, w_ref, bias_ref, cot_ref, pair_ref, msg_ref, bsum_ref,
    y_ref, x_ref, dx_ref, dy_ref, plain_ref, cot32_ref, scaled_ref,
):
    row, col = iota((256, 256), 0), iota((256, 256), 1)
    order = (col == (row % 16) * 16 + row // 16).astype(F32).astype(BF16)
    g = jnp.dot(order, g_ref[...], preferred_element_type=F32).astype(BF16)
    masks = g[:, 1536:]
    spread_i = (iota((128, 512), 0) == iota((128, 512), 1) % 16).astype(F32).astype(BF16)
    spread_jd = (iota((128, 1024), 0) == 16 + iota((128, 1024), 1) // 32).astype(F32).astype(BF16)
    lane = iota((128, 512), 1)
    spread_j = (iota((128, 512), 0) == 16 + 4 * ((lane // 16) % 8) + lane // 128).astype(F32).astype(BF16)
    mask_i = jnp.dot(masks, spread_i, preferred_element_type=F32)
    mask_jd = jnp.dot(masks, spread_jd, preferred_element_type=F32)
    mask_j = jnp.dot(masks, spread_j, preferred_element_type=F32)
    left = g[:, :512] * mask_i.astype(BF16)
    right = g[:, 512:1536] * mask_jd.astype(BF16)
    both = (mask_i * mask_j).astype(BF16)
    counts = (
        lax.dot_general(both, jnp.ones((256, 128), BF16), ROWS_ROWS, preferred_element_type=F32) + 1e-3
    )

    cot32 = cot_ref[...].astype(F32)
    cot32_ref[...] = cot32
    bsum_ref[...] = jnp.sum(cot32, axis=0, keepdims=True)
    for j in range(32):
        at = ((j % 4) * 8 + j // 4) * 16
        scaled_ref[at : at + 16, :] = (
            cot32_ref[pl.ds(j, 16, stride=32), :] / counts[at : at + 16, :]
        ).astype(BF16)

    y_ref[...] = lax.dot_general(left, right, ROWS_ROWS, preferred_element_type=F32)
    for u in range(8):
        lanes = slice(u * 128, u * 128 + 128)
        for t in range(8):
            tiles = swap_groups([y_ref[f * 128 + t * 16 : f * 128 + t * 16 + 16, lanes] for f in range(4)])
            for e in range(4):
                at = (e * 8 + u) * 16
                x_ref[at : at + 16, t * 128 : t * 128 + 128] = tiles[e].astype(BF16)

    summed = jnp.dot(x_ref[...], w_ref[...], preferred_element_type=F32)
    update = summed / counts + bias_ref[...]
    for j in range(32):
        at = ((j % 4) * 8 + j // 4) * 16
        plain_ref[pl.ds(j, 16, stride=32), :] = update[at : at + 16, :]
    pair_ref[...] = plain_ref[...].astype(BF16)

    scaled = scaled_ref[...]
    dx_ref[...] = lax.dot_general(scaled, w_ref[...], LANES_LANES, preferred_element_type=F32)
    for u in range(8):
        lanes = slice(u * 128, u * 128 + 128)
        for t in range(8):
            tiles = swap_groups(
                [dx_ref[(e * 8 + u) * 16 : (e * 8 + u) * 16 + 16, t * 128 : t * 128 + 128] for e in range(4)]
            )
            for f in range(4):
                dy_ref[f * 128 + t * 16 : f * 128 + t * 16 + 16, lanes] = tiles[f].astype(BF16)

    weight_part = lax.dot_general(x_ref[...], scaled, ROWS_ROWS, preferred_element_type=F32)
    right_part = jnp.dot(left, dy_ref[...], preferred_element_type=F32) * mask_jd
    left_part = lax.dot_general(right, dy_ref[...], LANES_LANES, preferred_element_type=F32) * mask_i
    for m in range(128):
        s, k = m // 8, m % 8
        msg_ref[m, 0:16, :] = right_part[s * 16 : s * 16 + 16, k * 128 : k * 128 + 128].astype(BF16)
        at = s * 16 + (k % 2) * 8
        msg_ref[m, 16:32, :] = jnp.concatenate(
            [weight_part[m * 8 : m * 8 + 8, :], left_part[at : at + 8, (k // 2) * 128 : (k // 2) * 128 + 128]], 0
        ).astype(BF16)


def reduce_kernel(in_ref, bsum_ref, out_ref, rows_ref):
    half = lax.rem(lax.axis_index("res"), 2)
    weight = jnp.zeros((8, 128), F32)
    for r in range(8):
        total = jnp.zeros((16, 128), F32)
        for q in range(16):
            total = total + in_ref[q * 8 + r, 0:16, :].astype(F32)
        rows_ref[pl.ds(r * 8, 16, stride=64), :] = total
    for q in range(16):
        total = jnp.zeros((16, 128), F32)
        for r in range(8):
            total = total + in_ref[q * 8 + r, 16:32, :].astype(F32)
        weight = weight + total[0:8]
        for side in range(2):
            at = side * 512 + (q // 2) * 8 + 1 + q % 2
            rows_ref[pl.ds(at, 8, stride=64), :] = jnp.where(half == side, total[8:16], 0.0)
    bias = jnp.broadcast_to(bsum_ref[...], (8, 128))
    high = bias.astype(BF16).astype(F32)
    low = bias - high
    sub = iota((8, 128), 0)
    for m in range(128):
        rows = rows_ref[m * 8 : m * 8 + 8, :]
        rows = jnp.where(sub < 3, rows, jnp.where(sub == 3, high, jnp.where(sub == 4, low, 0.0)))
        out_ref[m] = jnp.concatenate([weight, rows], 0).astype(BF16)


def final_kernel(in_ref, weight_ref, right_ref, left_ref, bias_ref, rows_ref):
    total = jnp.zeros((8, 128), F32)
    for m in range(128):
        block = in_ref[m].astype(F32)
        weight_ref[m * 8 : m * 8 + 8, :] = block[0:8]
        rows_ref[m * 8 : m * 8 + 8, :] = block[8:16]
        total = total + block[8:16]
    right_ref[...] = rows_ref[pl.ds(0, 128, stride=8), :]
    for h in range(2):
        left_ref[h] = rows_ref[pl.ds(1 + h, 64, stride=16), :] + rows_ref[pl.ds(9 + h, 64, stride=16), :]
    bias_ref[...] = total[3:4] + total[4:5]


def call(kernel, outs, scratch, *args):
    whole = pl.BlockSpec(memory_space=pltpu.VMEM)
    return pl.pallas_call(
        kernel,
        out_shape=outs,
        in_specs=[whole] * len(args),
        out_specs=tuple([whole] * len(outs)),
        scratch_shapes=scratch,
        compiler_params=pltpu.CompilerParams(vmem_limit_bytes=40 * 1024 * 1024),
    )(*args)


def shape(dims, dtype):
    return jax.ShapeDtypeStruct(dims, dtype)


def per_device(left, right, mask, weight, bias, cotangent):
    mask = mask.astype(BF16)
    left = left.reshape(16, 2, 16, 8, 4).transpose(1, 0, 4, 3, 2).reshape(2, 16, 512)
    mask_i = jnp.pad(mask.reshape(16, 2, 16).transpose(1, 0, 2), ((0, 0), (0, 0), (0, 112)))
    block = jnp.concatenate([left, mask_i], -1)
    block = lax.all_to_all(jnp.broadcast_to(block, (8, 2, 16, 640)), "res", 0, 0, tiled=True)
    block = block.reshape(16, 16, 640)
    mask_j = jnp.pad(mask, ((0, 0), (16, 80)))
    block = jnp.concatenate(
        [
            block[:, :, :512],
            jnp.broadcast_to(right.reshape(16, 1024), (16, 16, 1024)),
            block[:, :, 512:] + mask_j,
        ],
        -1,
    )
    block = lax.all_to_all(block, "seq", 0, 0, tiled=True).reshape(256, 1664)

    pair_update, parts, bias_part = call(
        pair_kernel,
        (shape((512, 128), BF16), shape((128, 32, 128), BF16), shape((1, 128), F32)),
        [
            pltpu.VMEM((512, 1024), F32),
            pltpu.VMEM((512, 1024), BF16),
            pltpu.VMEM((512, 1024), F32),
            pltpu.VMEM((512, 1024), BF16),
            pltpu.VMEM((512, 128), F32),
            pltpu.VMEM((512, 128), F32),
            pltpu.VMEM((512, 128), BF16),
        ],
        block,
        weight.reshape(1024, 128),
        bias.reshape(1, 128),
        cotangent.reshape(512, 128),
    )
    parts = lax.all_to_all(parts, ("seq", "res"), 0, 0, tiled=True)
    (sums,) = call(
        reduce_kernel, (shape((128, 16, 128), BF16),), [pltpu.VMEM((1024, 128), F32)], parts, bias_part
    )
    sums = lax.all_to_all(sums, ("seq", "res"), 0, 0, tiled=True)
    weight_grad, right_grad, left_grad, bias_grad = call(
        final_kernel,
        (shape((1024, 128), F32), shape((128, 128), F32), shape((2, 64, 128), F32), shape((1, 128), F32)),
        [pltpu.VMEM((1024, 128), F32)],
        sums,
    )
    left_grad = left_grad.reshape(2, 16, 4, 8, 16).transpose(1, 0, 4, 3, 2).reshape(16, 32, 32)
    return (
        pair_update.reshape(16, 32, 128),
        left_grad,
        right_grad.reshape(16, 32, 32),
        weight_grad.reshape(32, 32, 128),
        bias_grad.reshape(128),
    )


def solution(mesh):
    return jax.shard_map(
        per_device,
        mesh=mesh,
        in_specs=(
            P("seq", "res", None),
            P("seq", "res", None),
            P("seq", "res"),
            P(),
            P(),
            P("seq", "res", None),
        ),
        out_specs=(P("seq", "res", None), P("seq", "res", None), P("seq", "res", None), P(), P()),
        check_vma=False,
    )
```

time: 478 us -> 90.6 us (0.19)
  waiting for transfers between devices: 283 us -> 6.81 us
  blocking collectives: 116 us -> 63.9 us
  matrix products: 34.6 us -> 0 us
  local copies, waits for them, and re-layouts: 23.8 us -> 5.24 us
  between operations: 13.9 us -> 0.76 us
  starting transfers between devices: 0.39 us -> 6.88 us
  Pallas kernels: 0 us -> 5.85 us
    psum x1 -> x0, waiting for transfers between devices: 131 us -> none  [per_device(): lax.psum((weight_terms, bias_terms), ('seq', 'res'))]
    reduce_scatter x3 -> x0, waiting for transfers between devices: 101 us -> none  [the longest x1 83.3 us: per_device(): lax.psum_scatter(jnp.dot(picked, proj_flat, preferred_element_type=jnp.fl...]
    psum x1 -> x0, blocking collectives: 64.9 us -> none  [per_device(): lax.psum((weight_terms, bias_terms), ('seq', 'res'))]
    all_to_all x0 -> x3, blocking collectives: none -> 63.9 us  [the longest x1 23.6 us: per_device(): block = lax.all_to_all(block, 'seq', 0, 0, tiled=True).reshape(256, 1664)]
    all_gather x1 -> x0, waiting for transfers between devices: 51.4 us -> none  [per_device(): portion = lax.all_gather(scaled, 'seq', axis=0, tiled=True)]
    all_gather x2 -> x0, blocking collectives: 51.4 us -> none  [the longest x1 26.7 us: per_device(): left_all = lax.all_gather(left_under_mask, 'res', axis=1, tiled=True)]
    dot_general x7 -> x0, matrix products: 34.6 us -> none  [the longest x1 10.4 us: per_device(): jnp.einsum('scjh,cdh->sjd', grad_four, weight32, precision=lax.Precision....]
    unnamed x13 -> x10, local copies, waits for them, and re-layouts: 12 us -> 1.88 us
  transfers between devices with their start and end apart: 5 -> 1, of which waited for: 4 -> 1; matrix products, arithmetic and copies ran while one was open for 10% -> 0% of each run, Pallas kernels for 0% -> 0%
where the time goes in v1:
time: 90.6 us; the launch traced here: 90.2 us
  blocking collectives  63.9 us (71%)
  starting transfers between devices  6.88 us (8%)
  waiting for transfers between devices  6.81 us (8%)
  Pallas kernels  5.85 us (6%)
  local copies, waits for them, and re-layouts  5.24 us (6%)
    all_to_all x1, blocking collectives, per_device(): block = lax.all_to_all(block, 'seq', 0, 0, tiled=True).reshape(256, 1664)  23.6 us
    all_to_all x1, blocking collectives, per_device(): parts = lax.all_to_all(parts, ('seq', 'res'), 0, 0, tiled=True)  22.6 us
    all_to_all x1, blocking collectives, per_device(): sums = lax.all_to_all(sums, ('seq', 'res'), 0, 0, tiled=True)  17.8 us
    all_to_all x1, starting transfers between devices, per_device(): lax.all_to_all(jnp.broadcast_to(block, (8, 2, 16, 640)), 'res', 0, 0, til...  6.88 us
    all_to_all x1, waiting for transfers between devices, per_device(): lax.all_to_all(jnp.broadcast_to(block, (8, 2, 16, 640)), 'res', 0, 0, til...  6.81 us
    pallas_call x3, Pallas kernels, call(): pl.pallas_call(kernel, out_shape=outs, in_specs=[whole] * len(args), out_...  5.85 us
    unnamed x10, local copies, waits for them, and re-layouts  1.88 us
  transfers between devices with their start and end apart: 1, of which 1 were waited for; matrix products, arithmetic and copies ran while one was open for 0% of the time, Pallas kernels for 0%

profile of v1, /device:TPU:1, one launch (start us, length us, event | category | flops | bytes accessed | tf_op | source)
XLA Modules:
  0.0 90.2 jit_solution(7034834514394120919)
XLA Ops:
  0.6 0.7 convert_element_type.7
  1.3 0.1 reshape.58
  1.4 1.0 %copy.17 = bf16[16,32,32]{1,2,0:T(8,128)(2,1)S(1)} copy(bf16[16,32,32]{2,1,0:T(8,128)(2,1)} %param.6) | data formatting | bytes 65536 | tf_op args[0]
  2.4 0.1 reshape.56
  2.6 0.0 copy-start.3
  2.6 0.3 reshape.57
  3.0 0.8 broadcast_in_dim.7
  3.7 6.9 %all-to-all-start = ((bf16[8,2,16,640]{3,2,1,0:T(8,128)(2,1)}), bf16[8,2,16,640]{3,2,1,0:T(8,128)(2,1)S(1)}, u32[]{:S(2)}, u32[]{:S(2)}) async-start(bf16[8,2,16,640]{3,2,1,0:T(8,128)(2,1)} %broadcast_in_dim.7), calls=%async_computation | async-start | bytes 655360 | tf_op jit(solution)/shard_map/all_to_all | solution.py:166
  10.6 0.1 pad.9
  10.7 0.0 copy-done.3
  10.7 0.2 reshape.60
  10.9 6.8 %all-to-all-done = bf16[8,2,16,640]{3,2,1,0:T(8,128)(2,1)S(1)} async-done(((bf16[8,2,16,640]{3,2,1,0:T(8,128)(2,1)}), bf16[8,2,16,640]{3,2,1,0:T(8,128)(2,1)S(1)}, u32[]{:S(2)}, u32[]{:S(2)}) %all-to-all-start) | async-done | bytes 327712 | tf_op jit(solution)/shard_map/all_to_all | solution.py:166
  17.7 0.1 broadcast_in_dim.8
  17.8 0.1 pad_maximum_fusion
  17.8 0.0 copy-start
  17.9 0.0 copy-start.1
  17.9 0.0 copy-start.2
  17.9 23.6 %all_to_all.20 = bf16[16,16,1664]{2,1,0:T(8,128)(2,1)S(1)} all-to-all(bf16[16,16,1664]{2,1,0:T(8,128)(2,1)S(1)} %pad_maximum_fusion), channel_id=1, replica_groups=mesh['seq'=16,'res'=8] {'seq'}, dimensions={0} | all-to-all | bytes 1703936 | tf_op jit(solution)/shard_map/all_to_all | solution.py:177
  41.5 0.0 copy-done
  41.5 0.0 copy-done.1
  41.5 0.0 copy-done.2
  41.5 4.7 %shard_map.101 = (bf16[512,128]{1,0:T(8,128)(2,1)}, bf16[128,32,128]{2,1,0:T(8,128)(2,1)S(1)}, f32[1,128]{1,0:T(1,128)S(1)}) custom-call(bf16[256,1664]{1,0:T(8,128)(2,1)S(1)} %bitcast.21, bf16[1024,128]{1,0:T(8,128)(2,1)S(1)} %bitcast.22, f32[1,128]{1,0:T(1,128)S(1)} %bitcast.24, bf16[512,128]{1,0:T(8,128)(2,1)S(1)} %bitcast.23), custom_call_target="tpu_custom_call" | custom-call | tf_op jit(solution)/shard_map/pallas_call | solution.py:147
  46.2 22.6 %all_to_all.21.in_ref = bf16[128,32,128]{2,1,0:T(8,128)(2,1)S(1)} all-to-all(bf16[128,32,128]{2,1,0:T(8,128)(2,1)S(1)} %get-tuple-element.13), channel_id=1, replica_groups=mesh['seq'=16,'res'=8] {'seq','res'}, dimensions={0} | all-to-all | bytes 2097152 | tf_op jit(solution)/shard_map/all_to_all | solution.py:196
  68.7 0.3 shard_map.102
  69.0 17.8 %all_to_all.22.in_ref = bf16[128,16,128]{2,1,0:T(8,128)(2,1)S(1)} all-to-all(bf16[128,16,128]{2,1,0:T(8,128)(2,1)S(1)} %shard_map.102), channel_id=1, replica_groups=mesh['seq'=16,'res'=8] {'seq','res'}, dimensions={0} | all-to-all | bytes 1048576 | tf_op jit(solution)/shard_map/all_to_all | solution.py:200
  86.8 0.9 shard_map.103
  87.7 0.8 reshape.68
  88.5 0.2 reshape.66
  88.7 0.4 copy.24
  89.1 0.3 reshape.67
  89.4 0.8 copy.21
  (5 shorter events, 0.1 us)
Async XLA Ops:
  2.6 8.1 %copy-start.3 = (bf16[16,32,32]{2,1,0:T(8,128)(2,1)S(1)}, bf16[16,32,32]{2,1,0:T(8,128)(2,1)}, u32[]{:S(2)}) copy-start(bf16[16,32,32]{2,1,0:T(8,128)(2,1)} %param.7) | copy-start | bytes 98308
  3.7 13.9 %all-to-all-start = ((bf16[8,2,16,640]{3,2,1,0:T(8,128)(2,1)}), bf16[8,2,16,640]{3,2,1,0:T(8,128)(2,1)S(1)}, u32[]{:S(2)}, u32[]{:S(2)}) async-start(bf16[8,2,16,640]{3,2,1,0:T(8,128)(2,1)} %broadcast_in_dim.7), calls=%async_computation | async-start | bytes 655360 | tf_op jit(solution)/shard_map/all_to_all | solution.py:166
  17.8 23.6 %copy-start = (bf16[32,32,128]{2,1,0:T(8,128)(2,1)S(1)}, bf16[32,32,128]{2,1,0:T(8,128)(2,1)}, u32[]{:S(2)}) copy-start(bf16[32,32,128]{2,1,0:T(8,128)(2,1)} %param.9) | copy-start | bytes 786436
  17.9 23.6 %copy-start.1 = (bf16[16,32,128]{2,1,0:T(8,128)(2,1)S(1)}, bf16[16,32,128]{2,1,0:T(8,128)(2,1)}, u32[]{:S(2)}) copy-start(bf16[16,32,128]{2,1,0:T(8,128)(2,1)} %param.11) | copy-start | bytes 393220
  17.9 23.6 %copy-start.2 = (f32[128]{0:T(128)S(1)}, f32[128]{0:T(128)}, u32[]{:S(2)}) copy-start(f32[128]{0:T(128)} %param.10) | copy-start | bytes 1540

commit v2 on v1

--- a/solution.py
+++ b/solution.py
@@ -31,6 +31,45 @@
         jnp.where(odd, up3, b2),
         jnp.where(odd, b3, down2),
     )
+
+
+def choose(condition):
+    return condition.astype(F32).astype(BF16)
+
+
+def channel_lanes():
+    lane = iota((32, 512), 1)
+    return choose(iota((32, 512), 0) == 4 * ((lane % 128) // 16) + lane // 128)
+
+
+def own_residue():
+    return iota((512, 512), 0) % 16 == iota((512, 512), 1) % 16
+
+
+def prep_kernel(left_hbm, mask_hbm, out_ref, left_ref, mask_ref, sems):
+    copies = [
+        pltpu.make_async_copy(left_hbm, left_ref, sems.at[0]),
+        pltpu.make_async_copy(mask_hbm, mask_ref, sems.at[1]),
+    ]
+    for copy in copies:
+        copy.start()
+    for copy in copies:
+        copy.wait()
+    spread = jnp.dot(left_ref[...], channel_lanes(), preferred_element_type=F32)
+    spread = jnp.where(own_residue(), spread, 0.0).astype(BF16)
+    row, col = iota((32, 512), 0), iota((32, 512), 1)
+    gather = choose((col // 32 == row % 16) & ((col % 32) // 16 == row // 16))
+    block = jnp.dot(gather, spread, preferred_element_type=F32).astype(BF16)
+    mask = mask_ref[...].astype(F32).astype(BF16)
+    row, col = iota((32, 128), 0), iota((32, 128), 1)
+    halves = [
+        jnp.dot(mask, choose((row == h * 16 + col) & (col < 16)), preferred_element_type=F32)
+        for h in range(2)
+    ]
+    masks = jnp.concatenate(halves, 0).astype(BF16)
+    for r in range(8):
+        out_ref[r, :, 0:512] = block
+        out_ref[r, :, 512:640] = masks
 
 
 def pair_kernel(
@@ -55,14 +94,16 @@
         lax.dot_general(both, jnp.ones((256, 128), BF16), ROWS_ROWS, preferred_element_type=F32) + 1e-3
     )
 
+    inverse = 1.0 / counts
     cot32 = cot_ref[...].astype(F32)
     cot32_ref[...] = cot32
     bsum_ref[...] = jnp.sum(cot32, axis=0, keepdims=True)
     for j in range(32):
         at = ((j % 4) * 8 + j // 4) * 16
         scaled_ref[at : at + 16, :] = (
-            cot32_ref[pl.ds(j, 16, stride=32), :] / counts[at : at + 16, :]
+            cot32_ref[pl.ds(j, 16, stride=32), :] * inverse[at : at + 16, :]
         ).astype(BF16)
+    scaled = scaled_ref[...]
 
     y_ref[...] = lax.dot_general(left, right, ROWS_ROWS, preferred_element_type=F32)
     for u in range(8):
@@ -73,14 +114,6 @@
                 at = (e * 8 + u) * 16
                 x_ref[at : at + 16, t * 128 : t * 128 + 128] = tiles[e].astype(BF16)
 
-    summed = jnp.dot(x_ref[...], w_ref[...], preferred_element_type=F32)
-    update = summed / counts + bias_ref[...]
-    for j in range(32):
-        at = ((j % 4) * 8 + j // 4) * 16
-        plain_ref[pl.ds(j, 16, stride=32), :] = update[at : at + 16, :]
-    pair_ref[...] = plain_ref[...].astype(BF16)
-
-    scaled = scaled_ref[...]
     dx_ref[...] = lax.dot_general(scaled, w_ref[...], LANES_LANES, preferred_element_type=F32)
     for u in range(8):
         lanes = slice(u * 128, u * 128 + 128)
@@ -90,6 +123,12 @@
             )
             for f in range(4):
                 dy_ref[f * 128 + t * 16 : f * 128 + t * 16 + 16, lanes] = tiles[f].astype(BF16)
+
+    update = jnp.dot(x_ref[...], w_ref[...], preferred_element_type=F32) * inverse + bias_ref[...]
+    for j in range(32):
+        at = ((j % 4) * 8 + j // 4) * 16
+        plain_ref[pl.ds(j, 16, stride=32), :] = update[at : at + 16, :]
+    pair_ref[...] = plain_ref[...].astype(BF16)
 
     weight_part = lax.dot_general(x_ref[...], scaled, ROWS_ROWS, preferred_element_type=F32)
     right_part = jnp.dot(left, dy_ref[...], preferred_element_type=F32) * mask_jd
@@ -136,21 +175,41 @@
         weight_ref[m * 8 : m * 8 + 8, :] = block[0:8]
         rows_ref[m * 8 : m * 8 + 8, :] = block[8:16]
         total = total + block[8:16]
-    right_ref[...] = rows_ref[pl.ds(0, 128, stride=8), :]
-    for h in range(2):
-        left_ref[h] = rows_ref[pl.ds(1 + h, 64, stride=16), :] + rows_ref[pl.ds(9 + h, 64, stride=16), :]
+    for k in range(8):
+        tile = rows_ref[pl.ds(k * 8, 16, stride=64), :]
+        for e in range(4):
+            right_ref[pl.ds(k * 4 + e, 16, stride=32), :] = tile[:, e * 32 : e * 32 + 32]
+    left = jnp.concatenate(
+        [
+            jnp.concatenate(
+                [
+                    rows_ref[pl.ds(f * 16 + 1 + h, 16, stride=64), :]
+                    + rows_ref[pl.ds(f * 16 + 9 + h, 16, stride=64), :]
+                    for f in range(4)
+                ],
+                1,
+            )
+            for h in range(2)
+        ],
+        0,
+    ).astype(BF16)
+    row, col = iota((512, 32), 0), iota((512, 32), 1)
+    scatter = choose((row // 32 == col % 16) & ((row % 32) // 16 == col // 16))
+    spread = jnp.dot(scatter, left, preferred_element_type=F32)
+    spread = jnp.where(own_residue(), spread, 0.0).astype(BF16)
+    left_ref[...] = lax.dot_general(spread, channel_lanes(), LANES_LANES, preferred_element_type=F32)
     bias_ref[...] = total[3:4] + total[4:5]
 
 
-def call(kernel, outs, scratch, *args):
+def call(kernel, outs, scratch, *args, space=pltpu.VMEM, mib=40):
     whole = pl.BlockSpec(memory_space=pltpu.VMEM)
     return pl.pallas_call(
         kernel,
         out_shape=outs,
-        in_specs=[whole] * len(args),
+        in_specs=[pl.BlockSpec(memory_space=space)] * len(args),
         out_specs=tuple([whole] * len(outs)),
         scratch_shapes=scratch,
-        compiler_params=pltpu.CompilerParams(vmem_limit_bytes=40 * 1024 * 1024),
+        compiler_params=pltpu.CompilerParams(vmem_limit_bytes=mib * 1024 * 1024),
     )(*args)
 
 
@@ -159,13 +218,19 @@
 
 
 def per_device(left, right, mask, weight, bias, cotangent):
-    mask = mask.astype(BF16)
-    left = left.reshape(16, 2, 16, 8, 4).transpose(1, 0, 4, 3, 2).reshape(2, 16, 512)
-    mask_i = jnp.pad(mask.reshape(16, 2, 16).transpose(1, 0, 2), ((0, 0), (0, 0), (0, 112)))
-    block = jnp.concatenate([left, mask_i], -1)
-    block = lax.all_to_all(jnp.broadcast_to(block, (8, 2, 16, 640)), "res", 0, 0, tiled=True)
+    (block,) = call(
+        prep_kernel,
+        (shape((8, 32, 640), BF16),),
+        [pltpu.VMEM((512, 32), BF16), pltpu.VMEM((16, 32), jnp.int32), pltpu.SemaphoreType.DMA((2,))],
+        left.reshape(512, 32),
+        mask,
+        space=pltpu.HBM,
+        mib=60,
+    )
+    block = lax.all_to_all(block, "res", 0, 0, tiled=True)
+    block, right, mask = lax.optimization_barrier((block, right, mask))
     block = block.reshape(16, 16, 640)
-    mask_j = jnp.pad(mask, ((0, 0), (16, 80)))
+    mask_j = jnp.pad(mask.astype(BF16), ((0, 0), (16, 80)))
     block = jnp.concatenate(
         [
             block[:, :, :512],
@@ -200,14 +265,13 @@
     sums = lax.all_to_all(sums, ("seq", "res"), 0, 0, tiled=True)
     weight_grad, right_grad, left_grad, bias_grad = call(
         final_kernel,
-        (shape((1024, 128), F32), shape((128, 128), F32), shape((2, 64, 128), F32), shape((1, 128), F32)),
+        (shape((1024, 128), F32), shape((512, 32), F32), shape((512, 32), F32), shape((1, 128), F32)),
         [pltpu.VMEM((1024, 128), F32)],
         sums,
     )
-    left_grad = left_grad.reshape(2, 16, 4, 8, 16).transpose(1, 0, 4, 3, 2).reshape(16, 32, 32)
     return (
         pair_update.reshape(16, 32, 128),
-        left_grad,
+        left_grad.reshape(16, 32, 32),
         right_grad.reshape(16, 32, 32),
         weight_grad.reshape(32, 32, 128),
         bias_grad.reshape(128),

time: 90.6 us -> 86.9 us (0.959)
  blocking collectives: 63.9 us -> 78 us
  starting transfers between devices: 6.88 us -> 0 us
  waiting for transfers between devices: 6.81 us -> 0 us
  local copies, waits for them, and re-layouts: 5.24 us -> 0.35 us
  Pallas kernels: 5.85 us -> 7.48 us
    all_to_all x0 -> x1, blocking collectives: none -> 14 us  [per_device(): block = lax.all_to_all(block, 'res', 0, 0, tiled=True)]
    all_to_all x1 -> x0, starting transfers between devices: 6.88 us -> none  [per_device(): lax.all_to_all(jnp.broadcast_to(block, (8, 2, 16, 640)), 'res', 0, 0, til...]
    all_to_all x1 -> x0, waiting for transfers between devices: 6.81 us -> none  [per_device(): lax.all_to_all(jnp.broadcast_to(block, (8, 2, 16, 640)), 'res', 0, 0, til...]
    reshape x8 -> x0, local copies, waits for them, and re-layouts: 2.25 us -> none  [the longest x3 0.89 us: per_device(): left_grad.reshape(2, 16, 4, 8, 16).transpose(1, 0, 4, 3, 2)]
    unnamed x10, local copies, waits for them, and re-layouts: 1.88 us -> 0.03 us
    pallas_call x3 -> x4, Pallas kernels: 5.85 us -> 7.48 us  [call(): pl.pallas_call(kernel, out_shape=outs, in_specs=[pl.BlockSpec(memory_spac...]
  transfers between devices with their start and end apart: 1 -> 0, of which waited for: 1 -> 0; matrix products, arithmetic and copies ran while one was open for 0% -> 0% of each run, Pallas kernels for 0% -> 0%
where the time goes in v2:
time: 86.9 us; the launch traced here: 86.6 us
  blocking collectives  78 us (90%)
  Pallas kernels  7.48 us (9%)
    all_to_all x1, blocking collectives, per_device(): block = lax.all_to_all(block, 'seq', 0, 0, tiled=True).reshape(256, 1664)  23.7 us
    all_to_all x1, blocking collectives, per_device(): parts = lax.all_to_all(parts, ('seq', 'res'), 0, 0, tiled=True)  22.6 us
    all_to_all x1, blocking collectives, per_device(): sums = lax.all_to_all(sums, ('seq', 'res'), 0, 0, tiled=True)  17.8 us
    all_to_all x1, blocking collectives, per_device(): block = lax.all_to_all(block, 'res', 0, 0, tiled=True)  14 us
    pallas_call x4, Pallas kernels, call(): pl.pallas_call(kernel, out_shape=outs, in_specs=[pl.BlockSpec(memory_spac...  7.48 us

profile of v2, /device:TPU:1, one launch (start us, length us, event | category | flops | bytes accessed | tf_op | source)
XLA Modules:
  0.0 86.6 jit_solution(5962038184839610505)
XLA Ops:
  0.6 0.0 copy-start.4
  0.6 0.0 copy-start.3
  0.7 2.1 %shard_map.101 = bf16[8,32,640]{2,1,0:T(8,128)(2,1)} custom-call(bf16[512,32]{1,0:T(8,128)(2,1)} %bitcast.17, s32[16,32]{1,0:T(8,128)} %mask_hbm.1), custom_call_target="tpu_custom_call" | custom-call | tf_op jit(solution)/shard_map/pallas_call | solution.py:206
  2.8 14.0 %all_to_all.20 = bf16[8,32,640]{2,1,0:T(8,128)(2,1)S(1)} all-to-all(bf16[8,32,640]{2,1,0:T(8,128)(2,1)} %shard_map.101), channel_id=1, replica_groups=mesh['seq'=16,'res'=8] {'res'}, dimensions={0} | all-to-all | bytes 655360 | tf_op jit(solution)/shard_map/all_to_all | solution.py:230
  16.7 0.0 copy-done.4
  16.7 0.0 copy-done.3
  16.7 0.2 reshape.49
  16.9 0.1 pad.4
  17.0 0.1 broadcast_in_dim.4
  17.1 0.1 pad_maximum_fusion
  17.2 0.0 copy-start
  17.2 0.0 copy-start.1
  17.2 0.0 copy-start.2
  17.2 23.7 %all_to_all.21 = bf16[16,16,1664]{2,1,0:T(8,128)(2,1)S(1)} all-to-all(bf16[16,16,1664]{2,1,0:T(8,128)(2,1)S(1)} %pad_maximum_fusion), channel_id=1, replica_groups=mesh['seq'=16,'res'=8] {'seq'}, dimensions={0} | all-to-all | bytes 1703936 | tf_op jit(solution)/shard_map/all_to_all | solution.py:242
  40.9 0.0 copy-done
  40.9 0.0 copy-done.1
  40.9 0.0 copy-done.2
  40.9 3.6 %shard_map.102 = (bf16[512,128]{1,0:T(8,128)(2,1)}, bf16[128,32,128]{2,1,0:T(8,128)(2,1)S(1)}, f32[1,128]{1,0:T(1,128)S(1)}) custom-call(bf16[256,1664]{1,0:T(8,128)(2,1)S(1)} %bitcast.11, bf16[1024,128]{1,0:T(8,128)(2,1)S(1)} %bitcast.12, f32[1,128]{1,0:T(1,128)S(1)} %bitcast.14, bf16[512,128]{1,0:T(8,128)(2,1)S(1)} %bitcast.13), custom_call_target="tpu_custom_call" | custom-call | tf_op jit(solution)/shard_map/pallas_call | solution.py:206
  44.5 22.6 %all_to_all.22.in_ref = bf16[128,32,128]{2,1,0:T(8,128)(2,1)S(1)} all-to-all(bf16[128,32,128]{2,1,0:T(8,128)(2,1)S(1)} %get-tuple-element.19), channel_id=1, replica_groups=mesh['seq'=16,'res'=8] {'seq','res'}, dimensions={0} | all-to-all | bytes 2097152 | tf_op jit(solution)/shard_map/all_to_all | solution.py:261
  67.1 0.3 shard_map.103
  67.4 17.8 %all_to_all.23.in_ref = bf16[128,16,128]{2,1,0:T(8,128)(2,1)S(1)} all-to-all(bf16[128,16,128]{2,1,0:T(8,128)(2,1)S(1)} %shard_map.103), channel_id=1, replica_groups=mesh['seq'=16,'res'=8] {'seq','res'}, dimensions={0} | all-to-all | bytes 1048576 | tf_op jit(solution)/shard_map/all_to_all | solution.py:265
  85.2 1.5 %shard_map.104 = (f32[1024,128]{1,0:T(8,128)}, f32[512,32]{1,0:T(8,128)}, f32[512,32]{1,0:T(8,128)}, f32[1,128]{1,0:T(1,128)}) custom-call(bf16[128,16,128]{2,1,0:T(8,128)(2,1)S(1)} %all_to_all.23.in_ref), custom_call_target="tpu_custom_call" | custom-call | tf_op jit(solution)/shard_map/pallas_call | solution.py:206
  (3 shorter events, 0.0 us)
Async XLA Ops:
  0.6 16.1 %copy-start.4 = (s32[16,32]{1,0:T(8,128)S(1)}, s32[16,32]{1,0:T(8,128)}, u32[]{:S(2)}) copy-start(s32[16,32]{1,0:T(8,128)} %mask_hbm.1) | copy-start | bytes 6148
  0.6 16.1 %copy-start.3 = (bf16[16,32,32]{2,1,0:T(8,128)(2,1)S(1)}, bf16[16,32,32]{2,1,0:T(8,128)(2,1)}, u32[]{:S(2)}) copy-start(bf16[16,32,32]{2,1,0:T(8,128)(2,1)} %param.7) | copy-start | bytes 98308
  17.2 23.7 %copy-start = (bf16[32,32,128]{2,1,0:T(8,128)(2,1)S(1)}, bf16[32,32,128]{2,1,0:T(8,128)(2,1)}, u32[]{:S(2)}) copy-start(bf16[32,32,128]{2,1,0:T(8,128)(2,1)} %param.9) | copy-start | bytes 786436
  17.2 23.7 %copy-start.1 = (bf16[16,32,128]{2,1,0:T(8,128)(2,1)S(1)}, bf16[16,32,128]{2,1,0:T(8,128)(2,1)}, u32[]{:S(2)}) copy-start(bf16[16,32,128]{2,1,0:T(8,128)(2,1)} %param.11) | copy-start | bytes 393220
  17.2 23.7 %copy-start.2 = (f32[128]{0:T(128)S(1)}, f32[128]{0:T(128)}, u32[]{:S(2)}) copy-start(f32[128]{0:T(128)} %param.10) | copy-start | bytes 1540

commit v3 on v2

v3 whole, which is shorter than its diff:
```python
import jax
import jax.numpy as jnp
from jax import lax
from jax.experimental import pallas as pl
from jax.experimental.pallas import tpu as pltpu
from jax.sharding import Mesh
from jax.sharding import PartitionSpec as P

F32 = jnp.float32
BF16 = jnp.bfloat16
ROWS_ROWS = (((0,), (0,)), ((), ()))
LANES_LANES = (((1,), (1,)), ((), ()))


def iota(shape, dim):
    return lax.broadcasted_iota(jnp.int32, shape, dim)


def swap_groups(blocks):
    lane = iota(blocks[0].shape, 1)
    upper = lane >= 64
    odd = (lane // 32) % 2 == 1
    b0, b1, b2, b3 = blocks
    r0, r1, r2, r3 = (pltpu.roll(b, 64, 1) for b in blocks)
    b0, b2 = jnp.where(upper, r2, b0), jnp.where(upper, b2, r0)
    b1, b3 = jnp.where(upper, r3, b1), jnp.where(upper, b3, r1)
    up1, up3 = pltpu.roll(b1, 32, 1), pltpu.roll(b3, 32, 1)
    down0, down2 = pltpu.roll(b0, 96, 1), pltpu.roll(b2, 96, 1)
    return (
        jnp.where(odd, up1, b0),
        jnp.where(odd, b1, down0),
        jnp.where(odd, up3, b2),
        jnp.where(odd, b3, down2),
    )


def choose(condition):
    return condition.astype(F32).astype(BF16)


def channel_lanes():
    lane = iota((32, 512), 1)
    return choose(iota((32, 512), 0) == 4 * ((lane % 128) // 16) + lane // 128)


def own_residue():
    return iota((512, 512), 0) % 16 == iota((512, 512), 1) % 16


def low():
    return iota((8, 128), 1) < 64


def fold(first, second, lower):
    return (
        jnp.where(lower, first, pltpu.roll(second, 64, 1)),
        jnp.where(lower, pltpu.roll(first, 64, 1), second),
    )


def prep_kernel(left_hbm, mask_hbm, out_ref, left_ref, mask_ref, sems):
    copies = [
        pltpu.make_async_copy(left_hbm, left_ref, sems.at[0]),
        pltpu.make_async_copy(mask_hbm, mask_ref, sems.at[1]),
    ]
    for copy in copies:
        copy.start()
    for copy in copies:
        copy.wait()
    spread = jnp.dot(left_ref[...], channel_lanes(), preferred_element_type=F32)
    spread = jnp.where(own_residue(), spread, 0.0).astype(BF16)
    row, col = iota((32, 512), 0), iota((32, 512), 1)
    gather = choose((col // 32 == row % 16) & ((col % 32) // 16 == row // 16))
    block = jnp.dot(gather, spread, preferred_element_type=F32).astype(BF16)
    mask = mask_ref[...].astype(F32).astype(BF16)
    widen = choose(iota((32, 128), 0) == iota((32, 128), 1))
    masks = jnp.dot(mask, widen, preferred_element_type=F32).astype(BF16)
    for r in range(8):
        for h in range(2):
            out_ref[r, :, h * 512 : h * 512 + 512] = block[h * 16 : h * 16 + 16]
        out_ref[r, :, 1024:1152] = masks


def pair_kernel(
    own_ref, other_ref, w_ref, bias_ref, cot_ref,
    pair_ref, send_ref, right_ref, weight_ref, left_ref, bsum_ref,
    y_ref, x_ref, dx_ref, dy_ref, mask_ref, plain_ref, cot32_ref, scaled_ref,
):
    core = lax.axis_index("core")
    keep = pl.multiple_of(core * 512, 512)
    give = pl.multiple_of((1 - core) * 512, 512)

    def rows(lanes):
        return jnp.concatenate([own_ref[:, lanes], other_ref[:, lanes]], 0)

    row, col = iota((256, 256), 0), iota((256, 256), 1)
    device = row % 16
    order = choose(col == ((device + core) % 2) * 128 + (device // 2) * 16 + row // 16)
    masks = jnp.dot(order, rows(slice(2048, 2176)), preferred_element_type=F32).astype(BF16)
    left = jnp.dot(order, rows(pl.ds(keep, 512)), preferred_element_type=F32).astype(BF16)
    right = jnp.dot(order, rows(slice(1024, 2048)), preferred_element_type=F32).astype(BF16)
    lane = iota((128, 512), 1)
    spread_i = choose(iota((128, 512), 0) == core * 16 + lane % 16)
    spread_j = choose(iota((128, 512), 0) == 32 + 4 * ((lane // 16) % 8) + lane // 128)
    spread_jd = choose(iota((128, 1024), 0) == 32 + iota((128, 1024), 1) // 32)
    mask_i = jnp.dot(masks, spread_i, preferred_element_type=F32)
    mask_j = jnp.dot(masks, spread_j, preferred_element_type=F32)
    mask_jd = jnp.dot(masks, spread_jd, preferred_element_type=F32)
    mask_ref[...] = mask_jd
    left = left * mask_i.astype(BF16)
    right = right * mask_jd.astype(BF16)
    both = (mask_i * mask_j).astype(BF16)
    counts = (
        lax.dot_general(both, jnp.ones((256, 128), BF16), ROWS_ROWS, preferred_element_type=F32) + 1e-3
    )
    inverse = 1.0 / counts
    cot32 = cot_ref[...].astype(F32)
    cot32_ref[...] = cot32
    bsum_ref[...] = jnp.sum(cot32, axis=0, keepdims=True)
    for j in range(32):
        at = ((j % 4) * 8 + j // 4) * 16
        scaled_ref[at : at + 16, :] = (
            cot32_ref[pl.ds(j, 16, stride=32), :] * inverse[at : at + 16, :]
        ).astype(BF16)
    scaled = scaled_ref[...]

    y_ref[...] = lax.dot_general(left, right, ROWS_ROWS, preferred_element_type=F32)
    for u in range(8):
        lanes = slice(u * 128, u * 128 + 128)
        for t in range(8):
            tiles = swap_groups([y_ref[f * 128 + t * 16 : f * 128 + t * 16 + 16, lanes] for f in range(4)])
            for e in range(4):
                at = (e * 8 + u) * 16
                x_ref[at : at + 16, t * 128 : t * 128 + 128] = tiles[e].astype(BF16)

    dx_ref[...] = lax.dot_general(scaled, w_ref[...], LANES_LANES, preferred_element_type=F32)
    for u in range(8):
        lanes = slice(u * 128, u * 128 + 128)
        for t in range(8):
            tiles = swap_groups(
                [dx_ref[(e * 8 + u) * 16 : (e * 8 + u) * 16 + 16, t * 128 : t * 128 + 128] for e in range(4)]
            )
            for f in range(4):
                dy_ref[f * 128 + t * 16 : f * 128 + t * 16 + 16, lanes] = tiles[f].astype(BF16)

    def right_part(half):
        part = jnp.dot(left, dy_ref[:, pl.ds(half, 512)], preferred_element_type=F32)
        return part * mask_ref[:, pl.ds(half, 512)]

    def weight_part(half):
        return lax.dot_general(x_ref[:, pl.ds(half, 512)], scaled, ROWS_ROWS, preferred_element_type=F32)

    send_ref[:, 0:512] = right_part(give).astype(BF16)
    part = weight_part(give).astype(BF16)
    send_ref[:, 512:640] = part[0:256]
    send_ref[:, 640:768] = part[256:512]

    right_ref[...] = right_part(keep)
    weight_ref[...] = weight_part(keep)
    left_ref[...] = (
        lax.dot_general(right, dy_ref[...], LANES_LANES, preferred_element_type=F32) * mask_i
    )
    update = jnp.dot(x_ref[...], w_ref[...], preferred_element_type=F32) * inverse + bias_ref[...]
    for j in range(32):
        at = ((j % 4) * 8 + j // 4) * 16
        plain_ref[pl.ds(j, 16, stride=32), :] = update[at : at + 16, :]
    pair_ref[...] = plain_ref[...].astype(BF16)


def pack_kernel(got_ref, right_ref, weight_ref, left_ref, msg_ref):
    lower = low()
    upper_rows = iota((8, 128), 0) >= 4
    for s in range(16):
        for k in range(4):
            m = s * 8 + k * 2
            lanes = slice(k * 128, k * 128 + 128)
            total = right_ref[s * 16 : s * 16 + 16, lanes] + got_ref[s * 16 : s * 16 + 16, lanes].astype(F32)
            tiles = []
            for block in (total, left_ref[s * 16 : s * 16 + 16, lanes]):
                even, odd = fold(block[0:8], block[8:16], lower)
                tiles.append(jnp.where(upper_rows, pltpu.roll(odd, 4, 0), even))
                tiles.append(jnp.where(upper_rows, odd, pltpu.roll(even, 4, 0)))
            at = (m // 2) * 8
            side = slice(512 + (at // 256) * 128, 640 + (at // 256) * 128)
            first = at % 256 // 16 * 16
            got = got_ref[first : first + 16, side].astype(F32)
            tiles.append(weight_ref[at : at + 8, :] + got[at % 16 : at % 16 + 8])
            for n in range(5):
                tile = tiles[n].astype(BF16)
                msg_ref[m, :, n * 128 : n * 128 + 128] = tile[0:4]
                msg_ref[m + 1, :, n * 128 : n * 128 + 128] = tile[4:8]


def reduce_kernel(in_ref, bsum_ref, out_ref, rows_ref):
    lower = iota((4, 128), 1) < 64
    weight = [jnp.zeros((4, 128), F32) for core in range(2)]
    left = [jnp.zeros((4, 256), F32) for q in range(16)]

    def spread(parts, owner, row):
        for b in range(2):
            lanes = slice(b * 128, b * 128 + 128)
            near, far = fold(parts[0][:, lanes], parts[1][:, lanes], lower)
            rows_ref[pl.ds(b * 256 + owner * 8 + row, 4, stride=64), :] = near
            rows_ref[pl.ds(512 + b * 256 + owner * 8 + row, 4, stride=64), :] = far

    for r in range(8):
        right = []
        for core in range(2):
            total = jnp.zeros((4, 256), F32)
            for chip in range(8):
                q = chip * 2 + core
                block = in_ref[q * 8 + r].astype(F32)
                total = total + block[:, 0:256]
                left[q] = left[q] + block[:, 256:512]
                weight[core] = weight[core] + block[:, 512:640]
            right.append(total)
        spread(right, r, 4)
    for chip in range(8):
        spread(left[chip * 2 : chip * 2 + 2], chip, 5)
    bias = bsum_ref[...]
    high = bias.astype(BF16).astype(F32)
    tail = [jnp.zeros((2, 128), F32), high, bias - high]
    base = [jnp.concatenate([weight[core]] + tail, 0) for core in range(2)]
    sub = iota((8, 128), 0)
    mine = (sub == 4) | (sub == 5)
    for m in range(128):
        rows = rows_ref[m * 8 : m * 8 + 8, :]
        out_ref[m] = jnp.where(mine, rows, base[(m // 8) % 2]).astype(BF16)


def operand_kernel(in_ref, right_ref, left_ref, bias_ref, rows_ref):
    lower = iota((16, 128), 1) < 64
    total = jnp.zeros((8, 128), F32)
    for m in range(128):
        block = in_ref[m].astype(F32)
        rows_ref[m * 8 : m * 8 + 8, :] = block
        total = total + block
    bias_ref[...] = total[6:7] + total[7:8]

    def tiles(row):
        pairs = [
            fold(
                rows_ref[pl.ds(k * 16 + row, 16, stride=64), :],
                rows_ref[pl.ds(k * 16 + 8 + row, 16, stride=64), :],
                lower,
            )
            for k in range(4)
        ]
        return [p[0] for p in pairs], [p[1] for p in pairs]

    near, far = tiles(4)
    for k, tile in enumerate(near + far):
        for e in range(4):
            right_ref[pl.ds(k * 4 + e, 16, stride=32), :] = tile[:, e * 32 : e * 32 + 32]
    near, far = tiles(5)
    left = jnp.concatenate([jnp.concatenate(near, 1), jnp.concatenate(far, 1)], 0).astype(BF16)
    row, col = iota((512, 32), 0), iota((512, 32), 1)
    scatter = choose((row // 32 == col % 16) & ((row % 32) // 16 == col // 16))
    spread = jnp.dot(scatter, left, preferred_element_type=F32)
    spread = jnp.where(own_residue(), spread, 0.0).astype(BF16)
    left_ref[...] = lax.dot_general(spread, channel_lanes(), LANES_LANES, preferred_element_type=F32)


def weight_kernel(own_ref, other_ref, out_ref):
    core = lax.axis_index("core")
    upper_rows = iota((8, 128), 0) >= 4
    for p in range(64):
        for ref, half in ((own_ref, core), (other_ref, 1 - core)):
            even, odd = ref[p * 2].astype(F32), ref[p * 2 + 1].astype(F32)
            at = pl.multiple_of(half * 512 + p * 8, 8)
            out_ref[pl.ds(at, 8), :] = jnp.where(upper_rows, pltpu.roll(odd, 4, 0), even)


def call(kernel, outs, scratch, *args, space=pltpu.VMEM, mib=40):
    whole = pl.BlockSpec(memory_space=pltpu.VMEM)
    return pl.pallas_call(
        kernel,
        out_shape=outs,
        in_specs=[pl.BlockSpec(memory_space=space)] * len(args),
        out_specs=tuple([whole] * len(outs)),
        scratch_shapes=scratch,
        compiler_params=pltpu.CompilerParams(vmem_limit_bytes=mib * 1024 * 1024),
    )(*args)


def shape(dims, dtype):
    return jax.ShapeDtypeStruct(dims, dtype)


def per_device(left, right, mask, weight, bias, cotangent):
    swap = [(0, 1), (1, 0)]
    devices = ("chip", "core", "res")
    (block,) = call(
        prep_kernel,
        (shape((8, 16, 1152), BF16),),
        [pltpu.VMEM((512, 32), BF16), pltpu.VMEM((16, 32), jnp.int32), pltpu.SemaphoreType.DMA((2,))],
        left.reshape(512, 32),
        mask,
        space=pltpu.HBM,
        mib=60,
    )
    block = lax.all_to_all(block, "res", 0, 0, tiled=True)
    block, right, mask = lax.optimization_barrier((block, right, mask))
    masks = jnp.pad(mask.astype(BF16), ((0, 0), (32, 64)))
    rights = jnp.broadcast_to(right.reshape(16, 1024), (8, 16, 1024))
    block = jnp.concatenate([block[:, :, :1024], rights, block[:, :, 1024:] + masks], -1)
    own = lax.all_to_all(block, "chip", 0, 0, tiled=True).reshape(128, 2176)
    other = lax.ppermute(own, "core", swap)

    pair_update, send, right_part, weight_part, left_part, bias_part = call(
        pair_kernel,
        (
            shape((512, 128), BF16),
            shape((256, 768), BF16),
            shape((256, 512), F32),
            shape((512, 128), F32),
            shape((256, 512), F32),
            shape((1, 128), F32),
        ),
        [
            pltpu.VMEM((512, 1024), F32),
            pltpu.VMEM((512, 1024), BF16),
            pltpu.VMEM((512, 1024), F32),
            pltpu.VMEM((512, 1024), BF16),
            pltpu.VMEM((256, 1024), F32),
            pltpu.VMEM((512, 128), F32),
            pltpu.VMEM((512, 128), F32),
            pltpu.VMEM((512, 128), BF16),
        ],
        own,
        other,
        weight.reshape(1024, 128),
        bias.reshape(1, 128),
        cotangent.reshape(512, 128),
    )
    got = lax.ppermute(send, "core", swap)
    (parts,) = call(
        pack_kernel,
        (shape((128, 4, 640), BF16),),
        [],
        got,
        right_part,
        weight_part,
        left_part,
    )
    parts = lax.all_to_all(parts, devices, 0, 0, tiled=True)
    (sums,) = call(
        reduce_kernel, (shape((128, 8, 128), BF16),), [pltpu.VMEM((1024, 128), F32)], parts, bias_part
    )
    sums = lax.all_to_all(sums, devices, 0, 0, tiled=True)
    other_sums = lax.ppermute(sums, "core", swap)
    right_grad, left_grad, bias_grad = call(
        operand_kernel,
        (shape((512, 32), F32), shape((512, 32), F32), shape((1, 128), F32)),
        [pltpu.VMEM((1024, 128), F32)],
        sums,
    )
    (weight_grad,) = call(weight_kernel, (shape((1024, 128), F32),), [], sums, other_sums)
    return (
        pair_update.reshape(16, 32, 128),
        left_grad.reshape(16, 32, 32),
        right_grad.reshape(16, 32, 32),
        weight_grad.reshape(32, 32, 128),
        bias_grad.reshape(128),
    )


def solution(mesh):
    mesh = Mesh(mesh.devices.reshape(8, 2, 8), ("chip", "core", "res"))
    seq = ("chip", "core")
    return jax.shard_map(
        per_device,
        mesh=mesh,
        in_specs=(
            P(seq, "res", None),
            P(seq, "res", None),
            P(seq, "res"),
            P(),
            P(),
            P(seq, "res", None),
        ),
        out_specs=(P(seq, "res", None), P(seq, "res", None), P(seq, "res", None), P(), P()),
        check_vma=False,
    )
```

time: 86.9 us -> 81.6 us (0.939)
  blocking collectives: 78 us -> 62.7 us
  starting transfers between devices: 0 us -> 5.04 us
  waiting for transfers between devices: 0 us -> 2.94 us
  Pallas kernels: 7.48 us -> 9.47 us
    all_to_all x3, blocking collectives: 64 us -> 49.2 us  [the longest x1 18.3 us: per_device(): parts = lax.all_to_all(parts, devices, 0, 0, tiled=True)]
    ppermute x0 -> x3, starting transfers between devices: none -> 5.04 us  [the longest x1 3.66 us: per_device(): other = lax.ppermute(own, 'core', swap)]
    ppermute x0 -> x3, waiting for transfers between devices: none -> 2.94 us  [the longest x1 1.58 us: per_device(): other = lax.ppermute(own, 'core', swap)]
    pallas_call x4 -> x6, Pallas kernels: 7.48 us -> 9.47 us  [call(): pl.pallas_call(kernel, out_shape=outs, in_specs=[pl.BlockSpec(memory_spac...]
  transfers between devices with their start and end apart: 0 -> 3, of which waited for: 0 -> 2; matrix products, arithmetic and copies ran while one was open for 0% -> 0% of each run, Pallas kernels for 0% -> 2%
where the time goes in v3:
time: 81.6 us; the launch traced here: 81.3 us
  blocking collectives  62.7 us (77%)
  Pallas kernels  9.47 us (12%)
  starting transfers between devices  5.04 us (6%)
  waiting for transfers between devices  2.94 us (4%)
    all_to_all x1, blocking collectives, per_device(): parts = lax.all_to_all(parts, devices, 0, 0, tiled=True)  18.3 us
    all_to_all x1, blocking collectives, per_device(): own = lax.all_to_all(block, 'chip', 0, 0, tiled=True).reshape(128, 2176)  15.7 us
    all_to_all x1, blocking collectives, per_device(): sums = lax.all_to_all(sums, devices, 0, 0, tiled=True)  15.2 us
    all_to_all x1, blocking collectives, per_device(): block = lax.all_to_all(block, 'res', 0, 0, tiled=True)  13.6 us
    pallas_call x6, Pallas kernels, call(): pl.pallas_call(kernel, out_shape=outs, in_specs=[pl.BlockSpec(memory_spac...  9.47 us
    ppermute x1, starting transfers between devices, per_device(): other = lax.ppermute(own, 'core', swap)  3.66 us
  transfers between devices with their start and end apart: 3, of which 2 were waited for; matrix products, arithmetic and copies ran while one was open for 0% of the time, Pallas kernels for 2%

profile of v3, /device:TPU:1, one launch (start us, length us, event | category | flops | bytes accessed | tf_op | source)
XLA Modules:
  0.0 81.3 jit_solution(15600828479097101218)
XLA Ops:
  0.6 0.0 copy-start.4
  0.6 2.1 %shard_map.101 = bf16[8,16,1152]{2,1,0:T(8,128)(2,1)} custom-call(bf16[512,32]{1,0:T(8,128)(2,1)} %bitcast.16, s32[16,32]{1,0:T(8,128)} %mask_hbm.1), custom_call_target="tpu_custom_call" | custom-call | tf_op jit(solution)/shard_map/pallas_call | solution.py:276
  2.7 0.0 copy-start.3
  2.7 13.6 %all_to_all.20 = bf16[8,16,1152]{2,1,0:T(8,128)(2,1)S(1)} all-to-all(bf16[8,16,1152]{2,1,0:T(8,128)(2,1)} %shard_map.101), channel_id=1, replica_groups=mesh['chip'=8,'core'=2,'res'=8] {'res'}, dimensions={0} | all-to-all | bytes 589824 | tf_op jit(solution)/shard_map/all_to_all | solution.py:302
  16.3 0.0 copy-done.4
  16.3 0.1 pad.4
  16.4 0.0 copy-done.3
  16.4 0.2 reshape.45
  16.7 0.0 copy-start
  16.7 0.0 copy-start.1
  16.7 0.0 copy-start.2
  16.7 15.7 %all_to_all.21 = bf16[8,16,2176]{2,1,0:T(8,128)(2,1)S(1)} all-to-all(bf16[8,16,2176]{2,1,0:T(8,128)(2,1)S(1)} %pad_maximum_fusion), channel_id=1, replica_groups=mesh['chip'=8,'core'=2,'res'=8] {'chip'}, dimensions={0} | all-to-all | bytes 1114112 | tf_op jit(solution)/shard_map/all_to_all | solution.py:307
  32.4 3.7 %collective-permute-start = (bf16[128,2176]{1,0:T(8,128)(2,1)S(1)}, bf16[128,2176]{1,0:T(8,128)(2,1)S(1)}, u32[]{:S(2)}, u32[]{:S(2)}) collective-permute-start(bf16[128,2176]{1,0:T(8,128)(2,1)S(1)} %bitcast.10), channel_id=1, source_target_pairs={{0,8},{8,0},{1,9},{9,1},{2,10},{10,2},{3,11},{11,3},{4,12},{12,4},... | collective-permute-start | bytes 1671176 | tf_op jit(solution)/shard_map/ppermute | solution.py:308
  36.0 1.6 %collective-permute-done.other_ref = bf16[128,2176]{1,0:T(8,128)(2,1)S(1)} collective-permute-done((bf16[128,2176]{1,0:T(8,128)(2,1)S(1)}, bf16[128,2176]{1,0:T(8,128)(2,1)S(1)}, u32[]{:S(2)}, u32[]{:S(2)}) %collective-permute-start) | collective-permute-done | bytes 557088 | tf_op jit(solution)/shard_map/ppermute | solution.py:308
  37.6 0.0 copy-done
  37.6 0.0 copy-done.1
  37.6 0.0 copy-done.2
  37.6 4.5 %shard_map.102 = (bf16[512,128]{1,0:T(8,128)(2,1)}, bf16[256,768]{1,0:T(8,128)(2,1)S(1)}, f32[256,512]{1,0:T(8,128)S(1)}, f32[512,128]{1,0:T(8,128)S(1)}, f32[256,512]{1,0:T(8,128)S(1)}, /*index=5*/f32[1,128]{1,0:T(1,128)S(1)}) custom-call(bf16[128,2176]{1,0:T(8,128)(2,1)S(1)} %bitcast.11, bf16[128,2176]{1,0:T(8,128)(2,1)S(1)} %collective-permute-done.other_ref, ...), custom_call_target="tpu_custom_call" | custom-call | tf_op jit(solution)/shard_map/pallas_call | solution.py:276
  42.1 0.4 collective-permute-start.1
  42.5 1.3 %collective-permute-done.1.got_ref = bf16[256,768]{1,0:T(8,128)(2,1)S(1)} collective-permute-done((bf16[256,768]{1,0:T(8,128)(2,1)S(1)}, bf16[256,768]{1,0:T(8,128)(2,1)S(1)}, u32[]{:S(2)}, u32[]{:S(2)}) %collective-permute-start.1) | collective-permute-done | bytes 393248 | tf_op jit(solution)/shard_map/ppermute | solution.py:336
  43.9 0.4 shard_map.103
  44.3 18.3 %all_to_all.22.in_ref = bf16[128,4,640]{2,1,0:T(4,128)(2,1)S(1)} all-to-all(bf16[128,4,640]{2,1,0:T(4,128)(2,1)S(1)} %shard_map.103), channel_id=1, replica_groups=mesh['chip'=8,'core'=2,'res'=8] {'chip','core','res'}, dimensions={0} | all-to-all | bytes 1310720 | tf_op jit(solution)/shard_map/all_to_all | solution.py:346
  62.5 0.2 shard_map.104
  62.8 15.2 %all_to_all.23.in_ref.own_ref = bf16[128,8,128]{2,1,0:T(8,128)(2,1)S(1)} all-to-all(bf16[128,8,128]{2,1,0:T(8,128)(2,1)S(1)} %shard_map.104), channel_id=1, replica_groups=mesh['chip'=8,'core'=2,'res'=8] {'chip','core','res'}, dimensions={0} | all-to-all | bytes 524288 | tf_op jit(solution)/shard_map/all_to_all | solution.py:350
  78.0 1.0 %collective-permute-start.2 = (bf16[128,8,128]{2,1,0:T(8,128)(2,1)S(1)}, bf16[128,8,128]{2,1,0:T(8,128)(2,1)S(1)}, u32[]{:S(2)}, u32[]{:S(2)}) collective-permute-start(bf16[128,8,128]{2,1,0:T(8,128)(2,1)S(1)} %all_to_all.23.in_ref.own_ref), channel_id=1, source_target_pairs={{0,8},{8,0},{1,9},{9,1},{2,10},{10,2},{3,11},{11,3},{4,12},{12,4},... | collective-permute-start | bytes 786440 | tf_op jit(solution)/shard_map/ppermute | solution.py:351
  79.0 1.4 %shard_map.105 = (f32[512,32]{1,0:T(8,128)}, f32[512,32]{1,0:T(8,128)}, f32[1,128]{1,0:T(1,128)}) custom-call(bf16[128,8,128]{2,1,0:T(8,128)(2,1)S(1)} %all_to_all.23.in_ref.own_ref), custom_call_target="tpu_custom_call" | custom-call | tf_op jit(solution)/shard_map/pallas_call | solution.py:276
  80.4 0.0 collective-permute-done.2.other_ref
  80.4 0.9 %shard_map.106 = f32[1024,128]{1,0:T(8,128)} custom-call(bf16[128,8,128]{2,1,0:T(8,128)(2,1)S(1)} %all_to_all.23.in_ref.own_ref, bf16[128,8,128]{2,1,0:T(8,128)(2,1)S(1)} %collective-permute-done.2.other_ref), custom_call_target="tpu_custom_call" | custom-call | tf_op jit(solution)/shard_map/pallas_call | solution.py:276
  (5 shorter events, 0.1 us)
Async XLA Ops:
  0.6 15.6 %copy-start.4 = (s32[16,32]{1,0:T(8,128)S(1)}, s32[16,32]{1,0:T(8,128)}, u32[]{:S(2)}) copy-start(s32[16,32]{1,0:T(8,128)} %mask_hbm.1) | copy-start | bytes 6148
  2.7 13.7 %copy-start.3 = (bf16[16,32,32]{2,1,0:T(8,128)(2,1)S(1)}, bf16[16,32,32]{2,1,0:T(8,128)(2,1)}, u32[]{:S(2)}) copy-start(bf16[16,32,32]{2,1,0:T(8,128)(2,1)} %param.7) | copy-start | bytes 98308
  16.7 21.0 %copy-start = (bf16[32,32,128]{2,1,0:T(8,128)(2,1)S(1)}, bf16[32,32,128]{2,1,0:T(8,128)(2,1)}, u32[]{:S(2)}) copy-start(bf16[32,32,128]{2,1,0:T(8,128)(2,1)} %param.9) | copy-start | bytes 786436
  16.7 21.0 %copy-start.1 = (bf16[16,32,128]{2,1,0:T(8,128)(2,1)S(1)}, bf16[16,32,128]{2,1,0:T(8,128)(2,1)}, u32[]{:S(2)}) copy-start(bf16[16,32,128]{2,1,0:T(8,128)(2,1)} %param.11) | copy-start | bytes 393220
  16.7 20.9 %copy-start.2 = (f32[128]{0:T(128)S(1)}, f32[128]{0:T(128)}, u32[]{:S(2)}) copy-start(f32[128]{0:T(128)} %param.10) | copy-start | bytes 1540
  32.4 5.2 %collective-permute-start = (bf16[128,2176]{1,0:T(8,128)(2,1)S(1)}, bf16[128,2176]{1,0:T(8,128)(2,1)S(1)}, u32[]{:S(2)}, u32[]{:S(2)}) collective-permute-start(bf16[128,2176]{1,0:T(8,128)(2,1)S(1)} %bitcast.10), channel_id=1, source_target_pairs={{0,8},{8,0},{1,9},{9,1},{2,10},{10,2},{3,11},{11,3},{4,12},{12,4},... | collective-permute-start | bytes 1671176 | tf_op jit(solution)/shard_map/ppermute | solution.py:308
  42.1 1.8 %collective-permute-start.1 = (bf16[256,768]{1,0:T(8,128)(2,1)S(1)}, bf16[256,768]{1,0:T(8,128)(2,1)S(1)}, u32[]{:S(2)}, u32[]{:S(2)}) collective-permute-start(bf16[256,768]{1,0:T(8,128)(2,1)S(1)} %get-tuple-element.21), channel_id=1, source_target_pairs={{0,8},{8,0},{1,9},{9,1},{2,10},{10,2},{3,11},{11,3},{4,12},{12,4},... | collective-permute-start | bytes 1179656 | tf_op jit(solution)/shard_map/ppermute | solution.py:336
  78.0 2.4 %collective-permute-start.2 = (bf16[128,8,128]{2,1,0:T(8,128)(2,1)S(1)}, bf16[128,8,128]{2,1,0:T(8,128)(2,1)S(1)}, u32[]{:S(2)}, u32[]{:S(2)}) collective-permute-start(bf16[128,8,128]{2,1,0:T(8,128)(2,1)S(1)} %all_to_all.23.in_ref.own_ref), channel_id=1, source_target_pairs={{0,8},{8,0},{1,9},{9,1},{2,10},{10,2},{3,11},{11,3},{4,12},{12,4},... | collective-permute-start | bytes 786440 | tf_op jit(solution)/shard_map/ppermute | solution.py:351

commit v4 on v3

--- a/solution.py
+++ b/solution.py
@@ -58,10 +58,13 @@
     )
 
 
-def prep_kernel(left_hbm, mask_hbm, out_ref, left_ref, mask_ref, sems):
+def prep_kernel(
+    left_hbm, right_hbm, mask_hbm, left_out, right_out, left_ref, right_ref, mask_ref, right32_ref, sems
+):
     copies = [
         pltpu.make_async_copy(left_hbm, left_ref, sems.at[0]),
-        pltpu.make_async_copy(mask_hbm, mask_ref, sems.at[1]),
+        pltpu.make_async_copy(right_hbm, right_ref, sems.at[1]),
+        pltpu.make_async_copy(mask_hbm, mask_ref, sems.at[2]),
     ]
     for copy in copies:
         copy.start()
@@ -73,18 +76,23 @@
     gather = choose((col // 32 == row % 16) & ((col % 32) // 16 == row // 16))
     block = jnp.dot(gather, spread, preferred_element_type=F32).astype(BF16)
     mask = mask_ref[...].astype(F32).astype(BF16)
-    widen = choose(iota((32, 128), 0) == iota((32, 128), 1))
-    masks = jnp.dot(mask, widen, preferred_element_type=F32).astype(BF16)
+    row, col = iota((32, 128), 0), iota((32, 128), 1)
+    masks = jnp.dot(mask, choose(row == col), preferred_element_type=F32).astype(BF16)
     for r in range(8):
         for h in range(2):
-            out_ref[r, :, h * 512 : h * 512 + 512] = block[h * 16 : h * 16 + 16]
-        out_ref[r, :, 1024:1152] = masks
-
-
-def pair_kernel(
-    own_ref, other_ref, w_ref, bias_ref, cot_ref,
-    pair_ref, send_ref, right_ref, weight_ref, left_ref, bsum_ref,
-    y_ref, x_ref, dx_ref, dy_ref, mask_ref, plain_ref, cot32_ref, scaled_ref,
+            left_out[r, :, h * 512 : h * 512 + 512] = block[h * 16 : h * 16 + 16]
+        left_out[r, :, 1024:1152] = masks
+    right32_ref[...] = right_ref[...].astype(F32)
+    for k in range(8):
+        tile = [right32_ref[pl.ds(k * 4 + e, 16, stride=32), :] for e in range(4)]
+        right_out[:, k * 128 : k * 128 + 128] = jnp.concatenate(tile, 1).astype(BF16)
+    right_out[:, 1024:1152] = jnp.dot(mask, choose(row + 32 == col), preferred_element_type=F32).astype(BF16)
+
+
+def outer_kernel(
+    own_ref, other_ref, w_ref, cot_ref,
+    send_ref, x_ref, dy_ref, left_ref, right_ref, mask_i_ref, mask_jd_ref, scaled_ref, inverse_ref, bsum_ref,
+    y_ref, dx_ref, cot32_ref,
 ):
     core = lax.axis_index("core")
     keep = pl.multiple_of(core * 512, 512)
@@ -106,14 +114,18 @@
     mask_i = jnp.dot(masks, spread_i, preferred_element_type=F32)
     mask_j = jnp.dot(masks, spread_j, preferred_element_type=F32)
     mask_jd = jnp.dot(masks, spread_jd, preferred_element_type=F32)
-    mask_ref[...] = mask_jd
-    left = left * mask_i.astype(BF16)
-    right = right * mask_jd.astype(BF16)
+    mask_i_ref[...] = mask_i.astype(BF16)
+    mask_jd_ref[...] = mask_jd.astype(BF16)
+    left = left * mask_i_ref[...]
+    right = right * mask_jd_ref[...]
+    left_ref[...] = left
+    right_ref[...] = right
     both = (mask_i * mask_j).astype(BF16)
     counts = (
         lax.dot_general(both, jnp.ones((256, 128), BF16), ROWS_ROWS, preferred_element_type=F32) + 1e-3
     )
     inverse = 1.0 / counts
+    inverse_ref[...] = inverse
     cot32 = cot_ref[...].astype(F32)
     cot32_ref[...] = cot32
     bsum_ref[...] = jnp.sum(cot32, axis=0, keepdims=True)
@@ -143,28 +155,34 @@
             for f in range(4):
                 dy_ref[f * 128 + t * 16 : f * 128 + t * 16 + 16, lanes] = tiles[f].astype(BF16)
 
-    def right_part(half):
-        part = jnp.dot(left, dy_ref[:, pl.ds(half, 512)], preferred_element_type=F32)
-        return part * mask_ref[:, pl.ds(half, 512)]
-
-    def weight_part(half):
-        return lax.dot_general(x_ref[:, pl.ds(half, 512)], scaled, ROWS_ROWS, preferred_element_type=F32)
-
-    send_ref[:, 0:512] = right_part(give).astype(BF16)
-    part = weight_part(give).astype(BF16)
+    part = right_part(give, left, dy_ref, mask_jd_ref).astype(BF16)
+    send_ref[:, 0:512] = part
+    part = weight_part(give, x_ref, scaled).astype(BF16)
     send_ref[:, 512:640] = part[0:256]
     send_ref[:, 640:768] = part[256:512]
 
-    right_ref[...] = right_part(keep)
-    weight_ref[...] = weight_part(keep)
-    left_ref[...] = (
-        lax.dot_general(right, dy_ref[...], LANES_LANES, preferred_element_type=F32) * mask_i
-    )
-    update = jnp.dot(x_ref[...], w_ref[...], preferred_element_type=F32) * inverse + bias_ref[...]
-    for j in range(32):
-        at = ((j % 4) * 8 + j // 4) * 16
-        plain_ref[pl.ds(j, 16, stride=32), :] = update[at : at + 16, :]
-    pair_ref[...] = plain_ref[...].astype(BF16)
+
+def right_part(half, left, dy_ref, mask_ref):
+    part = jnp.dot(left, dy_ref[:, pl.ds(half, 512)], preferred_element_type=F32)
+    return part * mask_ref[:, pl.ds(half, 512)].astype(F32)
+
+
+def weight_part(half, x_ref, scaled):
+    return lax.dot_general(x_ref[:, pl.ds(half, 512)], scaled, ROWS_ROWS, preferred_element_type=F32)
+
+
+def sums_kernel(
+    x_ref, dy_ref, left_in, right_in, mask_i_ref, mask_jd_ref, scaled_ref, inverse_ref, w_ref, bias_ref,
+    update_ref, right_ref, weight_ref, left_ref,
+):
+    keep = pl.multiple_of(lax.axis_index("core") * 512, 512)
+    right_ref[...] = right_part(keep, left_in[...], dy_ref, mask_jd_ref)
+    weight_ref[...] = weight_part(keep, x_ref, scaled_ref[...])
+    left = lax.dot_general(right_in[...], dy_ref[...], LANES_LANES, preferred_element_type=F32)
+    left_ref[...] = left * mask_i_ref[...].astype(F32)
+    update_ref[...] = (
+        jnp.dot(x_ref[...], w_ref[...], preferred_element_type=F32) * inverse_ref[...] + bias_ref[...]
+    )
 
 
 def pack_kernel(got_ref, right_ref, weight_ref, left_ref, msg_ref):
@@ -228,7 +246,20 @@
         out_ref[m] = jnp.where(mine, rows, base[(m // 8) % 2]).astype(BF16)
 
 
-def operand_kernel(in_ref, right_ref, left_ref, bias_ref, rows_ref):
+def weight_rows(ref, out_ref):
+    upper_rows = iota((8, 128), 0) >= 4
+    for p in range(64):
+        even, odd = ref[p * 2].astype(F32), ref[p * 2 + 1].astype(F32)
+        out_ref[p * 8 : p * 8 + 8, :] = jnp.where(upper_rows, pltpu.roll(odd, 4, 0), even)
+
+
+def operand_kernel(
+    in_ref, update_ref, pair_ref, right_ref, left_ref, bias_ref, rows_ref, plain_ref
+):
+    for j in range(32):
+        at = ((j % 4) * 8 + j // 4) * 16
+        plain_ref[pl.ds(j, 16, stride=32), :] = update_ref[at : at + 16, :]
+    pair_ref[...] = plain_ref[...].astype(BF16)
     lower = iota((16, 128), 1) < 64
     total = jnp.zeros((8, 128), F32)
     for m in range(128):
@@ -261,23 +292,24 @@
     left_ref[...] = lax.dot_general(spread, channel_lanes(), LANES_LANES, preferred_element_type=F32)
 
 
-def weight_kernel(own_ref, other_ref, out_ref):
+def weight_kernel(own_ref, other_ref, out_hbm, rows_ref, sems):
     core = lax.axis_index("core")
-    upper_rows = iota((8, 128), 0) >= 4
-    for p in range(64):
-        for ref, half in ((own_ref, core), (other_ref, 1 - core)):
-            even, odd = ref[p * 2].astype(F32), ref[p * 2 + 1].astype(F32)
-            at = pl.multiple_of(half * 512 + p * 8, 8)
-            out_ref[pl.ds(at, 8), :] = jnp.where(upper_rows, pltpu.roll(odd, 4, 0), even)
-
-
-def call(kernel, outs, scratch, *args, space=pltpu.VMEM, mib=40):
-    whole = pl.BlockSpec(memory_space=pltpu.VMEM)
+    copies = []
+    for n, (ref, half) in enumerate(((own_ref, core), (other_ref, 1 - core))):
+        weight_rows(ref, rows_ref.at[n])
+        at = pl.ds(pl.multiple_of(half * 512, 512), 512)
+        copies.append(pltpu.make_async_copy(rows_ref.at[n], out_hbm.at[at], sems.at[n]))
+        copies[n].start()
+    for copy in copies:
+        copy.wait()
+
+
+def call(kernel, outs, scratch, *args, space=pltpu.VMEM, mib=40, out_space=pltpu.VMEM):
     return pl.pallas_call(
         kernel,
         out_shape=outs,
         in_specs=[pl.BlockSpec(memory_space=space)] * len(args),
-        out_specs=tuple([whole] * len(outs)),
+        out_specs=tuple([pl.BlockSpec(memory_space=out_space)] * len(outs)),
         scratch_shapes=scratch,
         compiler_params=pltpu.CompilerParams(vmem_limit_bytes=mib * 1024 * 1024),
     )(*args)
@@ -290,58 +322,75 @@
 def per_device(left, right, mask, weight, bias, cotangent):
     swap = [(0, 1), (1, 0)]
     devices = ("chip", "core", "res")
-    (block,) = call(
+    block, rights = call(
         prep_kernel,
-        (shape((8, 16, 1152), BF16),),
-        [pltpu.VMEM((512, 32), BF16), pltpu.VMEM((16, 32), jnp.int32), pltpu.SemaphoreType.DMA((2,))],
+        (shape((8, 16, 1152), BF16), shape((16, 1152), BF16)),
+        [
+            pltpu.VMEM((512, 32), BF16),
+            pltpu.VMEM((512, 32), BF16),
+            pltpu.VMEM((16, 32), jnp.int32),
+            pltpu.VMEM((512, 32), F32),
+            pltpu.SemaphoreType.DMA((3,)),
+        ],
         left.reshape(512, 32),
+        right.reshape(512, 32),
         mask,
         space=pltpu.HBM,
         mib=60,
     )
     block = lax.all_to_all(block, "res", 0, 0, tiled=True)
-    block, right, mask = lax.optimization_barrier((block, right, mask))
-    masks = jnp.pad(mask.astype(BF16), ((0, 0), (32, 64)))
-    rights = jnp.broadcast_to(right.reshape(16, 1024), (8, 16, 1024))
-    block = jnp.concatenate([block[:, :, :1024], rights, block[:, :, 1024:] + masks], -1)
+    rights = jnp.broadcast_to(rights, (8, 16, 1152))
+    block = jnp.concatenate(
+        [block[..., :1024], rights[..., :1024], block[..., 1024:] + rights[..., 1024:]], -1
+    )
     own = lax.all_to_all(block, "chip", 0, 0, tiled=True).reshape(128, 2176)
     other = lax.ppermute(own, "core", swap)
 
-    pair_update, send, right_part, weight_part, left_part, bias_part = call(
-        pair_kernel,
+    weight = weight.reshape(1024, 128)
+    send, outer, outer_grad, left_all, right_all, mask_i, mask_jd, scaled, inverse, bias_part = call(
+        outer_kernel,
         (
+            shape((256, 768), BF16),
+            shape((512, 1024), BF16),
+            shape((512, 1024), BF16),
+            shape((256, 512), BF16),
+            shape((256, 1024), BF16),
+            shape((256, 512), BF16),
+            shape((256, 1024), BF16),
             shape((512, 128), BF16),
-            shape((256, 768), BF16),
-            shape((256, 512), F32),
             shape((512, 128), F32),
-            shape((256, 512), F32),
             shape((1, 128), F32),
         ),
-        [
-            pltpu.VMEM((512, 1024), F32),
-            pltpu.VMEM((512, 1024), BF16),
-            pltpu.VMEM((512, 1024), F32),
-            pltpu.VMEM((512, 1024), BF16),
-            pltpu.VMEM((256, 1024), F32),
-            pltpu.VMEM((512, 128), F32),
-            pltpu.VMEM((512, 128), F32),
-            pltpu.VMEM((512, 128), BF16),
-        ],
+        [pltpu.VMEM((512, 1024), F32), pltpu.VMEM((512, 1024), F32), pltpu.VMEM((512, 128), F32)],
         own,
         other,
-        weight.reshape(1024, 128),
+        weight,
+        cotangent.reshape(512, 128),
+    )
+    got = lax.ppermute(send, "core", swap)
+    update, right_sum, weight_sum, left_sum = call(
+        sums_kernel,
+        (shape((512, 128), F32), shape((256, 512), F32), shape((512, 128), F32), shape((256, 512), F32)),
+        [],
+        outer,
+        outer_grad,
+        left_all,
+        right_all,
+        mask_i,
+        mask_jd,
+        scaled,
+        inverse,
+        weight,
         bias.reshape(1, 128),
-        cotangent.reshape(512, 128),
-    )
-    got = lax.ppermute(send, "core", swap)
+    )
     (parts,) = call(
         pack_kernel,
         (shape((128, 4, 640), BF16),),
         [],
         got,
-        right_part,
-        weight_part,
-        left_part,
+        right_sum,
+        weight_sum,
+        left_sum,
     )
     parts = lax.all_to_all(parts, devices, 0, 0, tiled=True)
     (sums,) = call(
@@ -349,13 +398,21 @@
     )
     sums = lax.all_to_all(sums, devices, 0, 0, tiled=True)
     other_sums = lax.ppermute(sums, "core", swap)
-    right_grad, left_grad, bias_grad = call(
+    pair_update, right_grad, left_grad, bias_grad = call(
         operand_kernel,
-        (shape((512, 32), F32), shape((512, 32), F32), shape((1, 128), F32)),
-        [pltpu.VMEM((1024, 128), F32)],
+        (shape((512, 128), BF16), shape((512, 32), F32), shape((512, 32), F32), shape((1, 128), F32)),
+        [pltpu.VMEM((1024, 128), F32), pltpu.VMEM((512, 128), F32)],
         sums,
-    )
-    (weight_grad,) = call(weight_kernel, (shape((1024, 128), F32),), [], sums, other_sums)
+        update,
+    )
+    (weight_grad,) = call(
+        weight_kernel,
+        (shape((1024, 128), F32),),
+        [pltpu.VMEM((2, 512, 128), F32), pltpu.SemaphoreType.DMA((2,))],
+        sums,
+        other_sums,
+        out_space=pltpu.HBM,
+    )
     return (
         pair_update.reshape(16, 32, 128),
         left_grad.reshape(16, 32, 32),

time: 81.6 us -> 80 us (0.980)
  blocking collectives: 62.7 us -> 49.2 us
  starting transfers between devices: 5.04 us -> 12 us
  waiting for transfers between devices: 2.94 us -> 6.91 us
  local copies, waits for them, and re-layouts: 0.32 us -> 1.5 us
    all_to_all x1 -> x0, blocking collectives: 13.6 us -> none  [per_device(): block = lax.all_to_all(block, 'res', 0, 0, tiled=True)]
    all_to_all x0 -> x1, starting transfers between devices: none -> 6.89 us  [per_device(): block = lax.all_to_all(block, 'res', 0, 0, tiled=True)]
    all_to_all x0 -> x1, waiting for transfers between devices: none -> 4.97 us  [per_device(): block = lax.all_to_all(block, 'res', 0, 0, tiled=True)]
    slice x1 -> x3, local copies, waits for them, and re-layouts: 0.02 us -> 1.47 us  [the longest x1 0.76 us: per_device(): rights[..., :1024]]
    ppermute x1, waiting for transfers between devices: 1.35 us -> 0.35 us  [per_device(): got = lax.ppermute(send, 'core', swap)]
    pallas_call x6 -> x7, Pallas kernels: 9.47 us -> 9.26 us  [call(): pl.pallas_call(kernel, out_shape=outs, in_specs=[pl.BlockSpec(memory_spac...]
  transfers between devices with their start and end apart: 3 -> 4, of which waited for: 2 -> 3; matrix products, arithmetic and copies ran while one was open for 0% -> 2% of each run, Pallas kernels for 2% -> 3%
where the time goes in v4:
time: 80 us; the launch traced here: 79.6 us
  blocking collectives  49.2 us (62%)
  starting transfers between devices  12 us (15%)
  Pallas kernels  9.26 us (12%)
  waiting for transfers between devices  6.91 us (9%)
  local copies, waits for them, and re-layouts  1.5 us (2%)
    all_to_all x1, blocking collectives, per_device(): parts = lax.all_to_all(parts, devices, 0, 0, tiled=True)  18.2 us
    all_to_all x1, blocking collectives, per_device(): own = lax.all_to_all(block, 'chip', 0, 0, tiled=True).reshape(128, 2176)  15.7 us
    all_to_all x1, blocking collectives, per_device(): sums = lax.all_to_all(sums, devices, 0, 0, tiled=True)  15.2 us
    pallas_call x7, Pallas kernels, call(): pl.pallas_call(kernel, out_shape=outs, in_specs=[pl.BlockSpec(memory_spac...  9.26 us
    all_to_all x1, starting transfers between devices, per_device(): block = lax.all_to_all(block, 'res', 0, 0, tiled=True)  6.89 us
    all_to_all x1, waiting for transfers between devices, per_device(): block = lax.all_to_all(block, 'res', 0, 0, tiled=True)  4.97 us
    ppermute x1, starting transfers between devices, per_device(): other = lax.ppermute(own, 'core', swap)  3.65 us
  transfers between devices with their start and end apart: 4, of which 3 were waited for; matrix products, arithmetic and copies ran while one was open for 2% of the time, Pallas kernels for 3%

profile of v4, /device:TPU:1, one launch (start us, length us, event | category | flops | bytes accessed | tf_op | source)
XLA Modules:
  0.0 79.6 jit_solution(13035428254904329335)
XLA Ops:
  0.6 2.2 %shard_map.101 = (bf16[8,16,1152]{2,1,0:T(8,128)(2,1)}, bf16[16,1152]{1,0:T(8,128)(2,1)}) custom-call(bf16[512,32]{1,0:T(8,128)(2,1)} %bitcast.18, bf16[512,32]{1,0:T(8,128)(2,1)} %bitcast.19, s32[16,32]{1,0:T(8,128)} %mask_hbm.1), custom_call_target="tpu_custom_call" | custom-call | tf_op jit(solution)/shard_map/pallas_call | solution.py:308
  2.8 6.9 %all-to-all-start = ((bf16[8,16,1152]{2,1,0:T(8,128)(2,1)}), bf16[8,16,1152]{2,1,0:T(8,128)(2,1)S(1)}, u32[]{:S(2)}, u32[]{:S(2)}) async-start(bf16[8,16,1152]{2,1,0:T(8,128)(2,1)} %get-tuple-element.25), calls=%async_computation | async-start | bytes 589824 | tf_op jit(solution)/shard_map/all_to_all | solution.py:341
  9.7 0.7 slice.17
  10.4 0.8 slice.15
  11.1 5.0 %all-to-all-done = bf16[8,16,1152]{2,1,0:T(8,128)(2,1)S(1)} async-done(((bf16[8,16,1152]{2,1,0:T(8,128)(2,1)}), bf16[8,16,1152]{2,1,0:T(8,128)(2,1)S(1)}, u32[]{:S(2)}, u32[]{:S(2)}) %all-to-all-start) | async-done | bytes 294944 | tf_op jit(solution)/shard_map/all_to_all | solution.py:341
  16.2 0.0 copy-start
  16.2 0.0 copy-start.1
  16.2 0.0 copy-start.2
  16.3 15.7 %all_to_all.20 = bf16[8,16,2176]{2,1,0:T(8,128)(2,1)S(1)} all-to-all(bf16[8,16,2176]{2,1,0:T(8,128)(2,1)S(1)} %pad_maximum_fusion), channel_id=1, replica_groups=mesh['chip'=8,'core'=2,'res'=8] {'chip'}, dimensions={0} | all-to-all | bytes 1114112 | tf_op jit(solution)/shard_map/all_to_all | solution.py:346
  32.0 3.6 %collective-permute-start = (bf16[128,2176]{1,0:T(8,128)(2,1)S(1)}, bf16[128,2176]{1,0:T(8,128)(2,1)S(1)}, u32[]{:S(2)}, u32[]{:S(2)}) collective-permute-start(bf16[128,2176]{1,0:T(8,128)(2,1)S(1)} %bitcast.11), channel_id=1, source_target_pairs={{0,8},{8,0},{1,9},{9,1},{2,10},{10,2},{3,11},{11,3},{4,12},{12,4},... | collective-permute-start | bytes 1671176 | tf_op jit(solution)/shard_map/ppermute | solution.py:347
  35.6 1.6 %collective-permute-done.other_ref = bf16[128,2176]{1,0:T(8,128)(2,1)S(1)} collective-permute-done((bf16[128,2176]{1,0:T(8,128)(2,1)S(1)}, bf16[128,2176]{1,0:T(8,128)(2,1)S(1)}, u32[]{:S(2)}, u32[]{:S(2)}) %collective-permute-start) | collective-permute-done | bytes 557088 | tf_op jit(solution)/shard_map/ppermute | solution.py:347
  37.2 0.0 copy-done
  37.2 0.0 copy-done.1
  37.2 3.0 %shard_map.102 = (bf16[256,768]{1,0:T(8,128)(2,1)S(1)}, bf16[512,1024]{1,0:T(8,128)(2,1)S(1)}, bf16[512,1024]{1,0:T(8,128)(2,1)S(1)}, bf16[256,512]{1,0:T(8,128)...) custom-call(bf16[128,2176]{1,0:T(8,128)(2,1)S(1)} %bitcast.12, ...), custom_call_target="tpu_custom_call" | custom-call | tf_op jit(solution)/shard_map/pallas_call | solution.py:308
  40.1 0.5 collective-permute-start.1
  40.6 0.0 copy-done.2
  40.6 1.0 %shard_map.103 = (f32[512,128]{1,0:T(8,128)S(1)}, f32[256,512]{1,0:T(8,128)S(1)}, f32[512,128]{1,0:T(8,128)S(1)}, f32[256,512]{1,0:T(8,128)S(1)}) custom-call(bf16[512,1024]{1,0:T(8,128)(2,1)S(1)} %get-tuple-element.28.x_ref, bf16[512,1024]{1,0:T(8,128)(2,1)S(1)} %get-tuple-element.29.dy_ref, bf16[256,512]{1,0:T(8,128)(2,1)S(1)} %get-tuple-element.30.left_in, ...), custom_call_target="tpu_custom_call" | custom-call | tf_op jit(solution)/shard_map/pallas_call | solution.py:308
  41.6 0.3 collective-permute-done.1.got_ref
  42.0 0.4 shard_map.104
  42.3 18.2 %all_to_all.21.in_ref = bf16[128,4,640]{2,1,0:T(4,128)(2,1)S(1)} all-to-all(bf16[128,4,640]{2,1,0:T(4,128)(2,1)S(1)} %shard_map.104), channel_id=1, replica_groups=mesh['chip'=8,'core'=2,'res'=8] {'chip','core','res'}, dimensions={0} | all-to-all | bytes 1310720 | tf_op jit(solution)/shard_map/all_to_all | solution.py:395
  60.6 0.2 shard_map.105
  60.8 15.2 %all_to_all.22.in_ref.own_ref = bf16[128,8,128]{2,1,0:T(8,128)(2,1)S(1)} all-to-all(bf16[128,8,128]{2,1,0:T(8,128)(2,1)S(1)} %shard_map.105), channel_id=1, replica_groups=mesh['chip'=8,'core'=2,'res'=8] {'chip','core','res'}, dimensions={0} | all-to-all | bytes 524288 | tf_op jit(solution)/shard_map/all_to_all | solution.py:399
  76.0 1.0 %collective-permute-start.2 = (bf16[128,8,128]{2,1,0:T(8,128)(2,1)S(1)}, bf16[128,8,128]{2,1,0:T(8,128)(2,1)S(1)}, u32[]{:S(2)}, u32[]{:S(2)}) collective-permute-start(bf16[128,8,128]{2,1,0:T(8,128)(2,1)S(1)} %all_to_all.22.in_ref.own_ref), channel_id=1, source_target_pairs={{0,8},{8,0},{1,9},{9,1},{2,10},{10,2},{3,11},{11,3},{4,12},{12,4},... | collective-permute-start | bytes 786440 | tf_op jit(solution)/shard_map/ppermute | solution.py:400
  77.0 1.7 %shard_map.106 = (bf16[512,128]{1,0:T(8,128)(2,1)}, f32[512,32]{1,0:T(8,128)}, f32[512,32]{1,0:T(8,128)}, f32[1,128]{1,0:T(1,128)}) custom-call(bf16[128,8,128]{2,1,0:T(8,128)(2,1)S(1)} %all_to_all.22.in_ref.own_ref, f32[512,128]{1,0:T(8,128)S(1)} %get-tuple-element.40.update_ref), custom_call_target="tpu_custom_call" | custom-call | tf_op jit(solution)/shard_map/pallas_call | solution.py:308
  78.7 0.0 collective-permute-done.2.other_ref
  78.7 0.8 %shard_map.107 = f32[1024,128]{1,0:T(8,128)} custom-call(bf16[128,8,128]{2,1,0:T(8,128)(2,1)S(1)} %all_to_all.22.in_ref.own_ref, bf16[128,8,128]{2,1,0:T(8,128)(2,1)S(1)} %collective-permute-done.2.other_ref), custom_call_target="tpu_custom_call" | custom-call | tf_op jit(solution)/shard_map/pallas_call | solution.py:308
  (4 shorter events, 0.1 us)
Async XLA Ops:
  2.8 13.3 %all-to-all-start = ((bf16[8,16,1152]{2,1,0:T(8,128)(2,1)}), bf16[8,16,1152]{2,1,0:T(8,128)(2,1)S(1)}, u32[]{:S(2)}, u32[]{:S(2)}) async-start(bf16[8,16,1152]{2,1,0:T(8,128)(2,1)} %get-tuple-element.25), calls=%async_computation | async-start | bytes 589824 | tf_op jit(solution)/shard_map/all_to_all | solution.py:341
  16.2 21.0 %copy-start = (bf16[32,32,128]{2,1,0:T(8,128)(2,1)S(1)}, bf16[32,32,128]{2,1,0:T(8,128)(2,1)}, u32[]{:S(2)}) copy-start(bf16[32,32,128]{2,1,0:T(8,128)(2,1)} %param.9) | copy-start | bytes 786436
  16.2 21.0 %copy-start.1 = (bf16[16,32,128]{2,1,0:T(8,128)(2,1)S(1)}, bf16[16,32,128]{2,1,0:T(8,128)(2,1)}, u32[]{:S(2)}) copy-start(bf16[16,32,128]{2,1,0:T(8,128)(2,1)} %param.11) | copy-start | bytes 393220
  16.2 24.4 %copy-start.2 = (f32[128]{0:T(128)S(1)}, f32[128]{0:T(128)}, u32[]{:S(2)}) copy-start(f32[128]{0:T(128)} %param.10) | copy-start | bytes 1540
  32.0 5.2 %collective-permute-start = (bf16[128,2176]{1,0:T(8,128)(2,1)S(1)}, bf16[128,2176]{1,0:T(8,128)(2,1)S(1)}, u32[]{:S(2)}, u32[]{:S(2)}) collective-permute-start(bf16[128,2176]{1,0:T(8,128)(2,1)S(1)} %bitcast.11), channel_id=1, source_target_pairs={{0,8},{8,0},{1,9},{9,1},{2,10},{10,2},{3,11},{11,3},{4,12},{12,4},... | collective-permute-start | bytes 1671176 | tf_op jit(solution)/shard_map/ppermute | solution.py:347
  40.1 1.8 %collective-permute-start.1 = (bf16[256,768]{1,0:T(8,128)(2,1)S(1)}, bf16[256,768]{1,0:T(8,128)(2,1)S(1)}, u32[]{:S(2)}, u32[]{:S(2)}) collective-permute-start(bf16[256,768]{1,0:T(8,128)(2,1)S(1)} %get-tuple-element.27), channel_id=1, source_target_pairs={{0,8},{8,0},{1,9},{9,1},{2,10},{10,2},{3,11},{11,3},{4,12},{12,4},... | collective-permute-start | bytes 1179656 | tf_op jit(solution)/shard_map/ppermute | solution.py:370
  76.0 2.7 %collective-permute-start.2 = (bf16[128,8,128]{2,1,0:T(8,128)(2,1)S(1)}, bf16[128,8,128]{2,1,0:T(8,128)(2,1)S(1)}, u32[]{:S(2)}, u32[]{:S(2)}) collective-permute-start(bf16[128,8,128]{2,1,0:T(8,128)(2,1)S(1)} %all_to_all.22.in_ref.own_ref), channel_id=1, source_target_pairs={{0,8},{8,0},{1,9},{9,1},{2,10},{10,2},{3,11},{11,3},{4,12},{12,4},... | collective-permute-start | bytes 786440 | tf_op jit(solution)/shard_map/ppermute | solution.py:400

commit v5 on v4

--- a/solution.py
+++ b/solution.py
@@ -1,13 +1,14 @@
 import jax
 import jax.numpy as jnp
+import numpy as np
 from jax import lax
 from jax.experimental import pallas as pl
 from jax.experimental.pallas import tpu as pltpu
-from jax.sharding import Mesh
 from jax.sharding import PartitionSpec as P
 
 F32 = jnp.float32
 BF16 = jnp.bfloat16
+DEVICES = ("seq", "res")
 ROWS_ROWS = (((0,), (0,)), ((), ()))
 LANES_LANES = (((1,), (1,)), ((), ()))
 
@@ -38,13 +39,14 @@
     return condition.astype(F32).astype(BF16)
 
 
-def channel_lanes():
-    lane = iota((32, 512), 1)
-    return choose(iota((32, 512), 0) == 4 * ((lane % 128) // 16) + lane // 128)
-
-
-def own_residue():
-    return iota((512, 512), 0) % 16 == iota((512, 512), 1) % 16
+def lane_order():
+    lane = np.arange(512)
+    source = (lane % 16) * 32 + 4 * ((lane % 128) // 16) + lane // 128
+    return jnp.asarray(np.arange(512)[:, None] == source[None, :], BF16)
+
+
+def core_index():
+    return lax.axis_index("seq") % 2
 
 
 def low():
@@ -59,7 +61,7 @@
 
 
 def prep_kernel(
-    left_hbm, right_hbm, mask_hbm, left_out, right_out, left_ref, right_ref, mask_ref, right32_ref, sems
+    left_hbm, right_hbm, mask_hbm, left_out, right_out, left_ref, right_ref, mask_ref, wide_ref, sems
 ):
     copies = [
         pltpu.make_async_copy(left_hbm, left_ref, sems.at[0]),
@@ -70,54 +72,52 @@
         copy.start()
     for copy in copies:
         copy.wait()
-    spread = jnp.dot(left_ref[...], channel_lanes(), preferred_element_type=F32)
-    spread = jnp.where(own_residue(), spread, 0.0).astype(BF16)
-    row, col = iota((32, 512), 0), iota((32, 512), 1)
-    gather = choose((col // 32 == row % 16) & ((col % 32) // 16 == row // 16))
-    block = jnp.dot(gather, spread, preferred_element_type=F32).astype(BF16)
     mask = mask_ref[...].astype(F32).astype(BF16)
-    row, col = iota((32, 128), 0), iota((32, 128), 1)
-    masks = jnp.dot(mask, choose(row == col), preferred_element_type=F32).astype(BF16)
-    for r in range(8):
-        for h in range(2):
-            left_out[r, :, h * 512 : h * 512 + 512] = block[h * 16 : h * 16 + 16]
-        left_out[r, :, 1024:1152] = masks
-    right32_ref[...] = right_ref[...].astype(F32)
-    for k in range(8):
-        tile = [right32_ref[pl.ds(k * 4 + e, 16, stride=32), :] for e in range(4)]
-        right_out[:, k * 128 : k * 128 + 128] = jnp.concatenate(tile, 1).astype(BF16)
-    right_out[:, 1024:1152] = jnp.dot(mask, choose(row + 32 == col), preferred_element_type=F32).astype(BF16)
+    widen = choose(iota((32, 128), 0) == iota((32, 128), 1))
+    masks = jnp.dot(mask, widen, preferred_element_type=F32).astype(BF16)
+    for n, (ref, out_ref) in enumerate(((left_ref, left_out), (right_ref, right_out))):
+        wide_ref[n] = ref[...].astype(F32)
+        for k in range(8):
+            tile = [wide_ref[n, pl.ds(k * 4 + e, 16, stride=32), :] for e in range(4)]
+            out_ref[:, k * 128 : k * 128 + 128] = jnp.concatenate(tile, 1).astype(BF16)
+        out_ref[:, 1024:1152] = masks
 
 
 def outer_kernel(
-    own_ref, other_ref, w_ref, cot_ref,
+    own_ref, other_ref, lanes_ref, w_ref, cot_ref,
     send_ref, x_ref, dy_ref, left_ref, right_ref, mask_i_ref, mask_jd_ref, scaled_ref, inverse_ref, bsum_ref,
     y_ref, dx_ref, cot32_ref,
 ):
-    core = lax.axis_index("core")
+    core = core_index()
     keep = pl.multiple_of(core * 512, 512)
     give = pl.multiple_of((1 - core) * 512, 512)
 
-    def rows(lanes):
-        return jnp.concatenate([own_ref[:, lanes], other_ref[:, lanes]], 0)
+    def rows(lanes, of_left):
+        return jnp.where(core == (0 if of_left else 1), own_ref[:, lanes], other_ref[:, lanes])
 
     row, col = iota((256, 256), 0), iota((256, 256), 1)
     device = row % 16
-    order = choose(col == ((device + core) % 2) * 128 + (device // 2) * 16 + row // 16)
-    masks = jnp.dot(order, rows(slice(2048, 2176)), preferred_element_type=F32).astype(BF16)
-    left = jnp.dot(order, rows(pl.ds(keep, 512)), preferred_element_type=F32).astype(BF16)
-    right = jnp.dot(order, rows(slice(1024, 2048)), preferred_element_type=F32).astype(BF16)
+    left_order = choose(col == ((device // 2 + 4) % 8) * 32 + (device % 2) * 16 + row // 16)
+    right_order = choose(col == (device // 2) * 32 + (1 - device % 2) * 16 + row // 16)
+
+    def ordered(order, block):
+        return jnp.dot(order, block, preferred_element_type=F32).astype(BF16)
+
+    masks = ordered(left_order, rows(slice(1024, 1152), True))
+    left = ordered(ordered(left_order, rows(pl.ds(keep, 512), True)), lanes_ref[...])
+    right = ordered(right_order, rows(slice(0, 1152), False))
     lane = iota((128, 512), 1)
     spread_i = choose(iota((128, 512), 0) == core * 16 + lane % 16)
-    spread_j = choose(iota((128, 512), 0) == 32 + 4 * ((lane // 16) % 8) + lane // 128)
-    spread_jd = choose(iota((128, 1024), 0) == 32 + iota((128, 1024), 1) // 32)
+    spread_j = choose(iota((128, 512), 0) == 4 * ((lane // 16) % 8) + lane // 128)
+    spread_jd = choose(iota((128, 1024), 0) == iota((128, 1024), 1) // 32)
+    masks_j = right[:, 1024:1152]
     mask_i = jnp.dot(masks, spread_i, preferred_element_type=F32)
-    mask_j = jnp.dot(masks, spread_j, preferred_element_type=F32)
-    mask_jd = jnp.dot(masks, spread_jd, preferred_element_type=F32)
+    mask_j = jnp.dot(masks_j, spread_j, preferred_element_type=F32)
+    mask_jd = jnp.dot(masks_j, spread_jd, preferred_element_type=F32)
     mask_i_ref[...] = mask_i.astype(BF16)
     mask_jd_ref[...] = mask_jd.astype(BF16)
     left = left * mask_i_ref[...]
-    right = right * mask_jd_ref[...]
+    right = right[:, 0:1024] * mask_jd_ref[...]
     left_ref[...] = left
     right_ref[...] = right
     both = (mask_i * mask_j).astype(BF16)
@@ -172,16 +172,17 @@
 
 
 def sums_kernel(
-    x_ref, dy_ref, left_in, right_in, mask_i_ref, mask_jd_ref, scaled_ref, inverse_ref, w_ref, bias_ref,
+    x_ref, dy_ref, left_in, right_in, mask_i_ref, mask_jd_ref, scaled_ref, inverse_ref, lanes_ref, w_ref, bias_ref,
     update_ref, right_ref, weight_ref, left_ref,
 ):
-    keep = pl.multiple_of(lax.axis_index("core") * 512, 512)
+    keep = pl.multiple_of(core_index() * 512, 512)
     right_ref[...] = right_part(keep, left_in[...], dy_ref, mask_jd_ref)
     weight_ref[...] = weight_part(keep, x_ref, scaled_ref[...])
     left = lax.dot_general(right_in[...], dy_ref[...], LANES_LANES, preferred_element_type=F32)
-    left_ref[...] = left * mask_i_ref[...].astype(F32)
+    left = (left * mask_i_ref[...].astype(F32)).astype(BF16)
+    left_ref[...] = lax.dot_general(left, lanes_ref[...], LANES_LANES, preferred_element_type=F32)
     update_ref[...] = (
-        jnp.dot(x_ref[...], w_ref[...], preferred_element_type=F32) * inverse_ref[...] + bias_ref[...]
+        jnp.dot(x_ref[...], w_ref[...], preferred_element_type=F32) * inverse_ref[...] + bias_ref[0:1, :]
     )
 
 
@@ -279,21 +280,15 @@
         ]
         return [p[0] for p in pairs], [p[1] for p in pairs]
 
-    near, far = tiles(4)
-    for k, tile in enumerate(near + far):
-        for e in range(4):
-            right_ref[pl.ds(k * 4 + e, 16, stride=32), :] = tile[:, e * 32 : e * 32 + 32]
-    near, far = tiles(5)
-    left = jnp.concatenate([jnp.concatenate(near, 1), jnp.concatenate(far, 1)], 0).astype(BF16)
-    row, col = iota((512, 32), 0), iota((512, 32), 1)
-    scatter = choose((row // 32 == col % 16) & ((row % 32) // 16 == col // 16))
-    spread = jnp.dot(scatter, left, preferred_element_type=F32)
-    spread = jnp.where(own_residue(), spread, 0.0).astype(BF16)
-    left_ref[...] = lax.dot_general(spread, channel_lanes(), LANES_LANES, preferred_element_type=F32)
+    for row, out_ref in ((4, right_ref), (5, left_ref)):
+        near, far = tiles(row)
+        for k, tile in enumerate(near + far):
+            for e in range(4):
+                out_ref[pl.ds(k * 4 + e, 16, stride=32), :] = tile[:, e * 32 : e * 32 + 32]
 
 
 def weight_kernel(own_ref, other_ref, out_hbm, rows_ref, sems):
-    core = lax.axis_index("core")
+    core = core_index()
     copies = []
     for n, (ref, half) in enumerate(((own_ref, core), (other_ref, 1 - core))):
         weight_rows(ref, rows_ref.at[n])
@@ -320,16 +315,27 @@
 
 
 def per_device(left, right, mask, weight, bias, cotangent):
-    swap = [(0, 1), (1, 0)]
-    devices = ("chip", "core", "res")
-    block, rights = call(
+    everyone = [(a, core, b) for a in range(8) for core in range(2) for b in range(8)]
+
+    def place(a, core, b):
+        return (a * 2 + core) * 8 + b
+
+    swap = [(place(a, core, b), place(a, 1 - core, b)) for a, core, b in everyone]
+    turn = [(place(a, core, b), place(b, core, (a + 4) % 8)) for a, core, b in everyone]
+    groups = [[place(a, 0, b) for b in range(8)] for a in range(8)]
+    groups += [[place(a, 1, b) for a in range(8)] for b in range(8)]
+
+    def exchange(block, groups=None):
+        return lax.all_to_all(block, DEVICES, 0, 0, axis_index_groups=groups, tiled=True)
+
+    left_block, right_block = call(
         prep_kernel,
-        (shape((8, 16, 1152), BF16), shape((16, 1152), BF16)),
+        (shape((16, 1152), BF16), shape((16, 1152), BF16)),
         [
             pltpu.VMEM((512, 32), BF16),
             pltpu.VMEM((512, 32), BF16),
             pltpu.VMEM((16, 32), jnp.int32),
-            pltpu.VMEM((512, 32), F32),
+            pltpu.VMEM((2, 512, 32), F32),
             pltpu.SemaphoreType.DMA((3,)),
         ],
         left.reshape(512, 32),
@@ -338,13 +344,17 @@
         space=pltpu.HBM,
         mib=60,
     )
-    block = lax.all_to_all(block, "res", 0, 0, tiled=True)
-    rights = jnp.broadcast_to(rights, (8, 16, 1152))
-    block = jnp.concatenate(
-        [block[..., :1024], rights[..., :1024], block[..., 1024:] + rights[..., 1024:]], -1
-    )
-    own = lax.all_to_all(block, "chip", 0, 0, tiled=True).reshape(128, 2176)
-    other = lax.ppermute(own, "core", swap)
+    bias = jnp.broadcast_to(bias, (8, 128))
+    left_block, bias = lax.optimization_barrier((lax.ppermute(left_block, DEVICES, turn), bias))
+    other_right = lax.ppermute(right_block, DEVICES, swap)
+    other_left = lax.ppermute(left_block, DEVICES, swap)
+    block = jnp.where(
+        core_index() == 0, jnp.stack([left_block, other_left]), jnp.stack([right_block, other_right])
+    )
+    block = jnp.broadcast_to(block, (8, 2, 16, 1152))
+    own = exchange(block, groups).reshape(256, 1152)
+    other = lax.ppermute(own, DEVICES, swap)
+    lanes = lane_order()
 
     weight = weight.reshape(1024, 128)
     send, outer, outer_grad, left_all, right_all, mask_i, mask_jd, scaled, inverse, bias_part = call(
@@ -364,10 +374,11 @@
         [pltpu.VMEM((512, 1024), F32), pltpu.VMEM((512, 1024), F32), pltpu.VMEM((512, 128), F32)],
         own,
         other,
+        lanes,
         weight,
         cotangent.reshape(512, 128),
     )
-    got = lax.ppermute(send, "core", swap)
+    got = lax.ppermute(send, DEVICES, swap)
     update, right_sum, weight_sum, left_sum = call(
         sums_kernel,
         (shape((512, 128), F32), shape((256, 512), F32), shape((512, 128), F32), shape((256, 512), F32)),
@@ -380,8 +391,9 @@
         mask_jd,
         scaled,
         inverse,
+        lanes,
         weight,
-        bias.reshape(1, 128),
+        bias,
     )
     (parts,) = call(
         pack_kernel,
@@ -392,12 +404,12 @@
         weight_sum,
         left_sum,
     )
-    parts = lax.all_to_all(parts, devices, 0, 0, tiled=True)
+    parts = exchange(parts)
     (sums,) = call(
         reduce_kernel, (shape((128, 8, 128), BF16),), [pltpu.VMEM((1024, 128), F32)], parts, bias_part
     )
-    sums = lax.all_to_all(sums, devices, 0, 0, tiled=True)
-    other_sums = lax.ppermute(sums, "core", swap)
+    sums = exchange(sums)
+    other_sums = lax.ppermute(sums, DEVICES, swap)
     pair_update, right_grad, left_grad, bias_grad = call(
         operand_kernel,
         (shape((512, 128), BF16), shape((512, 32), F32), shape((512, 32), F32), shape((1, 128), F32)),
@@ -423,19 +435,17 @@
 
 
 def solution(mesh):
-    mesh = Mesh(mesh.devices.reshape(8, 2, 8), ("chip", "core", "res"))
-    seq = ("chip", "core")
     return jax.shard_map(
         per_device,
         mesh=mesh,
         in_specs=(
-            P(seq, "res", None),
-            P(seq, "res", None),
-            P(seq, "res"),
+            P("seq", "res", None),
+            P("seq", "res", None),
+            P("seq", "res"),
             P(),
             P(),
-            P(seq, "res", None),
+            P("seq", "res", None),
         ),
-        out_specs=(P(seq, "res", None), P(seq, "res", None), P(seq, "res", None), P(), P()),
+        out_specs=(P("seq", "res", None), P("seq", "res", None), P("seq", "res", None), P(), P()),
         check_vma=False,
     )

time: 80 us -> 77.9 us (0.974)
  blocking collectives: 49.2 us -> 53.8 us
  waiting for transfers between devices: 6.91 us -> 3.08 us
  local copies, waits for them, and re-layouts: 1.5 us -> 0.08 us
  starting transfers between devices: 12 us -> 10.8 us
    all_to_all x1 -> x0, starting transfers between devices: 6.89 us -> none  [per_device(): block = lax.all_to_all(block, 'res', 0, 0, tiled=True)]
    ppermute x3 -> x6, starting transfers between devices: 5.08 us -> 10.8 us  [the longest x1 4.49 us: per_device(): lax.ppermute(left_block, DEVICES, turn)]
    all_to_all x1 -> x0, waiting for transfers between devices: 4.97 us -> none  [per_device(): block = lax.all_to_all(block, 'res', 0, 0, tiled=True)]
    all_to_all x3, blocking collectives: 49.2 us -> 53.8 us  [exchange(): lax.all_to_all(block, DEVICES, 0, 0, axis_index_groups=groups, tiled=True)]
    slice x3 -> x0, local copies, waits for them, and re-layouts: 1.47 us -> none  [the longest x1 0.76 us: per_device(): rights[..., :1024]]
    ppermute x3 -> x6, waiting for transfers between devices: 1.93 us -> 3.08 us  [the longest x1 1.63 us: per_device(): other = lax.ppermute(own, DEVICES, swap)]
  transfers between devices with their start and end apart: 4 -> 6, of which waited for: 3 -> 4; matrix products, arithmetic and copies ran while one was open for 2% -> 0% of each run, Pallas kernels for 3% -> 3%
where the time goes in v5:
time: 77.9 us; the launch traced here: 77.7 us
  blocking collectives  53.8 us (69%)
  starting transfers between devices  10.8 us (14%)
  Pallas kernels  9.18 us (12%)
  waiting for transfers between devices  3.08 us (4%)
    all_to_all x3, blocking collectives, exchange(): lax.all_to_all(block, DEVICES, 0, 0, axis_index_groups=groups, tiled=True)  53.8 us
    pallas_call x7, Pallas kernels, call(): pl.pallas_call(kernel, out_shape=outs, in_specs=[pl.BlockSpec(memory_spac...  9.18 us
    ppermute x1, starting transfers between devices, per_device(): lax.ppermute(left_block, DEVICES, turn)  4.49 us
    ppermute x1, starting transfers between devices, per_device(): other = lax.ppermute(own, DEVICES, swap)  2.35 us
    ppermute x1, waiting for transfers between devices, per_device(): other = lax.ppermute(own, DEVICES, swap)  1.63 us
  transfers between devices with their start and end apart: 6, of which 4 were waited for; matrix products, arithmetic and copies ran while one was open for 0% of the time, Pallas kernels for 3%

profile of v5, /device:TPU:1, one launch (start us, length us, event | category | flops | bytes accessed | tf_op | source)
XLA Modules:
  0.0 77.7 jit_solution(18037798674615853813)
XLA Ops:
  0.6 0.0 copy-start.4
  0.6 1.9 %shard_map.110 = (bf16[16,1152]{1,0:T(8,128)(2,1)}, bf16[16,1152]{1,0:T(8,128)(2,1)}) custom-call(bf16[512,32]{1,0:T(8,128)(2,1)} %bitcast.20, bf16[512,32]{1,0:T(8,128)(2,1)} %bitcast.21, s32[16,32]{1,0:T(8,128)} %mask_hbm.1), custom_call_target="tpu_custom_call" | custom-call | tf_op jit(solution)/shard_map/pallas_call | solution.py:303
  2.6 0.0 copy-start.3
  2.6 4.5 %collective-permute-start = (bf16[16,1152]{1,0:T(8,128)(2,1)}, bf16[16,1152]{1,0:T(8,128)(2,1)S(1)}, u32[]{:S(2)}, u32[]{:S(2)}) collective-permute-start(bf16[16,1152]{1,0:T(8,128)(2,1)} %get-tuple-element.27), channel_id=1, source_target_pairs={{0,4},{1,20},{2,36},{3,52},{4,68},{5,84},{6,100},{7,116},{8,12},{9... | collective-permute-start | bytes 110600 | tf_op jit(solution)/shard_map/ppermute | solution.py:348
  7.1 1.0 %collective-permute-start.2 = (bf16[16,1152]{1,0:T(8,128)(2,1)}, bf16[16,1152]{1,0:T(8,128)(2,1)S(1)}, u32[]{:S(2)}, u32[]{:S(2)}) collective-permute-start(bf16[16,1152]{1,0:T(8,128)(2,1)} %get-tuple-element.29), channel_id=1, source_target_pairs={{0,8},{1,9},{2,10},{3,11},{4,12},{5,13},{6,14},{7,15},{8,0},{9,1},... | collective-permute-start | bytes 110600 | tf_op jit(solution)/shard_map/ppermute | solution.py:349
  8.1 0.4 collective-permute-done
  8.5 0.0 copy-done.4
  8.5 1.5 %collective-permute-start.1 = (bf16[16,1152]{1,0:T(8,128)(2,1)S(1)}, bf16[16,1152]{1,0:T(8,128)(2,1)S(1)}, u32[]{:S(2)}, u32[]{:S(2)}) collective-permute-start(bf16[16,1152]{1,0:T(8,128)(2,1)S(1)} %collective-permute-done), channel_id=1, source_target_pairs={{0,8},{1,9},{2,10},{3,11},{4,12},{5,13},{6,14},{7,15},{8,0},{9,1},... | collective-permute-start | bytes 110600 | tf_op jit(solution)/shard_map/ppermute | solution.py:350
  10.0 0.0 collective-permute-done.2
  10.0 0.9 %collective-permute-done.1 = bf16[16,1152]{1,0:T(8,128)(2,1)S(1)} collective-permute-done((bf16[16,1152]{1,0:T(8,128)(2,1)S(1)}, bf16[16,1152]{1,0:T(8,128)(2,1)S(1)}, u32[]{:S(2)}, u32[]{:S(2)}) %collective-permute-start.1) | collective-permute-done | bytes 36896 | tf_op jit(solution)/shard_map/ppermute | solution.py:350
  10.9 0.0 copy-done.3
  11.0 0.0 copy-start
  11.0 0.0 copy-start.1
  11.0 0.0 copy-start.2
  11.0 17.2 %all_to_all.15 = bf16[8,2,16,1152]{3,2,1,0:T(8,128)(2,1)S(1)} all-to-all(bf16[8,2,16,1152]{3,2,1,0:T(8,128)(2,1)S(1)} %broadcast_in_dim.7), channel_id=1, replica_groups={{0,1,2,3,4,5,6,7},{16,17,18,19,20,21,22,23},{32,33,34,35,36,37,38,39},{..., dimensions={0} | all-to-all | bytes 1179648 | tf_op jit(solution)/shard_map/all_to_all | solution.py:329
  28.2 2.4 %collective-permute-start.3 = (bf16[256,1152]{1,0:T(8,128)(2,1)S(1)}, bf16[256,1152]{1,0:T(8,128)(2,1)S(1)}, u32[]{:S(2)}, u32[]{:S(2)}) collective-permute-start(bf16[256,1152]{1,0:T(8,128)(2,1)S(1)} %bitcast.14), channel_id=1, source_target_pairs={{0,8},{1,9},{2,10},{3,11},{4,12},{5,13},{6,14},{7,15},{8,0},{9,1},... | collective-permute-start | bytes 1769480 | tf_op jit(solution)/shard_map/ppermute | solution.py:356
  30.6 1.6 %collective-permute-done.3.other_ref = bf16[256,1152]{1,0:T(8,128)(2,1)S(1)} collective-permute-done((bf16[256,1152]{1,0:T(8,128)(2,1)S(1)}, bf16[256,1152]{1,0:T(8,128)(2,1)S(1)}, u32[]{:S(2)}, u32[]{:S(2)}) %collective-permute-start.3) | collective-permute-done | bytes 589856 | tf_op jit(solution)/shard_map/ppermute | solution.py:356
  32.2 0.0 copy-done
  32.2 0.0 copy-done.1
  32.2 0.0 copy-done.2
  32.2 3.2 %shard_map.111 = (bf16[256,768]{1,0:T(8,128)(2,1)S(1)}, bf16[512,1024]{1,0:T(8,128)(2,1)S(1)}, bf16[512,1024]{1,0:T(8,128)(2,1)S(1)}, bf16[256,512]{1,0:T(8,128)...) custom-call(bf16[256,1152]{1,0:T(8,128)(2,1)S(1)} %bitcast.15, ...), custom_call_target="tpu_custom_call" | custom-call | tf_op jit(solution)/shard_map/pallas_call | solution.py:303
  35.4 0.5 collective-permute-start.4
  35.9 1.2 %shard_map.112 = (f32[512,128]{1,0:T(8,128)S(1)}, f32[256,512]{1,0:T(8,128)S(1)}, f32[512,128]{1,0:T(8,128)S(1)}, f32[256,512]{1,0:T(8,128)S(1)}) custom-call(bf16[512,1024]{1,0:T(8,128)(2,1)S(1)} %get-tuple-element.31.x_ref, bf16[512,1024]{1,0:T(8,128)(2,1)S(1)} %get-tuple-element.32.dy_ref, bf16[256,512]{1,0:T(8,128)(2,1)S(1)} %get-tuple-element.33.left_in, ...), custom_call_target="tpu_custom_call" | custom-call | tf_op jit(solution)/shard_map/pallas_call | solution.py:303
  37.1 0.2 collective-permute-done.4.got_ref
  37.2 0.4 shard_map.113
  37.6 21.4 %all_to_all.16.in_ref = bf16[128,4,640]{2,1,0:T(4,128)(2,1)S(1)} all-to-all(bf16[128,4,640]{2,1,0:T(4,128)(2,1)S(1)} %shard_map.113), channel_id=1, replica_groups=mesh['seq'=16,'res'=8] {'seq','res'}, dimensions={0} | all-to-all | bytes 1310720 | tf_op jit(solution)/shard_map/all_to_all | solution.py:329
  59.0 0.2 shard_map.114
  59.2 15.2 %all_to_all.17.in_ref.own_ref = bf16[128,8,128]{2,1,0:T(8,128)(2,1)S(1)} all-to-all(bf16[128,8,128]{2,1,0:T(8,128)(2,1)S(1)} %shard_map.114), channel_id=1, replica_groups=mesh['seq'=16,'res'=8] {'seq','res'}, dimensions={0} | all-to-all | bytes 524288 | tf_op jit(solution)/shard_map/all_to_all | solution.py:329
  74.5 1.0 %collective-permute-start.5 = (bf16[128,8,128]{2,1,0:T(8,128)(2,1)S(1)}, bf16[128,8,128]{2,1,0:T(8,128)(2,1)S(1)}, u32[]{:S(2)}, u32[]{:S(2)}) collective-permute-start(bf16[128,8,128]{2,1,0:T(8,128)(2,1)S(1)} %all_to_all.17.in_ref.own_ref), channel_id=1, source_target_pairs={{0,8},{1,9},{2,10},{3,11},{4,12},{5,13},{6,14},{7,15},{8,0},{9,1},... | collective-permute-start | bytes 786440 | tf_op jit(solution)/shard_map/ppermute | solution.py:412
  75.4 1.4 %shard_map.115 = (bf16[512,128]{1,0:T(8,128)(2,1)}, f32[512,32]{1,0:T(8,128)}, f32[512,32]{1,0:T(8,128)}, f32[1,128]{1,0:T(1,128)}) custom-call(bf16[128,8,128]{2,1,0:T(8,128)(2,1)S(1)} %all_to_all.17.in_ref.own_ref, f32[512,128]{1,0:T(8,128)S(1)} %get-tuple-element.44.update_ref), custom_call_target="tpu_custom_call" | custom-call | tf_op jit(solution)/shard_map/pallas_call | solution.py:303
  76.8 0.0 collective-permute-done.5.other_ref
  76.8 0.8 %shard_map.116 = f32[1024,128]{1,0:T(8,128)} custom-call(bf16[128,8,128]{2,1,0:T(8,128)(2,1)S(1)} %all_to_all.17.in_ref.own_ref, bf16[128,8,128]{2,1,0:T(8,128)(2,1)S(1)} %collective-permute-done.5.other_ref), custom_call_target="tpu_custom_call" | custom-call | tf_op jit(solution)/shard_map/pallas_call | solution.py:303
  (3 shorter events, 0.1 us)
Async XLA Ops:
  0.6 7.8 %copy-start.4 = (f32[128]{0:T(128)S(1)}, f32[128]{0:T(128)}, u32[]{:S(2)}) copy-start(f32[128]{0:T(128)} %param.11) | copy-start | bytes 1540
  2.6 8.3 %copy-start.3 = (bf16[16,1152]{1,0:T(8,128)(2,1)S(1)}, bf16[16,1152]{1,0:T(8,128)(2,1)}, u32[]{:S(2)}) copy-start(bf16[16,1152]{1,0:T(8,128)(2,1)} %get-tuple-element.29) | copy-start | bytes 110596
  2.6 5.9 %collective-permute-start = (bf16[16,1152]{1,0:T(8,128)(2,1)}, bf16[16,1152]{1,0:T(8,128)(2,1)S(1)}, u32[]{:S(2)}, u32[]{:S(2)}) collective-permute-start(bf16[16,1152]{1,0:T(8,128)(2,1)} %get-tuple-element.27), channel_id=1, source_target_pairs={{0,4},{1,20},{2,36},{3,52},{4,68},{5,84},{6,100},{7,116},{8,12},{9... | collective-permute-start | bytes 110600 | tf_op jit(solution)/shard_map/ppermute | solution.py:348
  7.1 2.9 %collective-permute-start.2 = (bf16[16,1152]{1,0:T(8,128)(2,1)}, bf16[16,1152]{1,0:T(8,128)(2,1)S(1)}, u32[]{:S(2)}, u32[]{:S(2)}) collective-permute-start(bf16[16,1152]{1,0:T(8,128)(2,1)} %get-tuple-element.29), channel_id=1, source_target_pairs={{0,8},{1,9},{2,10},{3,11},{4,12},{5,13},{6,14},{7,15},{8,0},{9,1},... | collective-permute-start | bytes 110600 | tf_op jit(solution)/shard_map/ppermute | solution.py:349
  8.5 2.4 %collective-permute-start.1 = (bf16[16,1152]{1,0:T(8,128)(2,1)S(1)}, bf16[16,1152]{1,0:T(8,128)(2,1)S(1)}, u32[]{:S(2)}, u32[]{:S(2)}) collective-permute-start(bf16[16,1152]{1,0:T(8,128)(2,1)S(1)} %collective-permute-done), channel_id=1, source_target_pairs={{0,8},{1,9},{2,10},{3,11},{4,12},{5,13},{6,14},{7,15},{8,0},{9,1},... | collective-permute-start | bytes 110600 | tf_op jit(solution)/shard_map/ppermute | solution.py:350
  11.0 21.3 %copy-start = (bf16[512,512]{1,0:T(8,128)(2,1)S(1)}, bf16[512,512]{1,0:T(8,128)(2,1)}, u32[]{:S(2)}) copy-start(bf16[512,512]{1,0:T(8,128)(2,1)} %constant.22.clone.lanes_ref) | copy-start | bytes 1572868
  11.0 21.3 %copy-start.1 = (bf16[32,32,128]{2,1,0:T(8,128)(2,1)S(1)}, bf16[32,32,128]{2,1,0:T(8,128)(2,1)}, u32[]{:S(2)}) copy-start(bf16[32,32,128]{2,1,0:T(8,128)(2,1)} %param.10) | copy-start | bytes 786436
  11.0 21.2 %copy-start.2 = (bf16[16,32,128]{2,1,0:T(8,128)(2,1)S(1)}, bf16[16,32,128]{2,1,0:T(8,128)(2,1)}, u32[]{:S(2)}) copy-start(bf16[16,32,128]{2,1,0:T(8,128)(2,1)} %param.12) | copy-start | bytes 393220
  28.2 4.0 %collective-permute-start.3 = (bf16[256,1152]{1,0:T(8,128)(2,1)S(1)}, bf16[256,1152]{1,0:T(8,128)(2,1)S(1)}, u32[]{:S(2)}, u32[]{:S(2)}) collective-permute-start(bf16[256,1152]{1,0:T(8,128)(2,1)S(1)} %bitcast.14), channel_id=1, source_target_pairs={{0,8},{1,9},{2,10},{3,11},{4,12},{5,13},{6,14},{7,15},{8,0},{9,1},... | collective-permute-start | bytes 1769480 | tf_op jit(solution)/shard_map/ppermute | solution.py:356
  35.4 1.8 %collective-permute-start.4 = (bf16[256,768]{1,0:T(8,128)(2,1)S(1)}, bf16[256,768]{1,0:T(8,128)(2,1)S(1)}, u32[]{:S(2)}, u32[]{:S(2)}) collective-permute-start(bf16[256,768]{1,0:T(8,128)(2,1)S(1)} %get-tuple-element.30), channel_id=1, source_target_pairs={{0,8},{1,9},{2,10},{3,11},{4,12},{5,13},{6,14},{7,15},{8,0},{9,1},... | collective-permute-start | bytes 1179656 | tf_op jit(solution)/shard_map/ppermute | solution.py:381
  74.5 2.4 %collective-permute-start.5 = (bf16[128,8,128]{2,1,0:T(8,128)(2,1)S(1)}, bf16[128,8,128]{2,1,0:T(8,128)(2,1)S(1)}, u32[]{:S(2)}, u32[]{:S(2)}) collective-permute-start(bf16[128,8,128]{2,1,0:T(8,128)(2,1)S(1)} %all_to_all.17.in_ref.own_ref), channel_id=1, source_target_pairs={{0,8},{1,9},{2,10},{3,11},{4,12},{5,13},{6,14},{7,15},{8,0},{9,1},... | collective-permute-start | bytes 786440 | tf_op jit(solution)/shard_map/ppermute | solution.py:412

commit v6 on v5

--- a/solution.py
+++ b/solution.py
@@ -43,6 +43,18 @@
     lane = np.arange(512)
     source = (lane % 16) * 32 + 4 * ((lane % 128) // 16) + lane // 128
     return jnp.asarray(np.arange(512)[:, None] == source[None, :], BF16)
+
+
+def row_order():
+    row = np.arange(256)
+    return jnp.asarray((row % 16 * 16 + row // 16)[:, None] == row[None, :], BF16)
+
+
+def mask_spread():
+    lane = np.arange(512)
+    pairs = 4 * (lane // 16 % 8) + lane // 128
+    lanes = np.concatenate([pairs, np.arange(1024) // 32])
+    return jnp.asarray(np.arange(128)[:, None] == lanes[None, :], BF16)
 
 
 def core_index():
@@ -83,10 +95,19 @@
         out_ref[:, 1024:1152] = masks
 
 
+def cotangent_kernel(cot_ref, rows_ref, bsum_ref, cot32_ref):
+    cot32 = cot_ref[...].astype(F32)
+    cot32_ref[...] = cot32
+    bsum_ref[...] = jnp.sum(cot32, axis=0, keepdims=True)
+    for j in range(32):
+        at = ((j % 4) * 8 + j // 4) * 16
+        rows_ref[at : at + 16, :] = cot32_ref[pl.ds(j, 16, stride=32), :]
+
+
 def outer_kernel(
-    own_ref, other_ref, lanes_ref, w_ref, cot_ref,
-    send_ref, x_ref, dy_ref, left_ref, right_ref, mask_i_ref, mask_jd_ref, scaled_ref, inverse_ref, bsum_ref,
-    y_ref, dx_ref, cot32_ref,
+    own_ref, other_ref, lanes_ref, spread_ref, w_ref, cot_ref,
+    send_ref, x_ref, dy_ref, left_ref, right_ref, mask_i_ref, mask_jd_ref, scaled_ref, inverse_ref,
+    y_ref, dx_ref,
 ):
     core = core_index()
     keep = pl.multiple_of(core * 512, 512)
@@ -95,25 +116,18 @@
     def rows(lanes, of_left):
         return jnp.where(core == (0 if of_left else 1), own_ref[:, lanes], other_ref[:, lanes])
 
-    row, col = iota((256, 256), 0), iota((256, 256), 1)
-    device = row % 16
-    left_order = choose(col == ((device // 2 + 4) % 8) * 32 + (device % 2) * 16 + row // 16)
-    right_order = choose(col == (device // 2) * 32 + (1 - device % 2) * 16 + row // 16)
-
-    def ordered(order, block):
-        return jnp.dot(order, block, preferred_element_type=F32).astype(BF16)
-
-    masks = ordered(left_order, rows(slice(1024, 1152), True))
-    left = ordered(ordered(left_order, rows(pl.ds(keep, 512), True)), lanes_ref[...])
-    right = ordered(right_order, rows(slice(0, 1152), False))
-    lane = iota((128, 512), 1)
-    spread_i = choose(iota((128, 512), 0) == core * 16 + lane % 16)
-    spread_j = choose(iota((128, 512), 0) == 4 * ((lane // 16) % 8) + lane // 128)
-    spread_jd = choose(iota((128, 1024), 0) == iota((128, 1024), 1) // 32)
+    def turned(block):
+        return jnp.concatenate([block[128:256], block[0:128]], 0)
+
+    masks = turned(rows(slice(1024, 1152), True))
+    left = turned(rows(pl.ds(keep, 512), True))
+    left = jnp.dot(left, lanes_ref[...], preferred_element_type=F32).astype(BF16)
+    right = rows(slice(0, 1152), False)
+    spread_i = choose(iota((128, 512), 0) == core * 16 + iota((128, 512), 1) % 16)
     masks_j = right[:, 1024:1152]
     mask_i = jnp.dot(masks, spread_i, preferred_element_type=F32)
-    mask_j = jnp.dot(masks_j, spread_j, preferred_element_type=F32)
-    mask_jd = jnp.dot(masks_j, spread_jd, preferred_element_type=F32)
+    mask_j = jnp.dot(masks_j, spread_ref[:, 0:512], preferred_element_type=F32)
+    mask_jd = jnp.dot(masks_j, spread_ref[:, 512:1536], preferred_element_type=F32)
     mask_i_ref[...] = mask_i.astype(BF16)
     mask_jd_ref[...] = mask_jd.astype(BF16)
     left = left * mask_i_ref[...]
@@ -126,15 +140,8 @@
     )
     inverse = 1.0 / counts
     inverse_ref[...] = inverse
-    cot32 = cot_ref[...].astype(F32)
-    cot32_ref[...] = cot32
-    bsum_ref[...] = jnp.sum(cot32, axis=0, keepdims=True)
-    for j in range(32):
-        at = ((j % 4) * 8 + j // 4) * 16
-        scaled_ref[at : at + 16, :] = (
-            cot32_ref[pl.ds(j, 16, stride=32), :] * inverse[at : at + 16, :]
-        ).astype(BF16)
-    scaled = scaled_ref[...]
+    scaled = (cot_ref[...] * inverse).astype(BF16)
+    scaled_ref[...] = scaled
 
     y_ref[...] = lax.dot_general(left, right, ROWS_ROWS, preferred_element_type=F32)
     for u in range(8):
@@ -172,30 +179,33 @@
 
 
 def sums_kernel(
-    x_ref, dy_ref, left_in, right_in, mask_i_ref, mask_jd_ref, scaled_ref, inverse_ref, lanes_ref, w_ref, bias_ref,
+    x_ref, dy_ref, left_in, right_in, mask_i_ref, mask_jd_ref, scaled_ref, inverse_ref, lanes_ref, order_ref, w_ref, bias_ref,
     update_ref, right_ref, weight_ref, left_ref,
 ):
     keep = pl.multiple_of(core_index() * 512, 512)
-    right_ref[...] = right_part(keep, left_in[...], dy_ref, mask_jd_ref)
-    weight_ref[...] = weight_part(keep, x_ref, scaled_ref[...])
     left = lax.dot_general(right_in[...], dy_ref[...], LANES_LANES, preferred_element_type=F32)
     left = (left * mask_i_ref[...].astype(F32)).astype(BF16)
-    left_ref[...] = lax.dot_general(left, lanes_ref[...], LANES_LANES, preferred_element_type=F32)
+    right_ref[...] = right_part(keep, left_in[...], dy_ref, mask_jd_ref)
+    left = lax.dot_general(left, lanes_ref[...], LANES_LANES, preferred_element_type=F32).astype(BF16)
+    weight_ref[...] = weight_part(keep, x_ref, scaled_ref[...])
+    left_ref[...] = jnp.dot(order_ref[...], left, preferred_element_type=F32)
     update_ref[...] = (
         jnp.dot(x_ref[...], w_ref[...], preferred_element_type=F32) * inverse_ref[...] + bias_ref[0:1, :]
     )
 
 
-def pack_kernel(got_ref, right_ref, weight_ref, left_ref, msg_ref):
+def pack_kernel(got_ref, right_ref, weight_ref, left_ref, order_ref, msg_ref, sum_ref):
     lower = low()
     upper_rows = iota((8, 128), 0) >= 4
+    total = (right_ref[...] + got_ref[:, 0:512].astype(F32)).astype(BF16)
+    sum_ref[...] = jnp.dot(order_ref[...], total, preferred_element_type=F32)
     for s in range(16):
         for k in range(4):
             m = s * 8 + k * 2
             lanes = slice(k * 128, k * 128 + 128)
-            total = right_ref[s * 16 : s * 16 + 16, lanes] + got_ref[s * 16 : s * 16 + 16, lanes].astype(F32)
             tiles = []
-            for block in (total, left_ref[s * 16 : s * 16 + 16, lanes]):
+            for ref in (sum_ref, left_ref):
+                block = ref[s * 16 : s * 16 + 16, lanes]
                 even, odd = fold(block[0:8], block[8:16], lower)
                 tiles.append(jnp.where(upper_rows, pltpu.roll(odd, 4, 0), even))
                 tiles.append(jnp.where(upper_rows, odd, pltpu.roll(even, 4, 0)))
@@ -349,15 +359,22 @@
     other_right = lax.ppermute(right_block, DEVICES, swap)
     other_left = lax.ppermute(left_block, DEVICES, swap)
     block = jnp.where(
-        core_index() == 0, jnp.stack([left_block, other_left]), jnp.stack([right_block, other_right])
+        core_index() == 0, jnp.stack([left_block, other_left]), jnp.stack([other_right, right_block])
     )
     block = jnp.broadcast_to(block, (8, 2, 16, 1152))
     own = exchange(block, groups).reshape(256, 1152)
+    own, cotangent = lax.optimization_barrier((own, cotangent))
     other = lax.ppermute(own, DEVICES, swap)
-    lanes = lane_order()
+    cot_rows, bias_part = call(
+        cotangent_kernel,
+        (shape((512, 128), F32), shape((1, 128), F32)),
+        [pltpu.VMEM((512, 128), F32)],
+        cotangent.reshape(512, 128),
+    )
+    lanes, order = lane_order(), row_order()
 
     weight = weight.reshape(1024, 128)
-    send, outer, outer_grad, left_all, right_all, mask_i, mask_jd, scaled, inverse, bias_part = call(
+    send, outer, outer_grad, left_all, right_all, mask_i, mask_jd, scaled, inverse = call(
         outer_kernel,
         (
             shape((256, 768), BF16),
@@ -369,14 +386,14 @@
             shape((256, 1024), BF16),
             shape((512, 128), BF16),
             shape((512, 128), F32),
-            shape((1, 128), F32),
         ),
-        [pltpu.VMEM((512, 1024), F32), pltpu.VMEM((512, 1024), F32), pltpu.VMEM((512, 128), F32)],
+        [pltpu.VMEM((512, 1024), F32), pltpu.VMEM((512, 1024), F32)],
         own,
         other,
         lanes,
+        mask_spread(),
         weight,
-        cotangent.reshape(512, 128),
+        cot_rows,
     )
     got = lax.ppermute(send, DEVICES, swap)
     update, right_sum, weight_sum, left_sum = call(
@@ -392,17 +409,19 @@
         scaled,
         inverse,
         lanes,
+        order,
         weight,
         bias,
     )
     (parts,) = call(
         pack_kernel,
         (shape((128, 4, 640), BF16),),
-        [],
+        [pltpu.VMEM((256, 512), F32)],
         got,
         right_sum,
         weight_sum,
         left_sum,
+        order,
     )
     parts = exchange(parts)
     (sums,) = call(

time: 77.9 us -> 77.5 us (level)
    pallas_call x7 -> x8, Pallas kernels: 9.18 us -> 9.22 us  [call(): pl.pallas_call(kernel, out_shape=outs, in_specs=[pl.BlockSpec(memory_spac...]
  transfers between devices with their start and end apart: 6 -> 6, of which waited for: 4 -> 3; matrix products, arithmetic and copies ran while one was open for 0% -> 0% of each run, Pallas kernels for 3% -> 4%
where the time goes in v6:
time: 77.5 us; the launch traced here: 77.3 us
  blocking collectives  53.7 us (69%)
  starting transfers between devices  10.8 us (14%)
  Pallas kernels  9.22 us (12%)
  waiting for transfers between devices  2.74 us (4%)
    all_to_all x3, blocking collectives, exchange(): lax.all_to_all(block, DEVICES, 0, 0, axis_index_groups=groups, tiled=True)  53.7 us
    pallas_call x8, Pallas kernels, call(): pl.pallas_call(kernel, out_shape=outs, in_specs=[pl.BlockSpec(memory_spac...  9.22 us
    ppermute x1, starting transfers between devices, per_device(): lax.ppermute(left_block, DEVICES, turn)  4.49 us
    ppermute x1, starting transfers between devices, per_device(): other = lax.ppermute(own, DEVICES, swap)  2.35 us
  transfers between devices with their start and end apart: 6, of which 3 were waited for; matrix products, arithmetic and copies ran while one was open for 0% of the time, Pallas kernels for 4%

profile of v6, /device:TPU:1, one launch (start us, length us, event | category | flops | bytes accessed | tf_op | source)
XLA Modules:
  0.0 77.3 jit_solution(17681404534436503003)
XLA Ops:
  0.6 0.0 copy-start.6
  0.6 1.9 %shard_map.128 = (bf16[16,1152]{1,0:T(8,128)(2,1)}, bf16[16,1152]{1,0:T(8,128)(2,1)}) custom-call(bf16[512,32]{1,0:T(8,128)(2,1)} %bitcast.20, bf16[512,32]{1,0:T(8,128)(2,1)} %bitcast.21, s32[16,32]{1,0:T(8,128)} %mask_hbm.1), custom_call_target="tpu_custom_call" | custom-call | tf_op jit(solution)/shard_map/pallas_call | solution.py:313
  2.6 0.0 copy-start.5
  2.6 4.5 %collective-permute-start = (bf16[16,1152]{1,0:T(8,128)(2,1)}, bf16[16,1152]{1,0:T(8,128)(2,1)S(1)}, u32[]{:S(2)}, u32[]{:S(2)}) collective-permute-start(bf16[16,1152]{1,0:T(8,128)(2,1)} %get-tuple-element.30), channel_id=1, source_target_pairs={{0,4},{1,20},{2,36},{3,52},{4,68},{5,84},{6,100},{7,116},{8,12},{9... | collective-permute-start | bytes 110600 | tf_op jit(solution)/shard_map/ppermute | solution.py:358
  7.1 1.0 %collective-permute-start.2 = (bf16[16,1152]{1,0:T(8,128)(2,1)}, bf16[16,1152]{1,0:T(8,128)(2,1)S(1)}, u32[]{:S(2)}, u32[]{:S(2)}) collective-permute-start(bf16[16,1152]{1,0:T(8,128)(2,1)} %get-tuple-element.32), channel_id=1, source_target_pairs={{0,8},{1,9},{2,10},{3,11},{4,12},{5,13},{6,14},{7,15},{8,0},{9,1},... | collective-permute-start | bytes 110600 | tf_op jit(solution)/shard_map/ppermute | solution.py:359
  8.1 0.4 collective-permute-done
  8.5 0.0 copy-done.6
  8.5 1.5 %collective-permute-start.1 = (bf16[16,1152]{1,0:T(8,128)(2,1)S(1)}, bf16[16,1152]{1,0:T(8,128)(2,1)S(1)}, u32[]{:S(2)}, u32[]{:S(2)}) collective-permute-start(bf16[16,1152]{1,0:T(8,128)(2,1)S(1)} %collective-permute-done), channel_id=1, source_target_pairs={{0,8},{1,9},{2,10},{3,11},{4,12},{5,13},{6,14},{7,15},{8,0},{9,1},... | collective-permute-start | bytes 110600 | tf_op jit(solution)/shard_map/ppermute | solution.py:360
  10.0 0.0 collective-permute-done.2
  10.0 0.9 %collective-permute-done.1 = bf16[16,1152]{1,0:T(8,128)(2,1)S(1)} collective-permute-done((bf16[16,1152]{1,0:T(8,128)(2,1)S(1)}, bf16[16,1152]{1,0:T(8,128)(2,1)S(1)}, u32[]{:S(2)}, u32[]{:S(2)}) %collective-permute-start.1) | collective-permute-done | bytes 36896 | tf_op jit(solution)/shard_map/ppermute | solution.py:360
  10.9 0.0 copy-done.5
  10.9 0.0 copy-start.4
  11.0 0.0 copy-start
  11.0 0.0 copy-start.1
  11.0 0.0 copy-start.3
  11.0 17.2 %all_to_all.15 = bf16[8,2,16,1152]{3,2,1,0:T(8,128)(2,1)S(1)} all-to-all(bf16[8,2,16,1152]{3,2,1,0:T(8,128)(2,1)S(1)} %broadcast_in_dim.7), channel_id=1, replica_groups={{0,1,2,3,4,5,6,7},{16,17,18,19,20,21,22,23},{32,33,34,35,36,37,38,39},{..., dimensions={0} | all-to-all | bytes 1179648 | tf_op jit(solution)/shard_map/all_to_all | solution.py:339
  28.2 2.4 %collective-permute-start.3 = (bf16[256,1152]{1,0:T(8,128)(2,1)S(1)}, bf16[256,1152]{1,0:T(8,128)(2,1)S(1)}, u32[]{:S(2)}, u32[]{:S(2)}) collective-permute-start(bf16[256,1152]{1,0:T(8,128)(2,1)S(1)} %bitcast.14), channel_id=1, source_target_pairs={{0,8},{1,9},{2,10},{3,11},{4,12},{5,13},{6,14},{7,15},{8,0},{9,1},... | collective-permute-start | bytes 1769480 | tf_op jit(solution)/shard_map/ppermute | solution.py:367
  30.6 0.0 copy-done.4
  30.6 0.2 shard_map.129
  30.8 1.5 %collective-permute-done.3.other_ref = bf16[256,1152]{1,0:T(8,128)(2,1)S(1)} collective-permute-done((bf16[256,1152]{1,0:T(8,128)(2,1)S(1)}, bf16[256,1152]{1,0:T(8,128)(2,1)S(1)}, u32[]{:S(2)}, u32[]{:S(2)}) %collective-permute-start.3) | collective-permute-done | bytes 589856 | tf_op jit(solution)/shard_map/ppermute | solution.py:367
  32.2 2.7 %shard_map.130 = (bf16[256,768]{1,0:T(8,128)(2,1)S(1)}, bf16[512,1024]{1,0:T(8,128)(2,1)S(1)}, bf16[512,1024]{1,0:T(8,128)(2,1)S(1)}, bf16[256,512]{1,0:T(8,128)...) custom-call(bf16[256,1152]{1,0:T(8,128)(2,1)S(1)} %bitcast.15, ...), custom_call_target="tpu_custom_call" | custom-call | tf_op jit(solution)/shard_map/pallas_call | solution.py:313
  35.0 0.5 collective-permute-start.4
  35.5 1.5 %shard_map.131 = (f32[512,128]{1,0:T(8,128)S(1)}, f32[256,512]{1,0:T(8,128)S(1)}, f32[512,128]{1,0:T(8,128)S(1)}, f32[256,512]{1,0:T(8,128)S(1)}) custom-call(bf16[512,1024]{1,0:T(8,128)(2,1)S(1)} %get-tuple-element.37.x_ref, bf16[512,1024]{1,0:T(8,128)(2,1)S(1)} %get-tuple-element.38.dy_ref, bf16[256,512]{1,0:T(8,128)(2,1)S(1)} %get-tuple-element.39.left_in, ...), custom_call_target="tpu_custom_call" | custom-call | tf_op jit(solution)/shard_map/pallas_call | solution.py:313
  36.9 0.0 collective-permute-done.4.got_ref
  37.0 0.4 shard_map.132
  37.4 21.2 %all_to_all.16.in_ref = bf16[128,4,640]{2,1,0:T(4,128)(2,1)S(1)} all-to-all(bf16[128,4,640]{2,1,0:T(4,128)(2,1)S(1)} %shard_map.132), channel_id=1, replica_groups=mesh['seq'=16,'res'=8] {'seq','res'}, dimensions={0} | all-to-all | bytes 1310720 | tf_op jit(solution)/shard_map/all_to_all | solution.py:339
  58.6 0.2 shard_map.133
  58.9 15.2 %all_to_all.17.in_ref.own_ref = bf16[128,8,128]{2,1,0:T(8,128)(2,1)S(1)} all-to-all(bf16[128,8,128]{2,1,0:T(8,128)(2,1)S(1)} %shard_map.133), channel_id=1, replica_groups=mesh['seq'=16,'res'=8] {'seq','res'}, dimensions={0} | all-to-all | bytes 524288 | tf_op jit(solution)/shard_map/all_to_all | solution.py:339
  74.1 1.0 %collective-permute-start.5 = (bf16[128,8,128]{2,1,0:T(8,128)(2,1)S(1)}, bf16[128,8,128]{2,1,0:T(8,128)(2,1)S(1)}, u32[]{:S(2)}, u32[]{:S(2)}) collective-permute-start(bf16[128,8,128]{2,1,0:T(8,128)(2,1)S(1)} %all_to_all.17.in_ref.own_ref), channel_id=1, source_target_pairs={{0,8},{1,9},{2,10},{3,11},{4,12},{5,13},{6,14},{7,15},{8,0},{9,1},... | collective-permute-start | bytes 786440 | tf_op jit(solution)/shard_map/ppermute | solution.py:431
  75.1 1.4 %shard_map.134 = (bf16[512,128]{1,0:T(8,128)(2,1)}, f32[512,32]{1,0:T(8,128)}, f32[512,32]{1,0:T(8,128)}, f32[1,128]{1,0:T(1,128)}) custom-call(bf16[128,8,128]{2,1,0:T(8,128)(2,1)S(1)} %all_to_all.17.in_ref.own_ref, f32[512,128]{1,0:T(8,128)S(1)} %get-tuple-element.50.update_ref), custom_call_target="tpu_custom_call" | custom-call | tf_op jit(solution)/shard_map/pallas_call | solution.py:313
  76.4 0.0 collective-permute-done.5.other_ref
  76.5 0.8 %shard_map.135 = f32[1024,128]{1,0:T(8,128)} custom-call(bf16[128,8,128]{2,1,0:T(8,128)(2,1)S(1)} %all_to_all.17.in_ref.own_ref, bf16[128,8,128]{2,1,0:T(8,128)(2,1)S(1)} %collective-permute-done.5.other_ref), custom_call_target="tpu_custom_call" | custom-call | tf_op jit(solution)/shard_map/pallas_call | solution.py:313
  (8 shorter events, 0.1 us)
Async XLA Ops:
  0.6 7.8 %copy-start.6 = (f32[128]{0:T(128)S(1)}, f32[128]{0:T(128)}, u32[]{:S(2)}) copy-start(f32[128]{0:T(128)} %param.13) | copy-start | bytes 1540
  2.6 8.3 %copy-start.5 = (bf16[16,1152]{1,0:T(8,128)(2,1)S(1)}, bf16[16,1152]{1,0:T(8,128)(2,1)}, u32[]{:S(2)}) copy-start(bf16[16,1152]{1,0:T(8,128)(2,1)} %get-tuple-element.32) | copy-start | bytes 110596
  2.6 5.9 %collective-permute-start = (bf16[16,1152]{1,0:T(8,128)(2,1)}, bf16[16,1152]{1,0:T(8,128)(2,1)S(1)}, u32[]{:S(2)}, u32[]{:S(2)}) collective-permute-start(bf16[16,1152]{1,0:T(8,128)(2,1)} %get-tuple-element.30), channel_id=1, source_target_pairs={{0,4},{1,20},{2,36},{3,52},{4,68},{5,84},{6,100},{7,116},{8,12},{9... | collective-permute-start | bytes 110600 | tf_op jit(solution)/shard_map/ppermute | solution.py:358
  7.1 2.9 %collective-permute-start.2 = (bf16[16,1152]{1,0:T(8,128)(2,1)}, bf16[16,1152]{1,0:T(8,128)(2,1)S(1)}, u32[]{:S(2)}, u32[]{:S(2)}) collective-permute-start(bf16[16,1152]{1,0:T(8,128)(2,1)} %get-tuple-element.32), channel_id=1, source_target_pairs={{0,8},{1,9},{2,10},{3,11},{4,12},{5,13},{6,14},{7,15},{8,0},{9,1},... | collective-permute-start | bytes 110600 | tf_op jit(solution)/shard_map/ppermute | solution.py:359
  8.5 2.4 %collective-permute-start.1 = (bf16[16,1152]{1,0:T(8,128)(2,1)S(1)}, bf16[16,1152]{1,0:T(8,128)(2,1)S(1)}, u32[]{:S(2)}, u32[]{:S(2)}) collective-permute-start(bf16[16,1152]{1,0:T(8,128)(2,1)S(1)} %collective-permute-done), channel_id=1, source_target_pairs={{0,8},{1,9},{2,10},{3,11},{4,12},{5,13},{6,14},{7,15},{8,0},{9,1},... | collective-permute-start | bytes 110600 | tf_op jit(solution)/shard_map/ppermute | solution.py:360
  10.9 19.7 %copy-start.4 = (bf16[16,32,128]{2,1,0:T(8,128)(2,1)S(1)}, bf16[16,32,128]{2,1,0:T(8,128)(2,1)}, u32[]{:S(2)}) copy-start(bf16[16,32,128]{2,1,0:T(8,128)(2,1)} %param.14) | copy-start | bytes 393220
  11.0 21.3 %copy-start = (bf16[512,512]{1,0:T(8,128)(2,1)S(1)}, bf16[512,512]{1,0:T(8,128)(2,1)}, u32[]{:S(2)}) copy-start(bf16[512,512]{1,0:T(8,128)(2,1)} %constant.26.clone.lanes_ref) | copy-start | bytes 1572868
  11.0 21.3 %copy-start.1 = (bf16[32,32,128]{2,1,0:T(8,128)(2,1)S(1)}, bf16[32,32,128]{2,1,0:T(8,128)(2,1)}, u32[]{:S(2)}) copy-start(bf16[32,32,128]{2,1,0:T(8,128)(2,1)} %param.12) | copy-start | bytes 786436
  11.0 21.2 %copy-start.3 = (bf16[128,1536]{1,0:T(8,128)(2,1)S(1)}, bf16[128,1536]{1,0:T(8,128)(2,1)}, u32[]{:S(2)}) copy-start(bf16[128,1536]{1,0:T(8,128)(2,1)} %constant.28.clone.spread_ref) | copy-start | bytes 1179652
  28.2 4.0 %collective-permute-start.3 = (bf16[256,1152]{1,0:T(8,128)(2,1)S(1)}, bf16[256,1152]{1,0:T(8,128)(2,1)S(1)}, u32[]{:S(2)}, u32[]{:S(2)}) collective-permute-start(bf16[256,1152]{1,0:T(8,128)(2,1)S(1)} %bitcast.14), channel_id=1, source_target_pairs={{0,8},{1,9},{2,10},{3,11},{4,12},{5,13},{6,14},{7,15},{8,0},{9,1},... | collective-permute-start | bytes 1769480 | tf_op jit(solution)/shard_map/ppermute | solution.py:367
  32.2 3.2 %copy-start.2 = (bf16[256,256]{1,0:T(8,128)(2,1)S(1)}, bf16[256,256]{1,0:T(8,128)(2,1)}, u32[]{:S(2)}) copy-start(bf16[256,256]{1,0:T(8,128)(2,1)} %constant.27.clone.order_ref) | copy-start | bytes 393220
  35.0 2.0 %collective-permute-start.4 = (bf16[256,768]{1,0:T(8,128)(2,1)S(1)}, bf16[256,768]{1,0:T(8,128)(2,1)S(1)}, u32[]{:S(2)}, u32[]{:S(2)}) collective-permute-start(bf16[256,768]{1,0:T(8,128)(2,1)S(1)} %get-tuple-element.36), channel_id=1, source_target_pairs={{0,8},{1,9},{2,10},{3,11},{4,12},{5,13},{6,14},{7,15},{8,0},{9,1},... | collective-permute-start | bytes 1179656 | tf_op jit(solution)/shard_map/ppermute | solution.py:398
  74.1 2.4 %collective-permute-start.5 = (bf16[128,8,128]{2,1,0:T(8,128)(2,1)S(1)}, bf16[128,8,128]{2,1,0:T(8,128)(2,1)S(1)}, u32[]{:S(2)}, u32[]{:S(2)}) collective-permute-start(bf16[128,8,128]{2,1,0:T(8,128)(2,1)S(1)} %all_to_all.17.in_ref.own_ref), channel_id=1, source_target_pairs={{0,8},{1,9},{2,10},{3,11},{4,12},{5,13},{6,14},{7,15},{8,0},{9,1},... | collective-permute-start | bytes 786440 | tf_op jit(solution)/shard_map/ppermute | solution.py:431

commit v7 on v6

--- a/solution.py
+++ b/solution.py
@@ -72,27 +72,22 @@
     )
 
 
-def prep_kernel(
-    left_hbm, right_hbm, mask_hbm, left_out, right_out, left_ref, right_ref, mask_ref, wide_ref, sems
-):
-    copies = [
-        pltpu.make_async_copy(left_hbm, left_ref, sems.at[0]),
-        pltpu.make_async_copy(right_hbm, right_ref, sems.at[1]),
-        pltpu.make_async_copy(mask_hbm, mask_ref, sems.at[2]),
-    ]
+def prep_kernel(block_hbm, mask_hbm, out_ref, block_ref, mask_ref, wide_ref, sems):
+    copies = [pltpu.make_async_copy(mask_hbm, mask_ref, sems.at[4])]
+    for n in range(4):
+        part = slice(n * 128, n * 128 + 128)
+        copies.append(pltpu.make_async_copy(block_hbm.at[part], block_ref.at[part], sems.at[n]))
     for copy in copies:
         copy.start()
     for copy in copies:
         copy.wait()
+    wide_ref[...] = block_ref[...].astype(F32)
+    for k in range(8):
+        tile = [wide_ref[pl.ds(k * 4 + e, 16, stride=32), :] for e in range(4)]
+        out_ref[:, k * 128 : k * 128 + 128] = jnp.concatenate(tile, 1).astype(BF16)
     mask = mask_ref[...].astype(F32).astype(BF16)
     widen = choose(iota((32, 128), 0) == iota((32, 128), 1))
-    masks = jnp.dot(mask, widen, preferred_element_type=F32).astype(BF16)
-    for n, (ref, out_ref) in enumerate(((left_ref, left_out), (right_ref, right_out))):
-        wide_ref[n] = ref[...].astype(F32)
-        for k in range(8):
-            tile = [wide_ref[n, pl.ds(k * 4 + e, 16, stride=32), :] for e in range(4)]
-            out_ref[:, k * 128 : k * 128 + 128] = jnp.concatenate(tile, 1).astype(BF16)
-        out_ref[:, 1024:1152] = masks
+    out_ref[:, 1024:1152] = jnp.dot(mask, widen, preferred_element_type=F32).astype(BF16)
 
 
 def cotangent_kernel(cot_ref, rows_ref, bsum_ref, cot32_ref):
@@ -338,22 +333,24 @@
     def exchange(block, groups=None):
         return lax.all_to_all(block, DEVICES, 0, 0, axis_index_groups=groups, tiled=True)
 
-    left_block, right_block = call(
-        prep_kernel,
-        (shape((16, 1152), BF16), shape((16, 1152), BF16)),
-        [
-            pltpu.VMEM((512, 32), BF16),
-            pltpu.VMEM((512, 32), BF16),
-            pltpu.VMEM((16, 32), jnp.int32),
-            pltpu.VMEM((2, 512, 32), F32),
-            pltpu.SemaphoreType.DMA((3,)),
-        ],
-        left.reshape(512, 32),
-        right.reshape(512, 32),
-        mask,
-        space=pltpu.HBM,
-        mib=60,
-    )
+    def prepared(block):
+        (block,) = call(
+            prep_kernel,
+            (shape((16, 1152), BF16),),
+            [
+                pltpu.VMEM((512, 32), BF16),
+                pltpu.VMEM((16, 32), jnp.int32),
+                pltpu.VMEM((512, 32), F32),
+                pltpu.SemaphoreType.DMA((5,)),
+            ],
+            block.reshape(512, 32),
+            mask,
+            space=pltpu.HBM,
+            mib=60,
+        )
+        return block
+
+    left_block, right_block = prepared(left), prepared(right)
     bias = jnp.broadcast_to(bias, (8, 128))
     left_block, bias = lax.optimization_barrier((lax.ppermute(left_block, DEVICES, turn), bias))
     other_right = lax.ppermute(right_block, DEVICES, swap)

time: 77.5 us -> 77.4 us (level)
  Pallas kernels: 9.22 us -> 10.7 us
  starting transfers between devices: 10.8 us -> 9.48 us
    pallas_call x8 -> x9, Pallas kernels: 9.22 us -> 10.7 us  [call(): pl.pallas_call(kernel, out_shape=outs, in_specs=[pl.BlockSpec(memory_spac...]
    ppermute x1, starting transfers between devices: 1.53 us -> 0.16 us  [per_device(): other_left = lax.ppermute(left_block, DEVICES, swap)]
    ppermute x1, waiting for transfers between devices: 0.01 us -> 0.91 us  [per_device(): other_right = lax.ppermute(right_block, DEVICES, swap)]
  transfers between devices with their start and end apart: 6 -> 6, of which waited for: 3 -> 3; matrix products, arithmetic and copies ran while one was open for 0% -> 0% of each run, Pallas kernels for 4% -> 6%
where the time goes in v7:
time: 77.4 us; the launch traced here: 77 us
  blocking collectives  53.4 us (69%)
  Pallas kernels  10.7 us (14%)
  starting transfers between devices  9.48 us (12%)
  waiting for transfers between devices  2.59 us (3%)
    all_to_all x3, blocking collectives, exchange(): lax.all_to_all(block, DEVICES, 0, 0, axis_index_groups=groups, tiled=True)  53.4 us
    pallas_call x9, Pallas kernels, call(): pl.pallas_call(kernel, out_shape=outs, in_specs=[pl.BlockSpec(memory_spac...  10.7 us
    ppermute x1, starting transfers between devices, per_device(): lax.ppermute(left_block, DEVICES, turn)  4.49 us
    ppermute x1, starting transfers between devices, per_device(): other = lax.ppermute(own, DEVICES, swap)  2.35 us
  transfers between devices with their start and end apart: 6, of which 3 were waited for; matrix products, arithmetic and copies ran while one was open for 0% of the time, Pallas kernels for 6%

profile of v7, /device:TPU:1, one launch (start us, length us, event | category | flops | bytes accessed | tf_op | source)
XLA Modules:
  0.0 77.0 jit_solution(12866079087022601336)
XLA Ops:
  0.6 1.7 %shard_map.128 = bf16[16,1152]{1,0:T(8,128)(2,1)} custom-call(bf16[512,32]{1,0:T(8,128)(2,1)} %bitcast.21, s32[16,32]{1,0:T(8,128)} %mask_hbm.3), custom_call_target="tpu_custom_call" | custom-call | tf_op jit(solution)/shard_map/pallas_call | solution.py:308
  2.3 4.5 %collective-permute-start = (bf16[16,1152]{1,0:T(8,128)(2,1)}, bf16[16,1152]{1,0:T(8,128)(2,1)S(1)}, u32[]{:S(2)}, u32[]{:S(2)}) collective-permute-start(bf16[16,1152]{1,0:T(8,128)(2,1)} %shard_map.128), channel_id=1, source_target_pairs={{0,4},{1,20},{2,36},{3,52},{4,68},{5,84},{6,100},{7,116},{8,12},{9... | collective-permute-start | bytes 110600 | tf_op jit(solution)/shard_map/ppermute | solution.py:355
  6.8 1.7 %shard_map.129 = bf16[16,1152]{1,0:T(8,128)(2,1)} custom-call(bf16[512,32]{1,0:T(8,128)(2,1)} %bitcast.22, s32[16,32]{1,0:T(8,128)} %mask_hbm.3), custom_call_target="tpu_custom_call" | custom-call | tf_op jit(solution)/shard_map/pallas_call | solution.py:308
  8.5 0.0 copy-start.5
  8.5 1.0 %collective-permute-start.2 = (bf16[16,1152]{1,0:T(8,128)(2,1)}, bf16[16,1152]{1,0:T(8,128)(2,1)S(1)}, u32[]{:S(2)}, u32[]{:S(2)}) collective-permute-start(bf16[16,1152]{1,0:T(8,128)(2,1)} %shard_map.129), channel_id=1, source_target_pairs={{0,8},{1,9},{2,10},{3,11},{4,12},{5,13},{6,14},{7,15},{8,0},{9,1},... | collective-permute-start | bytes 110600 | tf_op jit(solution)/shard_map/ppermute | solution.py:356
  9.6 0.0 collective-permute-done
  9.6 0.2 collective-permute-start.1
  9.7 0.9 %collective-permute-done.2 = bf16[16,1152]{1,0:T(8,128)(2,1)S(1)} collective-permute-done((bf16[16,1152]{1,0:T(8,128)(2,1)}, bf16[16,1152]{1,0:T(8,128)(2,1)S(1)}, u32[]{:S(2)}, u32[]{:S(2)}) %collective-permute-start.2) | collective-permute-done | bytes 36896 | tf_op jit(solution)/shard_map/ppermute | solution.py:356
  10.6 0.2 collective-permute-done.1
  10.9 0.0 copy-done.5
  10.9 0.0 copy-start.4
  10.9 0.0 copy-start
  11.0 0.0 copy-start.1
  11.0 0.0 copy-start.3
  11.0 17.0 %all_to_all.15 = bf16[8,2,16,1152]{3,2,1,0:T(8,128)(2,1)S(1)} all-to-all(bf16[8,2,16,1152]{3,2,1,0:T(8,128)(2,1)S(1)} %broadcast_in_dim.7), channel_id=1, replica_groups={{0,1,2,3,4,5,6,7},{16,17,18,19,20,21,22,23},{32,33,34,35,36,37,38,39},{..., dimensions={0} | all-to-all | bytes 1179648 | tf_op jit(solution)/shard_map/all_to_all | solution.py:334
  28.0 2.4 %collective-permute-start.3 = (bf16[256,1152]{1,0:T(8,128)(2,1)S(1)}, bf16[256,1152]{1,0:T(8,128)(2,1)S(1)}, u32[]{:S(2)}, u32[]{:S(2)}) collective-permute-start(bf16[256,1152]{1,0:T(8,128)(2,1)S(1)} %bitcast.14), channel_id=1, source_target_pairs={{0,8},{1,9},{2,10},{3,11},{4,12},{5,13},{6,14},{7,15},{8,0},{9,1},... | collective-permute-start | bytes 1769480 | tf_op jit(solution)/shard_map/ppermute | solution.py:364
  30.3 0.2 shard_map.130
  30.5 1.5 %collective-permute-done.3.other_ref = bf16[256,1152]{1,0:T(8,128)(2,1)S(1)} collective-permute-done((bf16[256,1152]{1,0:T(8,128)(2,1)S(1)}, bf16[256,1152]{1,0:T(8,128)(2,1)S(1)}, u32[]{:S(2)}, u32[]{:S(2)}) %collective-permute-start.3) | collective-permute-done | bytes 589856 | tf_op jit(solution)/shard_map/ppermute | solution.py:364
  32.0 0.0 copy-done.3
  32.0 2.7 %shard_map.131 = (bf16[256,768]{1,0:T(8,128)(2,1)S(1)}, bf16[512,1024]{1,0:T(8,128)(2,1)S(1)}, bf16[512,1024]{1,0:T(8,128)(2,1)S(1)}, bf16[256,512]{1,0:T(8,128)...) custom-call(bf16[256,1152]{1,0:T(8,128)(2,1)S(1)} %bitcast.15, ...), custom_call_target="tpu_custom_call" | custom-call | tf_op jit(solution)/shard_map/pallas_call | solution.py:308
  34.7 0.5 collective-permute-start.4
  35.2 0.0 copy-done.2
  35.2 1.5 %shard_map.132 = (f32[512,128]{1,0:T(8,128)S(1)}, f32[256,512]{1,0:T(8,128)S(1)}, f32[512,128]{1,0:T(8,128)S(1)}, f32[256,512]{1,0:T(8,128)S(1)}) custom-call(bf16[512,1024]{1,0:T(8,128)(2,1)S(1)} %get-tuple-element.33.x_ref, bf16[512,1024]{1,0:T(8,128)(2,1)S(1)} %get-tuple-element.34.dy_ref, bf16[256,512]{1,0:T(8,128)(2,1)S(1)} %get-tuple-element.35.left_in, ...), custom_call_target="tpu_custom_call" | custom-call | tf_op jit(solution)/shard_map/pallas_call | solution.py:308
  36.7 0.0 collective-permute-done.4.got_ref
  36.7 0.4 shard_map.133
  37.1 21.2 %all_to_all.16.in_ref = bf16[128,4,640]{2,1,0:T(4,128)(2,1)S(1)} all-to-all(bf16[128,4,640]{2,1,0:T(4,128)(2,1)S(1)} %shard_map.133), channel_id=1, replica_groups=mesh['seq'=16,'res'=8] {'seq','res'}, dimensions={0} | all-to-all | bytes 1310720 | tf_op jit(solution)/shard_map/all_to_all | solution.py:334
  58.3 0.2 shard_map.134
  58.6 15.2 %all_to_all.17.in_ref.own_ref = bf16[128,8,128]{2,1,0:T(8,128)(2,1)S(1)} all-to-all(bf16[128,8,128]{2,1,0:T(8,128)(2,1)S(1)} %shard_map.134), channel_id=1, replica_groups=mesh['seq'=16,'res'=8] {'seq','res'}, dimensions={0} | all-to-all | bytes 524288 | tf_op jit(solution)/shard_map/all_to_all | solution.py:334
  73.8 1.0 %collective-permute-start.5 = (bf16[128,8,128]{2,1,0:T(8,128)(2,1)S(1)}, bf16[128,8,128]{2,1,0:T(8,128)(2,1)S(1)}, u32[]{:S(2)}, u32[]{:S(2)}) collective-permute-start(bf16[128,8,128]{2,1,0:T(8,128)(2,1)S(1)} %all_to_all.17.in_ref.own_ref), channel_id=1, source_target_pairs={{0,8},{1,9},{2,10},{3,11},{4,12},{5,13},{6,14},{7,15},{8,0},{9,1},... | collective-permute-start | bytes 786440 | tf_op jit(solution)/shard_map/ppermute | solution.py:428
  74.8 1.4 %shard_map.135 = (bf16[512,128]{1,0:T(8,128)(2,1)}, f32[512,32]{1,0:T(8,128)}, f32[512,32]{1,0:T(8,128)}, f32[1,128]{1,0:T(1,128)}) custom-call(bf16[128,8,128]{2,1,0:T(8,128)(2,1)S(1)} %all_to_all.17.in_ref.own_ref, f32[512,128]{1,0:T(8,128)S(1)} %get-tuple-element.46.update_ref), custom_call_target="tpu_custom_call" | custom-call | tf_op jit(solution)/shard_map/pallas_call | solution.py:308
  76.2 0.0 collective-permute-done.5.other_ref
  76.2 0.8 %shard_map.136 = f32[1024,128]{1,0:T(8,128)} custom-call(bf16[128,8,128]{2,1,0:T(8,128)(2,1)S(1)} %all_to_all.17.in_ref.own_ref, bf16[128,8,128]{2,1,0:T(8,128)(2,1)S(1)} %collective-permute-done.5.other_ref), custom_call_target="tpu_custom_call" | custom-call | tf_op jit(solution)/shard_map/pallas_call | solution.py:308
  (9 shorter events, 0.1 us)
Async XLA Ops:
  2.3 7.2 %collective-permute-start = (bf16[16,1152]{1,0:T(8,128)(2,1)}, bf16[16,1152]{1,0:T(8,128)(2,1)S(1)}, u32[]{:S(2)}, u32[]{:S(2)}) collective-permute-start(bf16[16,1152]{1,0:T(8,128)(2,1)} %shard_map.128), channel_id=1, source_target_pairs={{0,4},{1,20},{2,36},{3,52},{4,68},{5,84},{6,100},{7,116},{8,12},{9... | collective-permute-start | bytes 110600 | tf_op jit(solution)/shard_map/ppermute | solution.py:355
  6.8 2.8 %copy-start.6 = (f32[128]{0:T(128)S(1)}, f32[128]{0:T(128)}, u32[]{:S(2)}) copy-start(f32[128]{0:T(128)} %param.13) | copy-start | bytes 1540
  8.5 2.3 %copy-start.5 = (bf16[16,1152]{1,0:T(8,128)(2,1)S(1)}, bf16[16,1152]{1,0:T(8,128)(2,1)}, u32[]{:S(2)}) copy-start(bf16[16,1152]{1,0:T(8,128)(2,1)} %shard_map.129) | copy-start | bytes 110596
  8.5 2.1 %collective-permute-start.2 = (bf16[16,1152]{1,0:T(8,128)(2,1)}, bf16[16,1152]{1,0:T(8,128)(2,1)S(1)}, u32[]{:S(2)}, u32[]{:S(2)}) collective-permute-start(bf16[16,1152]{1,0:T(8,128)(2,1)} %shard_map.129), channel_id=1, source_target_pairs={{0,8},{1,9},{2,10},{3,11},{4,12},{5,13},{6,14},{7,15},{8,0},{9,1},... | collective-permute-start | bytes 110600 | tf_op jit(solution)/shard_map/ppermute | solution.py:356
  9.6 1.3 %collective-permute-start.1 = (bf16[16,1152]{1,0:T(8,128)(2,1)S(1)}, bf16[16,1152]{1,0:T(8,128)(2,1)S(1)}, u32[]{:S(2)}, u32[]{:S(2)}) collective-permute-start(bf16[16,1152]{1,0:T(8,128)(2,1)S(1)} %collective-permute-done), channel_id=1, source_target_pairs={{0,8},{1,9},{2,10},{3,11},{4,12},{5,13},{6,14},{7,15},{8,0},{9,1},... | collective-permute-start | bytes 110600 | tf_op jit(solution)/shard_map/ppermute | solution.py:357
  10.9 19.4 %copy-start.4 = (bf16[16,32,128]{2,1,0:T(8,128)(2,1)S(1)}, bf16[16,32,128]{2,1,0:T(8,128)(2,1)}, u32[]{:S(2)}) copy-start(bf16[16,32,128]{2,1,0:T(8,128)(2,1)} %param.14) | copy-start | bytes 393220
  10.9 21.0 %copy-start = (bf16[512,512]{1,0:T(8,128)(2,1)S(1)}, bf16[512,512]{1,0:T(8,128)(2,1)}, u32[]{:S(2)}) copy-start(bf16[512,512]{1,0:T(8,128)(2,1)} %constant.26.clone.lanes_ref) | copy-start | bytes 1572868
  11.0 21.0 %copy-start.1 = (bf16[32,32,128]{2,1,0:T(8,128)(2,1)S(1)}, bf16[32,32,128]{2,1,0:T(8,128)(2,1)}, u32[]{:S(2)}) copy-start(bf16[32,32,128]{2,1,0:T(8,128)(2,1)} %param.12) | copy-start | bytes 786436
  11.0 21.0 %copy-start.3 = (bf16[128,1536]{1,0:T(8,128)(2,1)S(1)}, bf16[128,1536]{1,0:T(8,128)(2,1)}, u32[]{:S(2)}) copy-start(bf16[128,1536]{1,0:T(8,128)(2,1)} %constant.28.clone.spread_ref) | copy-start | bytes 1179652
  28.0 4.0 %collective-permute-start.3 = (bf16[256,1152]{1,0:T(8,128)(2,1)S(1)}, bf16[256,1152]{1,0:T(8,128)(2,1)S(1)}, u32[]{:S(2)}, u32[]{:S(2)}) collective-permute-start(bf16[256,1152]{1,0:T(8,128)(2,1)S(1)} %bitcast.14), channel_id=1, source_target_pairs={{0,8},{1,9},{2,10},{3,11},{4,12},{5,13},{6,14},{7,15},{8,0},{9,1},... | collective-permute-start | bytes 1769480 | tf_op jit(solution)/shard_map/ppermute | solution.py:364
  32.0 3.2 %copy-start.2 = (bf16[256,256]{1,0:T(8,128)(2,1)S(1)}, bf16[256,256]{1,0:T(8,128)(2,1)}, u32[]{:S(2)}) copy-start(bf16[256,256]{1,0:T(8,128)(2,1)} %constant.27.clone.order_ref) | copy-start | bytes 393220
  34.7 2.0 %collective-permute-start.4 = (bf16[256,768]{1,0:T(8,128)(2,1)S(1)}, bf16[256,768]{1,0:T(8,128)(2,1)S(1)}, u32[]{:S(2)}, u32[]{:S(2)}) collective-permute-start(bf16[256,768]{1,0:T(8,128)(2,1)S(1)} %get-tuple-element.32), channel_id=1, source_target_pairs={{0,8},{1,9},{2,10},{3,11},{4,12},{5,13},{6,14},{7,15},{8,0},{9,1},... | collective-permute-start | bytes 1179656 | tf_op jit(solution)/shard_map/ppermute | solution.py:395
  73.8 2.4 %collective-permute-start.5 = (bf16[128,8,128]{2,1,0:T(8,128)(2,1)S(1)}, bf16[128,8,128]{2,1,0:T(8,128)(2,1)S(1)}, u32[]{:S(2)}, u32[]{:S(2)}) collective-permute-start(bf16[128,8,128]{2,1,0:T(8,128)(2,1)S(1)} %all_to_all.17.in_ref.own_ref), channel_id=1, source_target_pairs={{0,8},{1,9},{2,10},{3,11},{4,12},{5,13},{6,14},{7,15},{8,0},{9,1},... | collective-permute-start | bytes 786440 | tf_op jit(solution)/shard_map/ppermute | solution.py:428

commit v8 on v7

--- a/solution.py
+++ b/solution.py
@@ -47,14 +47,16 @@
 
 def row_order():
     row = np.arange(256)
-    return jnp.asarray((row % 16 * 16 + row // 16)[:, None] == row[None, :], BF16)
+    source = row % 2 * 128 + row % 16 // 2 * 16 + row // 16
+    return jnp.asarray(source[:, None] == row[None, :], BF16)
 
 
 def mask_spread():
     lane = np.arange(512)
     pairs = 4 * (lane // 16 % 8) + lane // 128
     lanes = np.concatenate([pairs, np.arange(1024) // 32])
-    return jnp.asarray(np.arange(128)[:, None] == lanes[None, :], BF16)
+    source = np.arange(128)[None, :, None] - 32 * np.arange(2)[:, None, None]
+    return jnp.asarray(source == lanes[None, None, :], BF16)
 
 
 def core_index():
@@ -86,7 +88,7 @@
         tile = [wide_ref[pl.ds(k * 4 + e, 16, stride=32), :] for e in range(4)]
         out_ref[:, k * 128 : k * 128 + 128] = jnp.concatenate(tile, 1).astype(BF16)
     mask = mask_ref[...].astype(F32).astype(BF16)
-    widen = choose(iota((32, 128), 0) == iota((32, 128), 1))
+    widen = choose(iota((32, 128), 0) + 32 * core_index() == iota((32, 128), 1))
     out_ref[:, 1024:1152] = jnp.dot(mask, widen, preferred_element_type=F32).astype(BF16)
 
 
@@ -112,21 +114,24 @@
         return jnp.where(core == (0 if of_left else 1), own_ref[:, lanes], other_ref[:, lanes])
 
     def turned(block):
-        return jnp.concatenate([block[128:256], block[0:128]], 0)
-
-    masks = turned(rows(slice(1024, 1152), True))
-    left = turned(rows(pl.ds(keep, 512), True))
+        return jnp.concatenate([block[64:128], block[0:64]], 0)
+
+    left = jnp.concatenate([turned(rows(pl.ds(n * 1024 + keep, 512), True)) for n in range(2)], 0)
     left = jnp.dot(left, lanes_ref[...], preferred_element_type=F32).astype(BF16)
-    right = rows(slice(0, 1152), False)
-    spread_i = choose(iota((128, 512), 0) == core * 16 + iota((128, 512), 1) % 16)
-    masks_j = right[:, 1024:1152]
-    mask_i = jnp.dot(masks, spread_i, preferred_element_type=F32)
-    mask_j = jnp.dot(masks_j, spread_ref[:, 0:512], preferred_element_type=F32)
-    mask_jd = jnp.dot(masks_j, spread_ref[:, 512:1536], preferred_element_type=F32)
+    right = jnp.concatenate([rows(slice(n * 1024, n * 1024 + 1024), False) for n in range(2)], 0)
+    masks, masks_j = turned(rows(slice(2048, 2176), True)), rows(slice(2048, 2176), False)
+    lane = iota((128, 512), 1) % 16 + core * 16
+
+    def spread(block, tables):
+        return jnp.concatenate([jnp.dot(block, table, preferred_element_type=F32) for table in tables], 0)
+
+    mask_i = spread(masks, [choose(iota((128, 512), 0) == lane + 32 * n) for n in range(2)])
+    mask_j = spread(masks_j, [spread_ref[n, :, 0:512] for n in range(2)])
+    mask_jd = spread(masks_j, [spread_ref[n, :, 512:1536] for n in range(2)])
     mask_i_ref[...] = mask_i.astype(BF16)
     mask_jd_ref[...] = mask_jd.astype(BF16)
     left = left * mask_i_ref[...]
-    right = right[:, 0:1024] * mask_jd_ref[...]
+    right = right * mask_jd_ref[...]
     left_ref[...] = left
     right_ref[...] = right
     both = (mask_i * mask_j).astype(BF16)
@@ -355,11 +360,11 @@
     left_block, bias = lax.optimization_barrier((lax.ppermute(left_block, DEVICES, turn), bias))
     other_right = lax.ppermute(right_block, DEVICES, swap)
     other_left = lax.ppermute(left_block, DEVICES, swap)
-    block = jnp.where(
-        core_index() == 0, jnp.stack([left_block, other_left]), jnp.stack([other_right, right_block])
-    )
-    block = jnp.broadcast_to(block, (8, 2, 16, 1152))
-    own = exchange(block, groups).reshape(256, 1152)
+    first = core_index() == 0
+    near = jnp.where(first, left_block, other_right)
+    far = jnp.where(first, other_left, right_block)
+    block = jnp.concatenate([near[:, :1024], far[:, :1024], near[:, 1024:] + far[:, 1024:]], 1)
+    own = exchange(jnp.broadcast_to(block, (8, 16, 2176)), groups).reshape(128, 2176)
     own, cotangent = lax.optimization_barrier((own, cotangent))
     other = lax.ppermute(own, DEVICES, swap)
     cot_rows, bias_part = call(

time: 77.4 us -> 77.2 us (level)
  no operation moved by 1% of the time
where the time goes in v8:
time: 77.2 us; the launch traced here: 76.7 us
  blocking collectives  52.7 us (68%)
  Pallas kernels  10.7 us (14%)
  starting transfers between devices  9.16 us (12%)
  waiting for transfers between devices  2.56 us (3%)
  between operations  0.79 us (1%)
    all_to_all x3, blocking collectives, exchange(): lax.all_to_all(block, DEVICES, 0, 0, axis_index_groups=groups, tiled=True)  52.7 us
    pallas_call x9, Pallas kernels, call(): pl.pallas_call(kernel, out_shape=outs, in_specs=[pl.BlockSpec(memory_spac...  10.7 us
    ppermute x1, starting transfers between devices, per_device(): lax.ppermute(left_block, DEVICES, turn)  4.49 us
    ppermute x1, starting transfers between devices, per_device(): other = lax.ppermute(own, DEVICES, swap)  2.18 us
  transfers between devices with their start and end apart: 6, of which 3 were waited for; matrix products, arithmetic and copies ran while one was open for 0% of the time, Pallas kernels for 6%

profile of v8, /device:TPU:1, one launch (start us, length us, event | category | flops | bytes accessed | tf_op | source)
XLA Modules:
  0.0 76.7 jit_solution(686647510561553386)
XLA Ops:
  0.6 1.7 %shard_map.128 = bf16[16,1152]{1,0:T(8,128)(2,1)} custom-call(bf16[512,32]{1,0:T(8,128)(2,1)} %bitcast.16, s32[16,32]{1,0:T(8,128)} %mask_hbm.3), custom_call_target="tpu_custom_call" | custom-call | tf_op jit(solution)/shard_map/pallas_call | solution.py:313
  2.3 4.5 %collective-permute-start = (bf16[16,1152]{1,0:T(8,128)(2,1)}, bf16[16,1152]{1,0:T(8,128)(2,1)S(1)}, u32[]{:S(2)}, u32[]{:S(2)}) collective-permute-start(bf16[16,1152]{1,0:T(8,128)(2,1)} %shard_map.128), channel_id=1, source_target_pairs={{0,4},{1,20},{2,36},{3,52},{4,68},{5,84},{6,100},{7,116},{8,12},{9... | collective-permute-start | bytes 110600 | tf_op jit(solution)/shard_map/ppermute | solution.py:360
  6.8 1.7 %shard_map.129 = bf16[16,1152]{1,0:T(8,128)(2,1)} custom-call(bf16[512,32]{1,0:T(8,128)(2,1)} %bitcast.17, s32[16,32]{1,0:T(8,128)} %mask_hbm.3), custom_call_target="tpu_custom_call" | custom-call | tf_op jit(solution)/shard_map/pallas_call | solution.py:313
  8.5 1.0 %collective-permute-start.1 = (bf16[16,1152]{1,0:T(8,128)(2,1)}, bf16[16,1152]{1,0:T(8,128)(2,1)S(1)}, u32[]{:S(2)}, u32[]{:S(2)}) collective-permute-start(bf16[16,1152]{1,0:T(8,128)(2,1)} %shard_map.129), channel_id=1, source_target_pairs={{0,8},{1,9},{2,10},{3,11},{4,12},{5,13},{6,14},{7,15},{8,0},{9,1},... | collective-permute-start | bytes 110600 | tf_op jit(solution)/shard_map/ppermute | solution.py:361
  9.5 0.0 collective-permute-done
  9.5 0.7 copy-done.6
  10.2 0.0 collective-permute-start.2
  10.2 0.4 collective-permute-done.1
  10.6 0.0 copy-start.5
  10.6 0.8 collective-permute-done.2
  11.4 0.0 copy-done.5
  11.5 0.0 copy-start.2
  11.5 0.0 copy-start.4
  11.5 0.0 copy-start
  11.5 0.0 copy-start.1
  11.6 16.4 %all_to_all.15 = bf16[8,16,2176]{2,1,0:T(8,128)(2,1)S(1)} all-to-all(bf16[8,16,2176]{2,1,0:T(8,128)(2,1)S(1)} %broadcast_in_dim.7), channel_id=1, replica_groups={{0,1,2,3,4,5,6,7},{16,17,18,19,20,21,22,23},{32,33,34,35,36,37,38,39},{..., dimensions={0} | all-to-all | bytes 1114112 | tf_op jit(solution)/shard_map/all_to_all | solution.py:339
  27.9 2.2 %collective-permute-start.3 = (bf16[128,2176]{1,0:T(8,128)(2,1)S(1)}, bf16[128,2176]{1,0:T(8,128)(2,1)S(1)}, u32[]{:S(2)}, u32[]{:S(2)}) collective-permute-start(bf16[128,2176]{1,0:T(8,128)(2,1)S(1)} %bitcast.10), channel_id=1, source_target_pairs={{0,8},{1,9},{2,10},{3,11},{4,12},{5,13},{6,14},{7,15},{8,0},{9,1},... | collective-permute-start | bytes 1671176 | tf_op jit(solution)/shard_map/ppermute | solution.py:369
  30.1 0.0 copy-done.4
  30.1 0.2 shard_map.130
  30.3 1.4 %collective-permute-done.3.other_ref = bf16[128,2176]{1,0:T(8,128)(2,1)S(1)} collective-permute-done((bf16[128,2176]{1,0:T(8,128)(2,1)S(1)}, bf16[128,2176]{1,0:T(8,128)(2,1)S(1)}, u32[]{:S(2)}, u32[]{:S(2)}) %collective-permute-start.3) | collective-permute-done | bytes 557088 | tf_op jit(solution)/shard_map/ppermute | solution.py:369
  31.7 2.8 %shard_map.131 = (bf16[256,768]{1,0:T(8,128)(2,1)S(1)}, bf16[512,1024]{1,0:T(8,128)(2,1)S(1)}, bf16[512,1024]{1,0:T(8,128)(2,1)S(1)}, bf16[256,512]{1,0:T(8,128)...) custom-call(bf16[128,2176]{1,0:T(8,128)(2,1)S(1)} %bitcast.11, ...), custom_call_target="tpu_custom_call" | custom-call | tf_op jit(solution)/shard_map/pallas_call | solution.py:313
  34.5 0.5 collective-permute-start.4
  35.0 1.5 %shard_map.132 = (f32[512,128]{1,0:T(8,128)S(1)}, f32[256,512]{1,0:T(8,128)S(1)}, f32[512,128]{1,0:T(8,128)S(1)}, f32[256,512]{1,0:T(8,128)S(1)}) custom-call(bf16[512,1024]{1,0:T(8,128)(2,1)S(1)} %get-tuple-element.33.x_ref, bf16[512,1024]{1,0:T(8,128)(2,1)S(1)} %get-tuple-element.34.dy_ref, bf16[256,512]{1,0:T(8,128)(2,1)S(1)} %get-tuple-element.35.left_in, ...), custom_call_target="tpu_custom_call" | custom-call | tf_op jit(solution)/shard_map/pallas_call | solution.py:313
  36.5 0.0 collective-permute-done.4.got_ref
  36.5 0.4 shard_map.133
  36.9 21.1 %all_to_all.16.in_ref = bf16[128,4,640]{2,1,0:T(4,128)(2,1)S(1)} all-to-all(bf16[128,4,640]{2,1,0:T(4,128)(2,1)S(1)} %shard_map.133), channel_id=1, replica_groups=mesh['seq'=16,'res'=8] {'seq','res'}, dimensions={0} | all-to-all | bytes 1310720 | tf_op jit(solution)/shard_map/all_to_all | solution.py:339
  58.1 0.2 shard_map.134
  58.3 15.2 %all_to_all.17.in_ref.own_ref = bf16[128,8,128]{2,1,0:T(8,128)(2,1)S(1)} all-to-all(bf16[128,8,128]{2,1,0:T(8,128)(2,1)S(1)} %shard_map.134), channel_id=1, replica_groups=mesh['seq'=16,'res'=8] {'seq','res'}, dimensions={0} | all-to-all | bytes 524288 | tf_op jit(solution)/shard_map/all_to_all | solution.py:339
  73.5 1.0 %collective-permute-start.5 = (bf16[128,8,128]{2,1,0:T(8,128)(2,1)S(1)}, bf16[128,8,128]{2,1,0:T(8,128)(2,1)S(1)}, u32[]{:S(2)}, u32[]{:S(2)}) collective-permute-start(bf16[128,8,128]{2,1,0:T(8,128)(2,1)S(1)} %all_to_all.17.in_ref.own_ref), channel_id=1, source_target_pairs={{0,8},{1,9},{2,10},{3,11},{4,12},{5,13},{6,14},{7,15},{8,0},{9,1},... | collective-permute-start | bytes 786440 | tf_op jit(solution)/shard_map/ppermute | solution.py:433
  74.5 1.4 %shard_map.135 = (bf16[512,128]{1,0:T(8,128)(2,1)}, f32[512,32]{1,0:T(8,128)}, f32[512,32]{1,0:T(8,128)}, f32[1,128]{1,0:T(1,128)}) custom-call(bf16[128,8,128]{2,1,0:T(8,128)(2,1)S(1)} %all_to_all.17.in_ref.own_ref, f32[512,128]{1,0:T(8,128)S(1)} %get-tuple-element.46.update_ref), custom_call_target="tpu_custom_call" | custom-call | tf_op jit(solution)/shard_map/pallas_call | solution.py:313
  75.9 0.0 collective-permute-done.5.other_ref
  75.9 0.8 %shard_map.136 = f32[1024,128]{1,0:T(8,128)} custom-call(bf16[128,8,128]{2,1,0:T(8,128)(2,1)S(1)} %all_to_all.17.in_ref.own_ref, bf16[128,8,128]{2,1,0:T(8,128)(2,1)S(1)} %collective-permute-done.5.other_ref), custom_call_target="tpu_custom_call" | custom-call | tf_op jit(solution)/shard_map/pallas_call | solution.py:313
  (14 shorter events, 0.1 us)
Async XLA Ops:
  2.3 7.2 %collective-permute-start = (bf16[16,1152]{1,0:T(8,128)(2,1)}, bf16[16,1152]{1,0:T(8,128)(2,1)S(1)}, u32[]{:S(2)}, u32[]{:S(2)}) collective-permute-start(bf16[16,1152]{1,0:T(8,128)(2,1)} %shard_map.128), channel_id=1, source_target_pairs={{0,4},{1,20},{2,36},{3,52},{4,68},{5,84},{6,100},{7,116},{8,12},{9... | collective-permute-start | bytes 110600 | tf_op jit(solution)/shard_map/ppermute | solution.py:360
  8.5 2.1 %collective-permute-start.1 = (bf16[16,1152]{1,0:T(8,128)(2,1)}, bf16[16,1152]{1,0:T(8,128)(2,1)S(1)}, u32[]{:S(2)}, u32[]{:S(2)}) collective-permute-start(bf16[16,1152]{1,0:T(8,128)(2,1)} %shard_map.129), channel_id=1, source_target_pairs={{0,8},{1,9},{2,10},{3,11},{4,12},{5,13},{6,14},{7,15},{8,0},{9,1},... | collective-permute-start | bytes 110600 | tf_op jit(solution)/shard_map/ppermute | solution.py:361
  9.5 0.7 copy-start.6
  10.2 1.2 %collective-permute-start.2 = (bf16[16,1152]{1,0:T(8,128)(2,1)S(1)}, bf16[16,1152]{1,0:T(8,128)(2,1)S(1)}, u32[]{:S(2)}, u32[]{:S(2)}) collective-permute-start(bf16[16,1152]{1,0:T(8,128)(2,1)S(1)} %collective-permute-done), channel_id=1, source_target_pairs={{0,8},{1,9},{2,10},{3,11},{4,12},{5,13},{6,14},{7,15},{8,0},{9,1},... | collective-permute-start | bytes 110600 | tf_op jit(solution)/shard_map/ppermute | solution.py:362
  10.6 0.8 %copy-start.5 = (bf16[16,1152]{1,0:T(8,128)(2,1)S(1)}, bf16[16,1152]{1,0:T(8,128)(2,1)}, u32[]{:S(2)}) copy-start(bf16[16,1152]{1,0:T(8,128)(2,1)} %shard_map.129) | copy-start | bytes 110596
  11.5 20.2 %copy-start.2 = (bf16[2,128,1536]{2,1,0:T(8,128)(2,1)S(1)}, bf16[2,128,1536]{2,1,0:T(8,128)(2,1)}, u32[]{:S(2)}) copy-start(bf16[2,128,1536]{2,1,0:T(8,128)(2,1)} %constant.28.clone.spread_ref) | copy-start | bytes 2359300
  11.5 18.6 %copy-start.4 = (bf16[16,32,128]{2,1,0:T(8,128)(2,1)S(1)}, bf16[16,32,128]{2,1,0:T(8,128)(2,1)}, u32[]{:S(2)}) copy-start(bf16[16,32,128]{2,1,0:T(8,128)(2,1)} %param.14) | copy-start | bytes 393220
  11.5 20.2 %copy-start = (bf16[512,512]{1,0:T(8,128)(2,1)S(1)}, bf16[512,512]{1,0:T(8,128)(2,1)}, u32[]{:S(2)}) copy-start(bf16[512,512]{1,0:T(8,128)(2,1)} %constant.26.clone.lanes_ref) | copy-start | bytes 1572868
  11.5 20.2 %copy-start.1 = (bf16[32,32,128]{2,1,0:T(8,128)(2,1)S(1)}, bf16[32,32,128]{2,1,0:T(8,128)(2,1)}, u32[]{:S(2)}) copy-start(bf16[32,32,128]{2,1,0:T(8,128)(2,1)} %param.12) | copy-start | bytes 786436
  27.9 3.8 %collective-permute-start.3 = (bf16[128,2176]{1,0:T(8,128)(2,1)S(1)}, bf16[128,2176]{1,0:T(8,128)(2,1)S(1)}, u32[]{:S(2)}, u32[]{:S(2)}) collective-permute-start(bf16[128,2176]{1,0:T(8,128)(2,1)S(1)} %bitcast.10), channel_id=1, source_target_pairs={{0,8},{1,9},{2,10},{3,11},{4,12},{5,13},{6,14},{7,15},{8,0},{9,1},... | collective-permute-start | bytes 1671176 | tf_op jit(solution)/shard_map/ppermute | solution.py:369
  31.7 3.3 %copy-start.3 = (bf16[256,256]{1,0:T(8,128)(2,1)S(1)}, bf16[256,256]{1,0:T(8,128)(2,1)}, u32[]{:S(2)}) copy-start(bf16[256,256]{1,0:T(8,128)(2,1)} %constant.27.clone.order_ref) | copy-start | bytes 393220
  34.5 2.0 %collective-permute-start.4 = (bf16[256,768]{1,0:T(8,128)(2,1)S(1)}, bf16[256,768]{1,0:T(8,128)(2,1)S(1)}, u32[]{:S(2)}, u32[]{:S(2)}) collective-permute-start(bf16[256,768]{1,0:T(8,128)(2,1)S(1)} %get-tuple-element.32), channel_id=1, source_target_pairs={{0,8},{1,9},{2,10},{3,11},{4,12},{5,13},{6,14},{7,15},{8,0},{9,1},... | collective-permute-start | bytes 1179656 | tf_op jit(solution)/shard_map/ppermute | solution.py:400
  73.5 2.4 %collective-permute-start.5 = (bf16[128,8,128]{2,1,0:T(8,128)(2,1)S(1)}, bf16[128,8,128]{2,1,0:T(8,128)(2,1)S(1)}, u32[]{:S(2)}, u32[]{:S(2)}) collective-permute-start(bf16[128,8,128]{2,1,0:T(8,128)(2,1)S(1)} %all_to_all.17.in_ref.own_ref), channel_id=1, source_target_pairs={{0,8},{1,9},{2,10},{3,11},{4,12},{5,13},{6,14},{7,15},{8,0},{9,1},... | collective-permute-start | bytes 786440 | tf_op jit(solution)/shard_map/ppermute | solution.py:433

commit v9 on v8

--- a/solution.py
+++ b/solution.py
@@ -143,6 +143,7 @@
     scaled = (cot_ref[...] * inverse).astype(BF16)
     scaled_ref[...] = scaled
 
+    dx_ref[...] = lax.dot_general(scaled, w_ref[...], LANES_LANES, preferred_element_type=F32)
     y_ref[...] = lax.dot_general(left, right, ROWS_ROWS, preferred_element_type=F32)
     for u in range(8):
         lanes = slice(u * 128, u * 128 + 128)
@@ -152,7 +153,10 @@
                 at = (e * 8 + u) * 16
                 x_ref[at : at + 16, t * 128 : t * 128 + 128] = tiles[e].astype(BF16)
 
-    dx_ref[...] = lax.dot_general(scaled, w_ref[...], LANES_LANES, preferred_element_type=F32)
+    part = weight_part(give, x_ref, scaled).astype(BF16)
+    send_ref[:, 512:640] = part[0:256]
+    send_ref[:, 640:768] = part[256:512]
+
     for u in range(8):
         lanes = slice(u * 128, u * 128 + 128)
         for t in range(8):
@@ -164,9 +168,6 @@
 
     part = right_part(give, left, dy_ref, mask_jd_ref).astype(BF16)
     send_ref[:, 0:512] = part
-    part = weight_part(give, x_ref, scaled).astype(BF16)
-    send_ref[:, 512:640] = part[0:256]
-    send_ref[:, 640:768] = part[256:512]
 
 
 def right_part(half, left, dy_ref, mask_ref):
@@ -257,9 +258,9 @@
         out_ref[m] = jnp.where(mine, rows, base[(m // 8) % 2]).astype(BF16)
 
 
-def weight_rows(ref, out_ref):
+def weight_rows(ref, out_ref, side):
     upper_rows = iota((8, 128), 0) >= 4
-    for p in range(64):
+    for p in range(side * 32, side * 32 + 32):
         even, odd = ref[p * 2].astype(F32), ref[p * 2 + 1].astype(F32)
         out_ref[p * 8 : p * 8 + 8, :] = jnp.where(upper_rows, pltpu.roll(odd, 4, 0), even)
 
@@ -301,10 +302,12 @@
     core = core_index()
     copies = []
     for n, (ref, half) in enumerate(((own_ref, core), (other_ref, 1 - core))):
-        weight_rows(ref, rows_ref.at[n])
-        at = pl.ds(pl.multiple_of(half * 512, 512), 512)
-        copies.append(pltpu.make_async_copy(rows_ref.at[n], out_hbm.at[at], sems.at[n]))
-        copies[n].start()
+        for side in range(2):
+            weight_rows(ref, rows_ref.at[n], side)
+            at = pl.ds(pl.multiple_of(half * 512 + side * 256, 256), 256)
+            part = rows_ref.at[n, side * 256 : side * 256 + 256]
+            copies.append(pltpu.make_async_copy(part, out_hbm.at[at], sems.at[n * 2 + side]))
+            copies[-1].start()
     for copy in copies:
         copy.wait()
 
@@ -441,7 +444,7 @@
     (weight_grad,) = call(
         weight_kernel,
         (shape((1024, 128), F32),),
-        [pltpu.VMEM((2, 512, 128), F32), pltpu.SemaphoreType.DMA((2,))],
+        [pltpu.VMEM((2, 512, 128), F32), pltpu.SemaphoreType.DMA((4,))],
         sums,
         other_sums,
         out_space=pltpu.HBM,

time: 77.2 us -> 77.1 us (level)
  no operation moved by 1% of the time
where the time goes in v9:
time: 77.1 us; the launch traced here: 76.7 us
  blocking collectives  52.7 us (68%)
  Pallas kernels  10.7 us (14%)
  starting transfers between devices  9.17 us (12%)
  waiting for transfers between devices  2.56 us (3%)
  between operations  0.79 us (1%)
    all_to_all x3, blocking collectives, exchange(): lax.all_to_all(block, DEVICES, 0, 0, axis_index_groups=groups, tiled=True)  52.7 us
    pallas_call x9, Pallas kernels, call(): pl.pallas_call(kernel, out_shape=outs, in_specs=[pl.BlockSpec(memory_spac...  10.7 us
    ppermute x1, starting transfers between devices, per_device(): lax.ppermute(left_block, DEVICES, turn)  4.49 us
    ppermute x1, starting transfers between devices, per_device(): other = lax.ppermute(own, DEVICES, swap)  2.18 us
  transfers between devices with their start and end apart: 6, of which 3 were waited for; matrix products, arithmetic and copies ran while one was open for 0% of the time, Pallas kernels for 6%

profile of v9, /device:TPU:1, one launch (start us, length us, event | category | flops | bytes accessed | tf_op | source)
XLA Modules:
  0.0 76.7 jit_solution(18239451351335567766)
XLA Ops:
  0.6 1.7 %shard_map.128 = bf16[16,1152]{1,0:T(8,128)(2,1)} custom-call(bf16[512,32]{1,0:T(8,128)(2,1)} %bitcast.16, s32[16,32]{1,0:T(8,128)} %mask_hbm.3), custom_call_target="tpu_custom_call" | custom-call | tf_op jit(solution)/shard_map/pallas_call | solution.py:316
  2.3 4.5 %collective-permute-start = (bf16[16,1152]{1,0:T(8,128)(2,1)}, bf16[16,1152]{1,0:T(8,128)(2,1)S(1)}, u32[]{:S(2)}, u32[]{:S(2)}) collective-permute-start(bf16[16,1152]{1,0:T(8,128)(2,1)} %shard_map.128), channel_id=1, source_target_pairs={{0,4},{1,20},{2,36},{3,52},{4,68},{5,84},{6,100},{7,116},{8,12},{9... | collective-permute-start | bytes 110600 | tf_op jit(solution)/shard_map/ppermute | solution.py:363
  6.8 1.7 %shard_map.129 = bf16[16,1152]{1,0:T(8,128)(2,1)} custom-call(bf16[512,32]{1,0:T(8,128)(2,1)} %bitcast.17, s32[16,32]{1,0:T(8,128)} %mask_hbm.3), custom_call_target="tpu_custom_call" | custom-call | tf_op jit(solution)/shard_map/pallas_call | solution.py:316
  8.5 1.0 %collective-permute-start.1 = (bf16[16,1152]{1,0:T(8,128)(2,1)}, bf16[16,1152]{1,0:T(8,128)(2,1)S(1)}, u32[]{:S(2)}, u32[]{:S(2)}) collective-permute-start(bf16[16,1152]{1,0:T(8,128)(2,1)} %shard_map.129), channel_id=1, source_target_pairs={{0,8},{1,9},{2,10},{3,11},{4,12},{5,13},{6,14},{7,15},{8,0},{9,1},... | collective-permute-start | bytes 110600 | tf_op jit(solution)/shard_map/ppermute | solution.py:364
  9.5 0.0 collective-permute-done
  9.5 0.7 copy-done.6
  10.2 0.0 collective-permute-start.2
  10.2 0.4 collective-permute-done.1
  10.6 0.0 copy-start.5
  10.6 0.8 collective-permute-done.2
  11.4 0.0 copy-done.5
  11.5 0.0 copy-start.2
  11.5 0.0 copy-start.4
  11.5 0.0 copy-start
  11.5 0.0 copy-start.1
  11.6 16.4 %all_to_all.15 = bf16[8,16,2176]{2,1,0:T(8,128)(2,1)S(1)} all-to-all(bf16[8,16,2176]{2,1,0:T(8,128)(2,1)S(1)} %broadcast_in_dim.7), channel_id=1, replica_groups={{0,1,2,3,4,5,6,7},{16,17,18,19,20,21,22,23},{32,33,34,35,36,37,38,39},{..., dimensions={0} | all-to-all | bytes 1114112 | tf_op jit(solution)/shard_map/all_to_all | solution.py:342
  27.9 2.2 %collective-permute-start.3 = (bf16[128,2176]{1,0:T(8,128)(2,1)S(1)}, bf16[128,2176]{1,0:T(8,128)(2,1)S(1)}, u32[]{:S(2)}, u32[]{:S(2)}) collective-permute-start(bf16[128,2176]{1,0:T(8,128)(2,1)S(1)} %bitcast.10), channel_id=1, source_target_pairs={{0,8},{1,9},{2,10},{3,11},{4,12},{5,13},{6,14},{7,15},{8,0},{9,1},... | collective-permute-start | bytes 1671176 | tf_op jit(solution)/shard_map/ppermute | solution.py:372
  30.1 0.0 copy-done.4
  30.1 0.2 shard_map.130
  30.3 1.4 %collective-permute-done.3.other_ref = bf16[128,2176]{1,0:T(8,128)(2,1)S(1)} collective-permute-done((bf16[128,2176]{1,0:T(8,128)(2,1)S(1)}, bf16[128,2176]{1,0:T(8,128)(2,1)S(1)}, u32[]{:S(2)}, u32[]{:S(2)}) %collective-permute-start.3) | collective-permute-done | bytes 557088 | tf_op jit(solution)/shard_map/ppermute | solution.py:372
  31.7 2.8 %shard_map.131 = (bf16[256,768]{1,0:T(8,128)(2,1)S(1)}, bf16[512,1024]{1,0:T(8,128)(2,1)S(1)}, bf16[512,1024]{1,0:T(8,128)(2,1)S(1)}, bf16[256,512]{1,0:T(8,128)...) custom-call(bf16[128,2176]{1,0:T(8,128)(2,1)S(1)} %bitcast.11, ...), custom_call_target="tpu_custom_call" | custom-call | tf_op jit(solution)/shard_map/pallas_call | solution.py:316
  34.5 0.5 collective-permute-start.4
  34.9 1.5 %shard_map.132 = (f32[512,128]{1,0:T(8,128)S(1)}, f32[256,512]{1,0:T(8,128)S(1)}, f32[512,128]{1,0:T(8,128)S(1)}, f32[256,512]{1,0:T(8,128)S(1)}) custom-call(bf16[512,1024]{1,0:T(8,128)(2,1)S(1)} %get-tuple-element.33.x_ref, bf16[512,1024]{1,0:T(8,128)(2,1)S(1)} %get-tuple-element.34.dy_ref, bf16[256,512]{1,0:T(8,128)(2,1)S(1)} %get-tuple-element.35.left_in, ...), custom_call_target="tpu_custom_call" | custom-call | tf_op jit(solution)/shard_map/pallas_call | solution.py:316
  36.5 0.0 collective-permute-done.4.got_ref
  36.5 0.4 shard_map.133
  36.9 21.1 %all_to_all.16.in_ref = bf16[128,4,640]{2,1,0:T(4,128)(2,1)S(1)} all-to-all(bf16[128,4,640]{2,1,0:T(4,128)(2,1)S(1)} %shard_map.133), channel_id=1, replica_groups=mesh['seq'=16,'res'=8] {'seq','res'}, dimensions={0} | all-to-all | bytes 1310720 | tf_op jit(solution)/shard_map/all_to_all | solution.py:342
  58.0 0.2 shard_map.134
  58.3 15.2 %all_to_all.17.in_ref.own_ref = bf16[128,8,128]{2,1,0:T(8,128)(2,1)S(1)} all-to-all(bf16[128,8,128]{2,1,0:T(8,128)(2,1)S(1)} %shard_map.134), channel_id=1, replica_groups=mesh['seq'=16,'res'=8] {'seq','res'}, dimensions={0} | all-to-all | bytes 524288 | tf_op jit(solution)/shard_map/all_to_all | solution.py:342
  73.5 1.0 %collective-permute-start.5 = (bf16[128,8,128]{2,1,0:T(8,128)(2,1)S(1)}, bf16[128,8,128]{2,1,0:T(8,128)(2,1)S(1)}, u32[]{:S(2)}, u32[]{:S(2)}) collective-permute-start(bf16[128,8,128]{2,1,0:T(8,128)(2,1)S(1)} %all_to_all.17.in_ref.own_ref), channel_id=1, source_target_pairs={{0,8},{1,9},{2,10},{3,11},{4,12},{5,13},{6,14},{7,15},{8,0},{9,1},... | collective-permute-start | bytes 786440 | tf_op jit(solution)/shard_map/ppermute | solution.py:436
  74.5 1.4 %shard_map.135 = (bf16[512,128]{1,0:T(8,128)(2,1)}, f32[512,32]{1,0:T(8,128)}, f32[512,32]{1,0:T(8,128)}, f32[1,128]{1,0:T(1,128)}) custom-call(bf16[128,8,128]{2,1,0:T(8,128)(2,1)S(1)} %all_to_all.17.in_ref.own_ref, f32[512,128]{1,0:T(8,128)S(1)} %get-tuple-element.46.update_ref), custom_call_target="tpu_custom_call" | custom-call | tf_op jit(solution)/shard_map/pallas_call | solution.py:316
  75.9 0.0 collective-permute-done.5.other_ref
  75.9 0.8 %shard_map.136 = f32[1024,128]{1,0:T(8,128)} custom-call(bf16[128,8,128]{2,1,0:T(8,128)(2,1)S(1)} %all_to_all.17.in_ref.own_ref, bf16[128,8,128]{2,1,0:T(8,128)(2,1)S(1)} %collective-permute-done.5.other_ref), custom_call_target="tpu_custom_call" | custom-call | tf_op jit(solution)/shard_map/pallas_call | solution.py:316
  (14 shorter events, 0.1 us)
Async XLA Ops:
  2.3 7.2 %collective-permute-start = (bf16[16,1152]{1,0:T(8,128)(2,1)}, bf16[16,1152]{1,0:T(8,128)(2,1)S(1)}, u32[]{:S(2)}, u32[]{:S(2)}) collective-permute-start(bf16[16,1152]{1,0:T(8,128)(2,1)} %shard_map.128), channel_id=1, source_target_pairs={{0,4},{1,20},{2,36},{3,52},{4,68},{5,84},{6,100},{7,116},{8,12},{9... | collective-permute-start | bytes 110600 | tf_op jit(solution)/shard_map/ppermute | solution.py:363
  8.5 2.1 %collective-permute-start.1 = (bf16[16,1152]{1,0:T(8,128)(2,1)}, bf16[16,1152]{1,0:T(8,128)(2,1)S(1)}, u32[]{:S(2)}, u32[]{:S(2)}) collective-permute-start(bf16[16,1152]{1,0:T(8,128)(2,1)} %shard_map.129), channel_id=1, source_target_pairs={{0,8},{1,9},{2,10},{3,11},{4,12},{5,13},{6,14},{7,15},{8,0},{9,1},... | collective-permute-start | bytes 110600 | tf_op jit(solution)/shard_map/ppermute | solution.py:364
  9.5 0.7 copy-start.6
  10.2 1.2 %collective-permute-start.2 = (bf16[16,1152]{1,0:T(8,128)(2,1)S(1)}, bf16[16,1152]{1,0:T(8,128)(2,1)S(1)}, u32[]{:S(2)}, u32[]{:S(2)}) collective-permute-start(bf16[16,1152]{1,0:T(8,128)(2,1)S(1)} %collective-permute-done), channel_id=1, source_target_pairs={{0,8},{1,9},{2,10},{3,11},{4,12},{5,13},{6,14},{7,15},{8,0},{9,1},... | collective-permute-start | bytes 110600 | tf_op jit(solution)/shard_map/ppermute | solution.py:365
  10.6 0.8 %copy-start.5 = (bf16[16,1152]{1,0:T(8,128)(2,1)S(1)}, bf16[16,1152]{1,0:T(8,128)(2,1)}, u32[]{:S(2)}) copy-start(bf16[16,1152]{1,0:T(8,128)(2,1)} %shard_map.129) | copy-start | bytes 110596
  11.5 20.2 %copy-start.2 = (bf16[2,128,1536]{2,1,0:T(8,128)(2,1)S(1)}, bf16[2,128,1536]{2,1,0:T(8,128)(2,1)}, u32[]{:S(2)}) copy-start(bf16[2,128,1536]{2,1,0:T(8,128)(2,1)} %constant.28.clone.spread_ref) | copy-start | bytes 2359300
  11.5 18.6 %copy-start.4 = (bf16[16,32,128]{2,1,0:T(8,128)(2,1)S(1)}, bf16[16,32,128]{2,1,0:T(8,128)(2,1)}, u32[]{:S(2)}) copy-start(bf16[16,32,128]{2,1,0:T(8,128)(2,1)} %param.14) | copy-start | bytes 393220
  11.5 20.2 %copy-start = (bf16[512,512]{1,0:T(8,128)(2,1)S(1)}, bf16[512,512]{1,0:T(8,128)(2,1)}, u32[]{:S(2)}) copy-start(bf16[512,512]{1,0:T(8,128)(2,1)} %constant.26.clone.lanes_ref) | copy-start | bytes 1572868
  11.5 20.2 %copy-start.1 = (bf16[32,32,128]{2,1,0:T(8,128)(2,1)S(1)}, bf16[32,32,128]{2,1,0:T(8,128)(2,1)}, u32[]{:S(2)}) copy-start(bf16[32,32,128]{2,1,0:T(8,128)(2,1)} %param.12) | copy-start | bytes 786436
  27.9 3.8 %collective-permute-start.3 = (bf16[128,2176]{1,0:T(8,128)(2,1)S(1)}, bf16[128,2176]{1,0:T(8,128)(2,1)S(1)}, u32[]{:S(2)}, u32[]{:S(2)}) collective-permute-start(bf16[128,2176]{1,0:T(8,128)(2,1)S(1)} %bitcast.10), channel_id=1, source_target_pairs={{0,8},{1,9},{2,10},{3,11},{4,12},{5,13},{6,14},{7,15},{8,0},{9,1},... | collective-permute-start | bytes 1671176 | tf_op jit(solution)/shard_map/ppermute | solution.py:372
  31.7 3.2 %copy-start.3 = (bf16[256,256]{1,0:T(8,128)(2,1)S(1)}, bf16[256,256]{1,0:T(8,128)(2,1)}, u32[]{:S(2)}) copy-start(bf16[256,256]{1,0:T(8,128)(2,1)} %constant.27.clone.order_ref) | copy-start | bytes 393220
  34.5 2.0 %collective-permute-start.4 = (bf16[256,768]{1,0:T(8,128)(2,1)S(1)}, bf16[256,768]{1,0:T(8,128)(2,1)S(1)}, u32[]{:S(2)}, u32[]{:S(2)}) collective-permute-start(bf16[256,768]{1,0:T(8,128)(2,1)S(1)} %get-tuple-element.32), channel_id=1, source_target_pairs={{0,8},{1,9},{2,10},{3,11},{4,12},{5,13},{6,14},{7,15},{8,0},{9,1},... | collective-permute-start | bytes 1179656 | tf_op jit(solution)/shard_map/ppermute | solution.py:403
  73.5 2.4 %collective-permute-start.5 = (bf16[128,8,128]{2,1,0:T(8,128)(2,1)S(1)}, bf16[128,8,128]{2,1,0:T(8,128)(2,1)S(1)}, u32[]{:S(2)}, u32[]{:S(2)}) collective-permute-start(bf16[128,8,128]{2,1,0:T(8,128)(2,1)S(1)} %all_to_all.17.in_ref.own_ref), channel_id=1, source_target_pairs={{0,8},{1,9},{2,10},{3,11},{4,12},{5,13},{6,14},{7,15},{8,0},{9,1},... | collective-permute-start | bytes 786440 | tf_op jit(solution)/shard_map/ppermute | solution.py:436

commit v10 on v9

--- a/solution.py
+++ b/solution.py
@@ -198,12 +198,12 @@
 def pack_kernel(got_ref, right_ref, weight_ref, left_ref, order_ref, msg_ref, sum_ref):
     lower = low()
     upper_rows = iota((8, 128), 0) >= 4
-    total = (right_ref[...] + got_ref[:, 0:512].astype(F32)).astype(BF16)
-    sum_ref[...] = jnp.dot(order_ref[...], total, preferred_element_type=F32)
-    for s in range(16):
-        for k in range(4):
+    for k in range(4):
+        lanes = slice(k * 128, k * 128 + 128)
+        total = (right_ref[:, lanes] + got_ref[:, lanes].astype(F32)).astype(BF16)
+        sum_ref[:, lanes] = jnp.dot(order_ref[...], total, preferred_element_type=F32)
+        for s in range(16):
             m = s * 8 + k * 2
-            lanes = slice(k * 128, k * 128 + 128)
             tiles = []
             for ref in (sum_ref, left_ref):
                 block = ref[s * 16 : s * 16 + 16, lanes]

time: 77.1 us -> 77.1 us (level)
  no operation moved by 1% of the time
where the time goes in v10:
time: 77.1 us; the launch traced here: 76.7 us
  blocking collectives  52.7 us (68%)
  Pallas kernels  10.7 us (14%)
  starting transfers between devices  9.17 us (12%)
  waiting for transfers between devices  2.56 us (3%)
  between operations  0.79 us (1%)
    all_to_all x3, blocking collectives, exchange(): lax.all_to_all(block, DEVICES, 0, 0, axis_index_groups=groups, tiled=True)  52.7 us
    pallas_call x9, Pallas kernels, call(): pl.pallas_call(kernel, out_shape=outs, in_specs=[pl.BlockSpec(memory_spac...  10.7 us
    ppermute x1, starting transfers between devices, per_device(): lax.ppermute(left_block, DEVICES, turn)  4.49 us
    ppermute x1, starting transfers between devices, per_device(): other = lax.ppermute(own, DEVICES, swap)  2.18 us
  transfers between devices with their start and end apart: 6, of which 3 were waited for; matrix products, arithmetic and copies ran while one was open for 0% of the time, Pallas kernels for 6%

profile of v10, /device:TPU:1, one launch (start us, length us, event | category | flops | bytes accessed | tf_op | source)
XLA Modules:
  0.0 76.7 jit_solution(4598482136892291895)
XLA Ops:
  0.6 1.7 %shard_map.128 = bf16[16,1152]{1,0:T(8,128)(2,1)} custom-call(bf16[512,32]{1,0:T(8,128)(2,1)} %bitcast.16, s32[16,32]{1,0:T(8,128)} %mask_hbm.3), custom_call_target="tpu_custom_call" | custom-call | tf_op jit(solution)/shard_map/pallas_call | solution.py:316
  2.3 4.5 %collective-permute-start = (bf16[16,1152]{1,0:T(8,128)(2,1)}, bf16[16,1152]{1,0:T(8,128)(2,1)S(1)}, u32[]{:S(2)}, u32[]{:S(2)}) collective-permute-start(bf16[16,1152]{1,0:T(8,128)(2,1)} %shard_map.128), channel_id=1, source_target_pairs={{0,4},{1,20},{2,36},{3,52},{4,68},{5,84},{6,100},{7,116},{8,12},{9... | collective-permute-start | bytes 110600 | tf_op jit(solution)/shard_map/ppermute | solution.py:363
  6.8 1.7 %shard_map.129 = bf16[16,1152]{1,0:T(8,128)(2,1)} custom-call(bf16[512,32]{1,0:T(8,128)(2,1)} %bitcast.17, s32[16,32]{1,0:T(8,128)} %mask_hbm.3), custom_call_target="tpu_custom_call" | custom-call | tf_op jit(solution)/shard_map/pallas_call | solution.py:316
  8.5 1.0 %collective-permute-start.1 = (bf16[16,1152]{1,0:T(8,128)(2,1)}, bf16[16,1152]{1,0:T(8,128)(2,1)S(1)}, u32[]{:S(2)}, u32[]{:S(2)}) collective-permute-start(bf16[16,1152]{1,0:T(8,128)(2,1)} %shard_map.129), channel_id=1, source_target_pairs={{0,8},{1,9},{2,10},{3,11},{4,12},{5,13},{6,14},{7,15},{8,0},{9,1},... | collective-permute-start | bytes 110600 | tf_op jit(solution)/shard_map/ppermute | solution.py:364
  9.5 0.0 collective-permute-done
  9.5 0.7 copy-done.6
  10.2 0.0 collective-permute-start.2
  10.2 0.4 collective-permute-done.1
  10.6 0.0 copy-start.5
  10.6 0.8 collective-permute-done.2
  11.4 0.0 copy-done.5
  11.5 0.0 copy-start.2
  11.5 0.0 copy-start.4
  11.5 0.0 copy-start
  11.5 0.0 copy-start.1
  11.6 16.4 %all_to_all.15 = bf16[8,16,2176]{2,1,0:T(8,128)(2,1)S(1)} all-to-all(bf16[8,16,2176]{2,1,0:T(8,128)(2,1)S(1)} %broadcast_in_dim.7), channel_id=1, replica_groups={{0,1,2,3,4,5,6,7},{16,17,18,19,20,21,22,23},{32,33,34,35,36,37,38,39},{..., dimensions={0} | all-to-all | bytes 1114112 | tf_op jit(solution)/shard_map/all_to_all | solution.py:342
  27.9 2.2 %collective-permute-start.3 = (bf16[128,2176]{1,0:T(8,128)(2,1)S(1)}, bf16[128,2176]{1,0:T(8,128)(2,1)S(1)}, u32[]{:S(2)}, u32[]{:S(2)}) collective-permute-start(bf16[128,2176]{1,0:T(8,128)(2,1)S(1)} %bitcast.10), channel_id=1, source_target_pairs={{0,8},{1,9},{2,10},{3,11},{4,12},{5,13},{6,14},{7,15},{8,0},{9,1},... | collective-permute-start | bytes 1671176 | tf_op jit(solution)/shard_map/ppermute | solution.py:372
  30.1 0.0 copy-done.4
  30.1 0.2 shard_map.130
  30.3 1.4 %collective-permute-done.3.other_ref = bf16[128,2176]{1,0:T(8,128)(2,1)S(1)} collective-permute-done((bf16[128,2176]{1,0:T(8,128)(2,1)S(1)}, bf16[128,2176]{1,0:T(8,128)(2,1)S(1)}, u32[]{:S(2)}, u32[]{:S(2)}) %collective-permute-start.3) | collective-permute-done | bytes 557088 | tf_op jit(solution)/shard_map/ppermute | solution.py:372
  31.7 2.8 %shard_map.131 = (bf16[256,768]{1,0:T(8,128)(2,1)S(1)}, bf16[512,1024]{1,0:T(8,128)(2,1)S(1)}, bf16[512,1024]{1,0:T(8,128)(2,1)S(1)}, bf16[256,512]{1,0:T(8,128)...) custom-call(bf16[128,2176]{1,0:T(8,128)(2,1)S(1)} %bitcast.11, ...), custom_call_target="tpu_custom_call" | custom-call | tf_op jit(solution)/shard_map/pallas_call | solution.py:316
  34.5 0.5 collective-permute-start.4
  34.9 1.5 %shard_map.132 = (f32[512,128]{1,0:T(8,128)S(1)}, f32[256,512]{1,0:T(8,128)S(1)}, f32[512,128]{1,0:T(8,128)S(1)}, f32[256,512]{1,0:T(8,128)S(1)}) custom-call(bf16[512,1024]{1,0:T(8,128)(2,1)S(1)} %get-tuple-element.33.x_ref, bf16[512,1024]{1,0:T(8,128)(2,1)S(1)} %get-tuple-element.34.dy_ref, bf16[256,512]{1,0:T(8,128)(2,1)S(1)} %get-tuple-element.35.left_in, ...), custom_call_target="tpu_custom_call" | custom-call | tf_op jit(solution)/shard_map/pallas_call | solution.py:316
  36.5 0.0 collective-permute-done.4.got_ref
  36.5 0.4 shard_map.133
  36.9 21.1 %all_to_all.16.in_ref = bf16[128,4,640]{2,1,0:T(4,128)(2,1)S(1)} all-to-all(bf16[128,4,640]{2,1,0:T(4,128)(2,1)S(1)} %shard_map.133), channel_id=1, replica_groups=mesh['seq'=16,'res'=8] {'seq','res'}, dimensions={0} | all-to-all | bytes 1310720 | tf_op jit(solution)/shard_map/all_to_all | solution.py:342
  58.0 0.2 shard_map.134
  58.3 15.2 %all_to_all.17.in_ref.own_ref = bf16[128,8,128]{2,1,0:T(8,128)(2,1)S(1)} all-to-all(bf16[128,8,128]{2,1,0:T(8,128)(2,1)S(1)} %shard_map.134), channel_id=1, replica_groups=mesh['seq'=16,'res'=8] {'seq','res'}, dimensions={0} | all-to-all | bytes 524288 | tf_op jit(solution)/shard_map/all_to_all | solution.py:342
  73.5 1.0 %collective-permute-start.5 = (bf16[128,8,128]{2,1,0:T(8,128)(2,1)S(1)}, bf16[128,8,128]{2,1,0:T(8,128)(2,1)S(1)}, u32[]{:S(2)}, u32[]{:S(2)}) collective-permute-start(bf16[128,8,128]{2,1,0:T(8,128)(2,1)S(1)} %all_to_all.17.in_ref.own_ref), channel_id=1, source_target_pairs={{0,8},{1,9},{2,10},{3,11},{4,12},{5,13},{6,14},{7,15},{8,0},{9,1},... | collective-permute-start | bytes 786440 | tf_op jit(solution)/shard_map/ppermute | solution.py:436
  74.4 1.4 %shard_map.135 = (bf16[512,128]{1,0:T(8,128)(2,1)}, f32[512,32]{1,0:T(8,128)}, f32[512,32]{1,0:T(8,128)}, f32[1,128]{1,0:T(1,128)}) custom-call(bf16[128,8,128]{2,1,0:T(8,128)(2,1)S(1)} %all_to_all.17.in_ref.own_ref, f32[512,128]{1,0:T(8,128)S(1)} %get-tuple-element.46.update_ref), custom_call_target="tpu_custom_call" | custom-call | tf_op jit(solution)/shard_map/pallas_call | solution.py:316
  75.8 0.0 collective-permute-done.5.other_ref
  75.8 0.8 %shard_map.136 = f32[1024,128]{1,0:T(8,128)} custom-call(bf16[128,8,128]{2,1,0:T(8,128)(2,1)S(1)} %all_to_all.17.in_ref.own_ref, bf16[128,8,128]{2,1,0:T(8,128)(2,1)S(1)} %collective-permute-done.5.other_ref), custom_call_target="tpu_custom_call" | custom-call | tf_op jit(solution)/shard_map/pallas_call | solution.py:316
  (14 shorter events, 0.1 us)
Async XLA Ops:
  2.3 7.2 %collective-permute-start = (bf16[16,1152]{1,0:T(8,128)(2,1)}, bf16[16,1152]{1,0:T(8,128)(2,1)S(1)}, u32[]{:S(2)}, u32[]{:S(2)}) collective-permute-start(bf16[16,1152]{1,0:T(8,128)(2,1)} %shard_map.128), channel_id=1, source_target_pairs={{0,4},{1,20},{2,36},{3,52},{4,68},{5,84},{6,100},{7,116},{8,12},{9... | collective-permute-start | bytes 110600 | tf_op jit(solution)/shard_map/ppermute | solution.py:363
  8.5 2.1 %collective-permute-start.1 = (bf16[16,1152]{1,0:T(8,128)(2,1)}, bf16[16,1152]{1,0:T(8,128)(2,1)S(1)}, u32[]{:S(2)}, u32[]{:S(2)}) collective-permute-start(bf16[16,1152]{1,0:T(8,128)(2,1)} %shard_map.129), channel_id=1, source_target_pairs={{0,8},{1,9},{2,10},{3,11},{4,12},{5,13},{6,14},{7,15},{8,0},{9,1},... | collective-permute-start | bytes 110600 | tf_op jit(solution)/shard_map/ppermute | solution.py:364
  9.5 0.7 copy-start.6
  10.2 1.2 %collective-permute-start.2 = (bf16[16,1152]{1,0:T(8,128)(2,1)S(1)}, bf16[16,1152]{1,0:T(8,128)(2,1)S(1)}, u32[]{:S(2)}, u32[]{:S(2)}) collective-permute-start(bf16[16,1152]{1,0:T(8,128)(2,1)S(1)} %collective-permute-done), channel_id=1, source_target_pairs={{0,8},{1,9},{2,10},{3,11},{4,12},{5,13},{6,14},{7,15},{8,0},{9,1},... | collective-permute-start | bytes 110600 | tf_op jit(solution)/shard_map/ppermute | solution.py:365
  10.6 0.8 %copy-start.5 = (bf16[16,1152]{1,0:T(8,128)(2,1)S(1)}, bf16[16,1152]{1,0:T(8,128)(2,1)}, u32[]{:S(2)}) copy-start(bf16[16,1152]{1,0:T(8,128)(2,1)} %shard_map.129) | copy-start | bytes 110596
  11.5 20.2 %copy-start.2 = (bf16[2,128,1536]{2,1,0:T(8,128)(2,1)S(1)}, bf16[2,128,1536]{2,1,0:T(8,128)(2,1)}, u32[]{:S(2)}) copy-start(bf16[2,128,1536]{2,1,0:T(8,128)(2,1)} %constant.28.clone.spread_ref) | copy-start | bytes 2359300
  11.5 18.6 %copy-start.4 = (bf16[16,32,128]{2,1,0:T(8,128)(2,1)S(1)}, bf16[16,32,128]{2,1,0:T(8,128)(2,1)}, u32[]{:S(2)}) copy-start(bf16[16,32,128]{2,1,0:T(8,128)(2,1)} %param.14) | copy-start | bytes 393220
  11.5 20.2 %copy-start = (bf16[512,512]{1,0:T(8,128)(2,1)S(1)}, bf16[512,512]{1,0:T(8,128)(2,1)}, u32[]{:S(2)}) copy-start(bf16[512,512]{1,0:T(8,128)(2,1)} %constant.26.clone.lanes_ref) | copy-start | bytes 1572868
  11.5 20.2 %copy-start.1 = (bf16[32,32,128]{2,1,0:T(8,128)(2,1)S(1)}, bf16[32,32,128]{2,1,0:T(8,128)(2,1)}, u32[]{:S(2)}) copy-start(bf16[32,32,128]{2,1,0:T(8,128)(2,1)} %param.12) | copy-start | bytes 786436
  27.9 3.8 %collective-permute-start.3 = (bf16[128,2176]{1,0:T(8,128)(2,1)S(1)}, bf16[128,2176]{1,0:T(8,128)(2,1)S(1)}, u32[]{:S(2)}, u32[]{:S(2)}) collective-permute-start(bf16[128,2176]{1,0:T(8,128)(2,1)S(1)} %bitcast.10), channel_id=1, source_target_pairs={{0,8},{1,9},{2,10},{3,11},{4,12},{5,13},{6,14},{7,15},{8,0},{9,1},... | collective-permute-start | bytes 1671176 | tf_op jit(solution)/shard_map/ppermute | solution.py:372
  31.7 3.2 %copy-start.3 = (bf16[256,256]{1,0:T(8,128)(2,1)S(1)}, bf16[256,256]{1,0:T(8,128)(2,1)}, u32[]{:S(2)}) copy-start(bf16[256,256]{1,0:T(8,128)(2,1)} %constant.27.clone.order_ref) | copy-start | bytes 393220
  34.5 2.0 %collective-permute-start.4 = (bf16[256,768]{1,0:T(8,128)(2,1)S(1)}, bf16[256,768]{1,0:T(8,128)(2,1)S(1)}, u32[]{:S(2)}, u32[]{:S(2)}) collective-permute-start(bf16[256,768]{1,0:T(8,128)(2,1)S(1)} %get-tuple-element.32), channel_id=1, source_target_pairs={{0,8},{1,9},{2,10},{3,11},{4,12},{5,13},{6,14},{7,15},{8,0},{9,1},... | collective-permute-start | bytes 1179656 | tf_op jit(solution)/shard_map/ppermute | solution.py:403
  73.5 2.4 %collective-permute-start.5 = (bf16[128,8,128]{2,1,0:T(8,128)(2,1)S(1)}, bf16[128,8,128]{2,1,0:T(8,128)(2,1)S(1)}, u32[]{:S(2)}, u32[]{:S(2)}) collective-permute-start(bf16[128,8,128]{2,1,0:T(8,128)(2,1)S(1)} %all_to_all.17.in_ref.own_ref), channel_id=1, source_target_pairs={{0,8},{1,9},{2,10},{3,11},{4,12},{5,13},{6,14},{7,15},{8,0},{9,1},... | collective-permute-start | bytes 786440 | tf_op jit(solution)/shard_map/ppermute | solution.py:436
